TPU v7x, 256 devices: a whole 4x4x8 slice. The times are simulated.
256 devices in a mesh: grp: 32 (over x, y, core), sub: 8 (over z).
Axes of the slice: x: 4, y: 4, z: 8, core: 2. Of those that a mesh axis runs over, the one named last changes fastest.
Arguments:
- q_local: bfloat16 [32768, 1024], P(('grp', 'sub')), may hold values from -6 to 6
- k_local: bfloat16 [32768, 1024], P(('grp', 'sub')), may hold values from -6 to 6
- v_local: bfloat16 [32768, 1024], P(('grp', 'sub')), may hold values from -6 to 6
- q_short: bfloat16 [4096, 1024], P(('grp', 'sub')), may hold values from -6 to 6
- k_short: bfloat16 [4096, 1024], P(('grp', 'sub')), may hold values from -6 to 6
- v_short: bfloat16 [4096, 1024], P(('grp', 'sub')), may hold values from -6 to 6
- grad_out: bfloat16 [32768, 1024], P(('grp', 'sub')), may hold values from -6 to 6
Outputs:
- local_out: bfloat16 [32768, 1024], P(('grp', 'sub'))
- local_dq: bfloat16 [32768, 1024], P(('grp', 'sub'))
- local_dk: bfloat16 [32768, 1024], P(('grp', 'sub'))
- local_dv: bfloat16 [32768, 1024], P(('grp', 'sub'))
- short_out: bfloat16 [4096, 1024], P('grp', 'sub')
- short_dq: bfloat16 [4096, 1024], P('grp', 'sub')
- short_dk: bfloat16 [4096, 1024], P('grp', 'sub')
- short_dv: bfloat16 [4096, 1024], P('grp', 'sub')
All inputs are finite; a program needn't handle non-finite values.
Results may differ from a plain program's by a relative error of at most 0.0318.
Values may be sent and summed in bfloat16 or wider, within the bound.
No kernel may reach another device: no remote copies, remote signals or barrier semaphores. Data moves between devices by JAX's collectives and lax.ppermute only.
A program may use at most 64 MiB of HBM per device.

v0:
```python
import math

import jax
import jax.numpy as jnp
from jax import lax
from jax.sharding import PartitionSpec as P

HD = 64
WINDOW = 128
POOL = 8


def passed_along(value, axis, steps):
    count = lax.axis_size(axis)
    first, last = (max(0, -steps), min(count, count - steps))
    return lax.ppermute(value, axis, [(source, source + steps) for source in range(first, last)])


def attend(queries, key_rows, values, cotangent, key_mask, score_scale):
    scores = (
        jnp.einsum("ihd,jhd->hij", queries, key_rows, preferred_element_type=jnp.float32)
        * score_scale
    )
    scores = jnp.where(key_mask[None], scores, -jnp.inf)
    row_max = jnp.max(scores, axis=-1)
    log_total = row_max + jnp.log(jnp.sum(jnp.exp(scores - row_max[..., None]), axis=-1))
    weights = jnp.exp(scores - log_total[..., None])
    weights_bf = weights.astype(jnp.bfloat16)
    output = jnp.einsum(
        "hij,jhd->ihd", weights_bf, values, preferred_element_type=jnp.float32
    ).astype(jnp.bfloat16)
    row_dots = jnp.einsum("ihd,ihd->hi", cotangent, output, preferred_element_type=jnp.float32)
    dprob = jnp.einsum("ihd,jhd->hij", cotangent, values, preferred_element_type=jnp.float32)
    dscore = (weights * (dprob - row_dots[..., None])).astype(jnp.bfloat16)
    grad_q = (
        jnp.einsum("hij,jhd->ihd", dscore, key_rows, preferred_element_type=jnp.float32)
        * score_scale
    ).astype(jnp.bfloat16)
    grad_k = None
    grad_v = None
    grad_k = (
        jnp.einsum("hij,ihd->jhd", dscore, queries, preferred_element_type=jnp.float32)
        * score_scale
    )
    grad_v = jnp.einsum("hij,ihd->jhd", weights_bf, cotangent, preferred_element_type=jnp.float32)
    return (output, grad_q, grad_k, grad_v, log_total, row_dots, weights_bf, dscore)


def on_device(q_local, k_local, v_local, q_short, k_short, v_short, grad_out):
    num_rows, feat_width = q_local.shape
    num_heads = feat_width // HD
    score_scale = 1.0 / math.sqrt(HD)
    prev_k, prev_v = passed_along((k_local, v_local), ("grp", "sub"), 1)
    key_rows = jnp.concatenate([prev_k, k_local], axis=0).reshape(2 * num_rows, num_heads, HD)
    value_rows = jnp.concatenate([prev_v, v_local], axis=0).reshape(2 * num_rows, num_heads, HD)
    first_pos = lax.axis_index(("grp", "sub")) * num_rows
    query_pos = first_pos + jnp.arange(num_rows, dtype=jnp.int32)
    key_pos = first_pos - num_rows + jnp.arange(2 * num_rows, dtype=jnp.int32)
    key_mask = (
        (key_pos[None, :] <= query_pos[:, None])
        & (key_pos[None, :] > query_pos[:, None] - WINDOW)
        & (key_pos[None, :] >= 0)
    )
    own_queries = q_local.reshape(num_rows, num_heads, HD)
    own_grads = grad_out.reshape(num_rows, num_heads, HD)
    output, grad_q, grad_k, grad_v, unused_total, unused_dots, unused_w, unused_s = attend(
        own_queries, key_rows, value_rows, own_grads, key_mask, score_scale
    )
    grad_k = grad_k.reshape(2 * num_rows, feat_width)
    grad_v = grad_v.reshape(2 * num_rows, feat_width)
    back_k, back_v = (
        passed_along(grad_k[:num_rows].astype(jnp.bfloat16), ("grp", "sub"), -1).astype(
            jnp.float32
        ),
        passed_along(grad_v[:num_rows].astype(jnp.bfloat16), ("grp", "sub"), -1).astype(
            jnp.float32
        ),
    )
    local_dk = (grad_k[num_rows:] + back_k).astype(jnp.bfloat16)
    local_dv = (grad_v[num_rows:] + back_v).astype(jnp.bfloat16)
    local_out = output.reshape(num_rows, feat_width)
    local_dq = grad_q.reshape(num_rows, feat_width)
    pooled = jnp.sum(
        grad_out.reshape(num_rows // POOL, POOL, feat_width), axis=1, dtype=jnp.float32
    ).astype(jnp.bfloat16)
    head_q, head_k, head_v, head_g = (
        lax.all_to_all(q_short, "sub", split_axis=1, concat_axis=0, tiled=True),
        lax.all_to_all(k_short, "sub", split_axis=1, concat_axis=0, tiled=True),
        lax.all_to_all(v_short, "sub", split_axis=1, concat_axis=0, tiled=True),
        lax.all_to_all(pooled, "sub", split_axis=1, concat_axis=0, tiled=True),
    )
    group_rows, head_width = head_q.shape
    local_heads = head_width // HD
    every_k, every_v = (
        lax.all_gather(head_k, "grp", axis=0, tiled=True),
        lax.all_gather(head_v, "grp", axis=0, tiled=True),
    )
    short_len = every_k.shape[0]
    group_first = lax.axis_index("grp") * group_rows
    own_pos = group_first + jnp.arange(group_rows, dtype=jnp.int32)
    all_pos = jnp.arange(short_len, dtype=jnp.int32)
    causal = all_pos[None, :] <= own_pos[:, None]
    out_list = []
    dq_list = []
    dk_list = []
    dv_list = []
    total_list = []
    dots_list = []
    for head_idx in range(local_heads):
        low_col = head_idx * HD
        high_col = low_col + HD
        head_out, head_dq, head_dk, head_dv, head_total, head_dots, unused_w, unused_s = attend(
            head_q[:, low_col:high_col].reshape(group_rows, 1, HD),
            every_k[:, low_col:high_col].reshape(short_len, 1, HD),
            every_v[:, low_col:high_col].reshape(short_len, 1, HD),
            head_g[:, low_col:high_col].reshape(group_rows, 1, HD),
            causal,
            score_scale,
        )
        out_list.append(head_out.reshape(group_rows, HD))
        dq_list.append(head_dq.reshape(group_rows, HD))
        total_list.append(head_total.reshape(group_rows, 1))
        dots_list.append(head_dots.reshape(group_rows, 1))
        dk_list.append(head_dk.reshape(short_len, HD))
        dv_list.append(head_dv.reshape(short_len, HD))
    short_out = jnp.concatenate(out_list, axis=1)
    short_dq = jnp.concatenate(dq_list, axis=1)
    key_terms = jnp.concatenate(dk_list + dv_list, axis=1)
    summed = lax.psum_scatter(
        key_terms.astype(jnp.bfloat16), "grp", scatter_dimension=0, tiled=True
    ).astype(jnp.float32)
    short_dk = summed[:, :head_width].astype(jnp.bfloat16)
    short_dv = summed[:, head_width:].astype(jnp.bfloat16)
    return (local_out, local_dq, local_dk, local_dv, short_out, short_dq, short_dk, short_dv)


def solution(mesh):
    return jax.shard_map(
        on_device,
        mesh=mesh,
        in_specs=(
            P(("grp", "sub"), None),
            P(("grp", "sub"), None),
            P(("grp", "sub"), None),
            P(("grp", "sub"), None),
            P(("grp", "sub"), None),
            P(("grp", "sub"), None),
            P(("grp", "sub"), None),
        ),
        out_specs=(
            P(("grp", "sub"), None),
            P(("grp", "sub"), None),
            P(("grp", "sub"), None),
            P(("grp", "sub"), None),
            P("grp", "sub"),
            P("grp", "sub"),
            P("grp", "sub"),
            P("grp", "sub"),
        ),
        check_vma=False,
    )
```

profile of v0, /device:TPU:1, one launch (start us, length us, event | category | flops | bytes accessed | tf_op | source)
XLA Modules:
  0.0 227.3 jit_solution(12827367560728629502)
XLA Ops:
  7.2 0.7 copy-done
  7.9 15.8 %all_to_all.76 = bf16[16,8,128]{2,0,1:T(8,128)(2,1)} all-to-all(bf16[16,8,128]{2,0,1:T(8,128)(2,1)S(1)} %copy_bitcast_fusion.2), channel_id=1, replica_groups=mesh['grp'=32,'sub'=8] {'sub'}, dimensions={1} | all-to-all | bytes 65536 | tf_op jit(solution)/shard_map/all_to_all | solution.py:88
  23.7 1.4 copy_bitcast_fusion.1
  25.1 3.3 %all-to-all-start.2 = ((bf16[16,8,128]{2,0,1:T(8,128)(2,1)}), bf16[16,8,128]{2,0,1:T(8,128)(2,1)S(1)}, u32[]{:S(2)}, u32[]{:S(2)}) async-start(bf16[16,8,128]{2,0,1:T(8,128)(2,1)} %copy_bitcast_fusion.1), calls=%async_computation.2 | async-start | bytes 65536 | tf_op jit(solution)/shard_map/all_to_all | solution.py:89
  28.5 3.3 %collective-permute-start.1 = (bf16[128,1024]{1,0:T(8,128)(2,1)}, bf16[128,1024]{1,0:T(8,128)(2,1)S(1)}, u32[]{:S(2)}, u32[]{:S(2)}) collective-permute-start(bf16[128,1024]{1,0:T(8,128)(2,1)} %param.8), channel_id=1, source_target_pairs={{0,1},{1,2},{2,3},{3,4},{4,5},{5,6},{6,7},{7,8},{8,9},{9,10},{10,1... | collective-permute-start | bytes 786440 | tf_op jit(solution)/shard_map/ppermute | solution.py:16
  31.7 3.1 %collective-permute-start = (bf16[128,1024]{1,0:T(8,128)(2,1)}, bf16[128,1024]{1,0:T(8,128)(2,1)}, u32[]{:S(2)}, u32[]{:S(2)}) collective-permute-start(bf16[128,1024]{1,0:T(8,128)(2,1)} %param.9), channel_id=1, source_target_pairs={{0,1},{1,2},{2,3},{3,4},{4,5},{5,6},{6,7},{7,8},{8,9},{9,10},{10,1... | collective-permute-start | bytes 786440 | tf_op jit(solution)/shard_map/ppermute | solution.py:16
  34.9 1.1 bitcast_reduce_fusion
  36.0 1.4 copy_bitcast_fusion.3
  37.4 0.6 copy_bitcast_fusion
  38.0 6.3 %all-to-all-start.3 = ((bf16[16,8,128]{2,0,1:T(8,128)(2,1)}), bf16[16,8,128]{2,0,1:T(8,128)(2,1)S(1)}, u32[]{:S(2)}, u32[]{:S(2)}) async-start(bf16[16,8,128]{2,0,1:T(8,128)(2,1)} %copy_bitcast_fusion), calls=%async_computation.3 | async-start | bytes 65536 | tf_op jit(solution)/shard_map/all_to_all | solution.py:90
  44.4 0.7 all-gather.5.cloned.1.call-update
  45.1 0.8 and_and_fusion
  45.9 1.1 copy.79
  47.0 1.1 copy.77
  48.1 3.1 %all-to-all-done.3 = bf16[16,8,128]{2,0,1:T(8,128)(2,1)S(1)} async-done(((bf16[16,8,128]{2,0,1:T(8,128)(2,1)}), bf16[16,8,128]{2,0,1:T(8,128)(2,1)S(1)}, u32[]{:S(2)}, u32[]{:S(2)}) %all-to-all-start.3) | async-done | bytes 32800 | tf_op jit(solution)/shard_map/all_to_all | solution.py:90
  51.3 3.5 %all-to-all-start = ((bf16[16,8,128]{2,0,1:T(8,128)(2,1)}), bf16[16,8,128]{2,0,1:T(8,128)(2,1)S(1)}, u32[]{:S(2)}, u32[]{:S(2)}) async-start(bf16[16,8,128]{2,0,1:T(8,128)(2,1)} %copy_bitcast_fusion.3), calls=%async_computation | async-start | bytes 65536 | tf_op jit(solution)/shard_map/all_to_all | solution.py:87
  55.0 0.7 copy.114
  56.0 1.4 fusion.42
  57.4 1.0 pad_maximum_fusion.1
  58.4 1.0 copy.75
  59.4 2.3 all-to-all-done
  61.7 8.2 %all-gather.3.cloned.1.call-done = bf16[4096,128]{1,0:T(8,128)(2,1)} async-done(((bf16[128,128]{1,0:T(8,128)(2,1)}), bf16[4096,128]{1,0:T(8,128)(2,1)}) %all-gather.3.cloned.1.call-update) | async-done | bytes 1048592 | tf_op jit(solution)/shard_map/all_gather | solution.py:95
  69.9 2.0 fusion.43
  71.9 0.4 exponential_reduce_fusion
  72.3 0.9 copy-done.1
  73.2 1.4 fusion.9
  74.6 45.7 %all-gather.5.cloned.1.call-done = bf16[4096,128]{1,0:T(8,128)(2,1)} async-done(((bf16[128,128]{1,0:T(8,128)(2,1)}), bf16[4096,128]{1,0:T(8,128)(2,1)}) %all-gather.5.cloned.1.call-update) | async-done | bytes 1048592 | tf_op jit(solution)/shard_map/all_gather | solution.py:96
  120.2 3.7 %multiply_reduce_fusion = (f32[128]{0:T(128)S(1)}, bf16[128,64]{0,1:T(8,128)(2,1)}) fusion(f32[128,64]{0,1:T(8,128)S(1)} %copy-done.20, bf16[4096,128]{1,0:T(8,128)(2,1)} %all-gather.5.cloned.1.call-done, f32[128,4096]{1,0:T(8,128)} %copy-done.1, f32[128]{0:T(128)S(1)} %log_add_fusion.1), kind=kOutput, calls=%fused_computation.68 | convolution fusion | flops 68190080 | bytes 3195904 | tf_op jit(solution)/shard_map/hij,jhd->ihd/dot_general | solution.py:29
  123.9 0.8 fusion.5
  124.7 0.4 fusion.7
  125.1 0.6 fusion.44
  125.7 0.4 exponential_reduce_fusion.1
  126.2 0.6 fusion.8
  126.7 1.2 multiply_reduce_fusion.1
  128.0 0.6 fusion.4
  128.6 1.0 copy-done.4
  129.5 0.4 fusion.6
  129.9 1.5 pad_maximum_fusion
  131.4 4.1 %copy.117 = bf16[4096,256]{1,0:T(8,128)(2,1)} copy(bf16[4096,256]{0,1:T(8,128)(2,1)} %pad_maximum_fusion) | data formatting | bytes 4194304
  135.8 0.7 copy-done.8
  136.6 1.2 fusion.26
  137.8 0.7 fusion.10
  138.5 1.0 copy-done.6
  139.4 0.5 fusion.14
  139.9 1.0 copy-done.11
  140.9 0.7 slice.121
  141.6 1.8 copy.82
  143.5 0.5 convolution_bitcast_fusion
  144.0 1.0 copy-done.12
  145.1 5.2 %collective-permute-start.3 = (bf16[128,1024]{1,0:T(8,128)(2,1)S(1)}, bf16[128,1024]{1,0:T(8,128)(2,1)}, u32[]{:S(2)}, u32[]{:S(2)}) collective-permute-start(bf16[128,1024]{1,0:T(8,128)(2,1)S(1)} %copy.85), channel_id=1, source_target_pairs={{1,0},{2,1},{3,2},{4,3},{5,4},{6,5},{7,6},{8,7},{9,8},{10,9},{11,1... | collective-permute-start | bytes 786440 | tf_op jit(solution)/shard_map/ppermute | solution.py:16
  150.3 3.5 %collective-permute-start.2 = (bf16[128,1024]{1,0:T(8,128)(2,1)}, bf16[128,1024]{1,0:T(8,128)(2,1)}, u32[]{:S(2)}, u32[]{:S(2)}) collective-permute-start(bf16[128,1024]{1,0:T(8,128)(2,1)} %copy.82), channel_id=1, source_target_pairs={{1,0},{2,1},{3,2},{4,3},{5,4},{6,5},{7,6},{8,7},{9,8},{10,9},{11,1... | collective-permute-start | bytes 786440 | tf_op jit(solution)/shard_map/ppermute | solution.py:16
  153.8 1.7 fusion.15
  155.6 0.9 copy.91
  156.4 0.8 copy.92
  157.3 1.0 copy.83
  158.3 1.0 copy.86
  159.3 2.0 add_convert_fusion
  161.2 1.7 add_convert_fusion.1
  163.0 1.0 fusion.17
  164.0 0.6 fusion.16
  164.6 0.7 copy.94
  165.3 0.7 copy.93
  166.0 53.3 %reduce-scatter.4.cloned.1.call-done = bf16[128,256]{1,0:T(8,128)(2,1)} async-done(((bf16[4096,256]{1,0:T(8,128)(2,1)}), bf16[128,256]{1,0:T(8,128)(2,1)}) %reduce-scatter.4.cloned.1.call-update) | async-done | bytes 65552
  219.4 1.4 fusion.41
  (72 shorter events, 1.2 us)
Async XLA Ops:
  7.2 0.8 copy-start
  7.2 48.5 %copy-start.18 = (bf16[128,1024]{1,0:T(8,128)(2,1)S(1)}, bf16[128,1024]{1,0:T(8,128)(2,1)}, u32[]{:S(2)}) copy-start(bf16[128,1024]{1,0:T(8,128)(2,1)} %param.8) | copy-start | bytes 786436
  7.2 62.7 %all-gather.3.cloned.1.call-start = ((), (), s32[]{:S(2)}) async-start(), calls=%async_computation.5 | async-start | bytes 1081344 | tf_op jit(solution)/shard_map/all_gather | solution.py:95
  25.1 12.9 %all-to-all-start.2 = ((bf16[16,8,128]{2,0,1:T(8,128)(2,1)}), bf16[16,8,128]{2,0,1:T(8,128)(2,1)S(1)}, u32[]{:S(2)}, u32[]{:S(2)}) async-start(bf16[16,8,128]{2,0,1:T(8,128)(2,1)} %copy_bitcast_fusion.1), calls=%async_computation.2 | async-start | bytes 65536 | tf_op jit(solution)/shard_map/all_to_all | solution.py:89
  28.5 27.2 %collective-permute-start.1 = (bf16[128,1024]{1,0:T(8,128)(2,1)}, bf16[128,1024]{1,0:T(8,128)(2,1)S(1)}, u32[]{:S(2)}, u32[]{:S(2)}) collective-permute-start(bf16[128,1024]{1,0:T(8,128)(2,1)} %param.8), channel_id=1, source_target_pairs={{0,1},{1,2},{2,3},{3,4},{4,5},{5,6},{6,7},{7,8},{8,9},{9,10},{10,1... | collective-permute-start | bytes 786440 | tf_op jit(solution)/shard_map/ppermute | solution.py:16
  31.7 25.7 %collective-permute-start = (bf16[128,1024]{1,0:T(8,128)(2,1)}, bf16[128,1024]{1,0:T(8,128)(2,1)}, u32[]{:S(2)}, u32[]{:S(2)}) collective-permute-start(bf16[128,1024]{1,0:T(8,128)(2,1)} %param.9), channel_id=1, source_target_pairs={{0,1},{1,2},{2,3},{3,4},{4,5},{5,6},{6,7},{7,8},{8,9},{9,10},{10,1... | collective-permute-start | bytes 786440 | tf_op jit(solution)/shard_map/ppermute | solution.py:16
  38.0 6.4 %copy-start.21 = (bf16[16,8,128]{2,0,1:T(8,128)(2,1)}, bf16[16,8,128]{2,0,1:T(8,128)(2,1)S(1)}, u32[]{:S(2)}) copy-start(bf16[16,8,128]{2,0,1:T(8,128)(2,1)S(1)} %all-to-all-done.2) | copy-start | bytes 98308
  38.0 13.2 %all-to-all-start.3 = ((bf16[16,8,128]{2,0,1:T(8,128)(2,1)}), bf16[16,8,128]{2,0,1:T(8,128)(2,1)S(1)}, u32[]{:S(2)}, u32[]{:S(2)}) async-start(bf16[16,8,128]{2,0,1:T(8,128)(2,1)} %copy_bitcast_fusion), calls=%async_computation.3 | async-start | bytes 65536 | tf_op jit(solution)/shard_map/all_to_all | solution.py:90
  44.4 75.9 %all-gather.5.cloned.1.call-start = ((), (), s32[]{:S(2)}) async-start(), calls=%async_computation.6 | async-start | bytes 1081344 | tf_op jit(solution)/shard_map/all_gather | solution.py:96
  48.1 9.3 %copy-start.13 = (bf16[128,1024]{0,1:T(8,128)(2,1)}, bf16[128,1024]{0,1:T(8,128)(2,1)S(1)}, u32[]{:S(2)}) copy-start(bf16[128,1024]{0,1:T(8,128)(2,1)S(1)} %copy.77) | copy-start | bytes 786436
  51.3 10.4 %all-to-all-start = ((bf16[16,8,128]{2,0,1:T(8,128)(2,1)}), bf16[16,8,128]{2,0,1:T(8,128)(2,1)S(1)}, u32[]{:S(2)}, u32[]{:S(2)}) async-start(bf16[16,8,128]{2,0,1:T(8,128)(2,1)} %copy_bitcast_fusion.3), calls=%async_computation | async-start | bytes 65536 | tf_op jit(solution)/shard_map/all_to_all | solution.py:87
  54.8 164.6 %reduce-scatter.4.cloned.1.call-start = ((), (), s32[]{:S(2)}) async-start(), calls=%async_computation.7 | async-start | bytes 2162688
  56.0 3.5 %copy-start.7 = (bf16[256,1024]{0,1:T(8,128)(2,1)}, bf16[256,1024]{0,1:T(8,128)(2,1)S(1)}, u32[]{:S(2)}) copy-start(bf16[256,1024]{0,1:T(8,128)(2,1)S(1)} %copy.76) | copy-start | bytes 1572868
  56.0 1.4 copy-start.19
  71.9 1.3 copy-start.1
  71.9 48.4 %copy-start.20 = (f32[128,64]{0,1:T(8,128)S(1)}, f32[128,64]{0,1:T(8,128)}, u32[]{:S(2)}) copy-start(f32[128,64]{0,1:T(8,128)} %copy.114) | copy-start | bytes 98308
  120.2 3.7 %copy-start.2 = (f32[128,4096]{1,0:T(8,128)S(1)}, f32[128,4096]{1,0:T(8,128)}, u32[]{:S(2)}) copy-start(f32[128,4096]{1,0:T(8,128)} %copy-done.1) | copy-start | bytes 6291460
  120.2 3.7 %copy-start.3 = (bf16[4096,128]{1,0:T(8,128)(2,1)S(1)}, bf16[4096,128]{1,0:T(8,128)(2,1)}, u32[]{:S(2)}) copy-start(bf16[4096,128]{1,0:T(8,128)(2,1)} %all-gather.5.cloned.1.call-done) | copy-start | bytes 3145732
  123.9 1.2 copy-start.9
  128.0 1.9 copy-start.16
  128.5 1.0 copy-start.4
  135.5 1.0 copy-start.8
  137.8 1.7 copy-start.14
  138.5 1.0 copy-start.6
  139.9 1.0 copy-start.11
  144.0 1.0 copy-start.12
  145.1 10.4 %copy-start.17 = (bf16[16,64,128]{2,1,0:T(8,128)(2,1)S(1)}, bf16[16,64,128]{2,1,0:T(8,128)(2,1)}, u32[]{:S(2)}) copy-start(bf16[16,64,128]{2,1,0:T(8,128)(2,1)} %get-tuple-element.47) | copy-start | bytes 786436
  145.1 12.1 %slice-start = ((f32[256,16,64]{0,2,1:T(8,128)}), f32[128,16,64]{0,2,1:T(8,128)S(1)}, s32[]{:S(2)}) async-start(f32[256,16,64]{0,2,1:T(8,128)} %copy-done.11), calls=%async_computation.8 | async-start | bytes 1048576 | tf_op jit(solution)/shard_map/slice | solution.py:79
  145.1 14.1 %collective-permute-start.3 = (bf16[128,1024]{1,0:T(8,128)(2,1)S(1)}, bf16[128,1024]{1,0:T(8,128)(2,1)}, u32[]{:S(2)}, u32[]{:S(2)}) collective-permute-start(bf16[128,1024]{1,0:T(8,128)(2,1)S(1)} %copy.85), channel_id=1, source_target_pairs={{1,0},{2,1},{3,2},{4,3},{5,4},{6,5},{7,6},{8,7},{9,8},{10,9},{11,1... | collective-permute-start | bytes 786440 | tf_op jit(solution)/shard_map/ppermute | solution.py:16
  150.3 10.9 %collective-permute-start.2 = (bf16[128,1024]{1,0:T(8,128)(2,1)}, bf16[128,1024]{1,0:T(8,128)(2,1)}, u32[]{:S(2)}, u32[]{:S(2)}) collective-permute-start(bf16[128,1024]{1,0:T(8,128)(2,1)} %copy.82), channel_id=1, source_target_pairs={{1,0},{2,1},{3,2},{4,3},{5,4},{6,5},{7,6},{8,7},{9,8},{10,9},{11,1... | collective-permute-start | bytes 786440 | tf_op jit(solution)/shard_map/ppermute | solution.py:16
  155.6 2.7 %slice-start.1 = ((f32[256,16,64]{0,2,1:T(8,128)}), f32[128,16,64]{0,2,1:T(8,128)S(1)}, s32[]{:S(2)}) async-start(f32[256,16,64]{0,2,1:T(8,128)} %copy-done.12), calls=%async_computation.9 | async-start | bytes 1048576 | tf_op jit(solution)/shard_map/slice | solution.py:80
  157.3 5.7 %copy-start.10 = (bf16[4096,128]{1,0:T(8,128)(2,1)S(1)}, bf16[4096,128]{1,0:T(8,128)(2,1)}, u32[]{:S(2)}) copy-start(bf16[4096,128]{1,0:T(8,128)(2,1)} %all-gather.3.cloned.1.call-done) | copy-start | bytes 3145732
  158.3 3.0 %copy-start.15 = (f32[128,1024]{1,0:T(8,128)S(1)}, f32[128,1024]{1,0:T(8,128)}, u32[]{:S(2)}) copy-start(f32[128,1024]{1,0:T(8,128)} %copy.83) | copy-start | bytes 1572868
  159.3 4.7 %copy-start.5 = (bf16[128,4096]{1,0:T(8,128)(2,1)S(1)}, bf16[128,4096]{1,0:T(8,128)(2,1)}, u32[]{:S(2)}) copy-start(bf16[128,4096]{1,0:T(8,128)(2,1)} %copy-done.4) | copy-start | bytes 3145732
  163.0 2.3 %copy-start.22 = (bf16[128,64]{0,1:T(8,128)(2,1)S(1)}, bf16[128,64]{0,1:T(8,128)(2,1)}, u32[]{:S(2)}) copy-start(bf16[128,64]{0,1:T(8,128)(2,1)} %get-tuple-element.53) | copy-start | bytes 49156
  163.0 2.3 %copy-start.23 = (bf16[128,64]{0,1:T(8,128)(2,1)S(1)}, bf16[128,64]{0,1:T(8,128)(2,1)}, u32[]{:S(2)}) copy-start(bf16[128,64]{0,1:T(8,128)(2,1)} %get-tuple-element.55) | copy-start | bytes 49156
Sparse Core Ops, SparseCore 0:
  23.9 45.9 all-gather.2
  73.0 47.1 all-gather.4
  135.6 83.6 reduce-scatter.3
where the time goes:
time: 229 us; the launch traced here: 227 us
  waiting for transfers between devices  113 us (49%)
  starting transfers between devices  28.3 us (12%)
  local copies, waits for them, and re-layouts  27.2 us (12%)
  matrix products  19 us (8%)
  blocking collectives  15.8 us (7%)
  between operations  14.2 us (6%)
  other arithmetic  9.42 us (4%)
    unnamed x4, waiting for transfers between devices  54.1 us
    all_gather x1, waiting for transfers between devices, on_device(): lax.all_gather(head_v, 'grp', axis=0, tiled=True)  45.7 us
    unnamed x57, local copies, waits for them, and re-layouts  16.5 us
    all_to_all x1, blocking collectives, on_device(): lax.all_to_all(k_short, 'sub', split_axis=1, concat_axis=0, tiled=True)  15.8 us
    ppermute x4, starting transfers between devices, passed_along(): lax.ppermute(value, axis, [(source, source + steps) for source in range(f...  15 us
    all_gather x1, waiting for transfers between devices, on_device(): lax.all_gather(head_k, 'grp', axis=0, tiled=True)  8.22 us
    all_to_all x1, starting transfers between devices, on_device(): lax.all_to_all(pooled, 'sub', split_axis=1, concat_axis=0, tiled=True)  6.34 us
    dot_general x3, matrix products, attend(): jnp.einsum('hij,jhd->ihd', weights_bf, values, preferred_element_type=jnp...  6.12 us
  transfers between devices with their start and end apart: 10, of which 5 were waited for; matrix products, arithmetic and copies ran while one was open for 15% of the time, Pallas kernels for 0%

commit v1 on v0

v1 whole, which is shorter than its diff:
```python
import math

import jax
import jax.numpy as jnp
from jax import lax
from jax.experimental import pallas as pl
from jax.experimental.pallas import tpu as pltpu
from jax.sharding import Mesh
from jax.sharding import PartitionSpec as P

HD = 64
WINDOW = 128
POOL = 8
LANES = 128
NEG = float("-inf")


def dot_t(a, b):
    return lax.dot_general(a, b, (((1,), (1,)), ((), ())), preferred_element_type=jnp.float32)


def dot_n(a, b):
    return lax.dot_general(a, b, (((1,), (0,)), ((), ())), preferred_element_type=jnp.float32)


def t_dot(a, b):
    return lax.dot_general(a, b, (((0,), (0,)), ((), ())), preferred_element_type=jnp.float32)


def local_kernel(first_ref, q_ref, k_ref, v_ref, g_ref, pk_ref, pv_ref,
                 out_ref, dq_ref, dk_ref, dv_ref, bk_ref, bv_ref):
    rows, width = q_ref.shape
    scale = 1.0 / math.sqrt(HD)
    lane = lax.broadcasted_iota(jnp.int32, (rows, LANES), 1)
    low = lane < HD
    row2 = lax.broadcasted_iota(jnp.int32, (2 * rows, rows), 0) & (rows - 1)
    col2 = lax.broadcasted_iota(jnp.int32, (2 * rows, rows), 1)
    from_prev = col2 > row2
    dead = from_prev & (first_ref[0] == 0)
    zero_b = jnp.zeros((rows, LANES), jnp.bfloat16)
    zero_f = jnp.zeros((2 * rows, rows), jnp.bfloat16)
    for pair in range(width // LANES):
        cols = slice(pair * LANES, (pair + 1) * LANES)
        q, g = q_ref[:, cols], g_ref[:, cols]
        q2 = jnp.concatenate([jnp.where(low, q, zero_b), jnp.where(low, zero_b, q)], axis=0)
        g2 = jnp.concatenate([jnp.where(low, g, zero_b), jnp.where(low, zero_b, g)], axis=0)
        kc = jnp.concatenate([pk_ref[:, cols], k_ref[:, cols]], axis=0)
        vc = jnp.concatenate([pv_ref[:, cols], v_ref[:, cols]], axis=0)
        s_all = dot_t(q2, kc)
        s = jnp.where(from_prev, s_all[:, :rows], s_all[:, rows:]) * scale
        s = jnp.where(dead, NEG, s)
        p = jnp.exp(s - jnp.max(s, axis=1, keepdims=True))
        p = p * (1.0 / jnp.sum(p, axis=1, keepdims=True))
        pb = p.astype(jnp.bfloat16)
        pc = jnp.concatenate(
            [jnp.where(from_prev, pb, zero_f), jnp.where(from_prev, zero_f, pb)], axis=1)
        o2 = dot_n(pc, vc).astype(jnp.bfloat16)
        out_ref[:, cols] = jnp.where(low, o2[:rows], o2[rows:])
        dots = jnp.sum(g2.astype(jnp.float32) * o2.astype(jnp.float32), axis=1, keepdims=True)
        dp_all = dot_t(g2, vc)
        dp = jnp.where(from_prev, dp_all[:, :rows], dp_all[:, rows:])
        ds = (p * (dp - dots)).astype(jnp.bfloat16)
        dc = jnp.concatenate(
            [jnp.where(from_prev, ds, zero_f), jnp.where(from_prev, zero_f, ds)], axis=1)
        dq2 = dot_n(dc, kc) * scale
        dq_ref[:, cols] = jnp.where(low, dq2[:rows], dq2[rows:]).astype(jnp.bfloat16)
        dkc = t_dot(dc, q2) * scale
        dvc = t_dot(pc, g2)
        bk_ref[:, cols] = dkc[:rows].astype(jnp.bfloat16)
        bv_ref[:, cols] = dvc[:rows].astype(jnp.bfloat16)
        dk_ref[:, cols] = dkc[rows:]
        dv_ref[:, cols] = dvc[rows:]


def local_call(first, q, k, v, g, pk, pv):
    rows, width = q.shape
    wide = jax.ShapeDtypeStruct((rows, width), jnp.float32)
    half = jax.ShapeDtypeStruct((rows, width), jnp.bfloat16)
    vm = pl.BlockSpec(memory_space=pltpu.VMEM)
    return pl.pallas_call(
        local_kernel,
        out_shape=(half, half, wide, wide, half, half),
        in_specs=[pl.BlockSpec(memory_space=pltpu.SMEM)] + [vm] * 6,
        out_specs=(vm,) * 6,
        compiler_params=pltpu.CompilerParams(vmem_limit_bytes=32 * 1024 * 1024),
        cost_estimate=pl.CostEstimate(
            flops=12 * rows * 256 * width * 2, bytes_accessed=12 * rows * width * 2,
            transcendentals=rows * rows * 16),
        name="local_layer",
    )(first, q, k, v, g, pk, pv)


def pack_kernel(q_ref, k_ref, v_ref, g_ref, packed_ref):
    small = q_ref.shape[0]
    low = lax.broadcasted_iota(jnp.int32, (small, LANES), 1) < HD

    def halves(a, b):
        swap_a = pltpu.roll(a, HD, 1)
        swap_b = pltpu.roll(b, HD, 1)
        return jnp.where(low, a, swap_b), jnp.where(low, swap_a, b)

    pairs = q_ref.shape[1] // LANES
    for pair in range(pairs):
        cols = slice(pair * LANES, (pair + 1) * LANES)
        grads = g_ref[:, cols].astype(jnp.float32).reshape(small, POOL, LANES)
        pooled = jnp.sum(grads, axis=1).astype(jnp.bfloat16).astype(jnp.float32)
        quarter = [r[:, cols].astype(jnp.float32) for r in (q_ref, k_ref, v_ref)]
        qg = halves(quarter[0], pooled)
        kv = halves(quarter[1], quarter[2])
        for core in range(2):
            packed_ref[core * pairs + pair, :, :LANES] = qg[core].astype(jnp.bfloat16)
            packed_ref[core * pairs + pair, :, LANES:] = kv[core].astype(jnp.bfloat16)


def pack_call(q, k, v, g):
    small, width = q.shape
    vm = pl.BlockSpec(memory_space=pltpu.VMEM)
    return pl.pallas_call(
        pack_kernel,
        out_shape=jax.ShapeDtypeStruct((width // HD, small, 4 * HD), jnp.bfloat16),
        in_specs=[vm] * 4,
        out_specs=vm,
        name="pack_heads",
    )(q, k, v, g)


def spread_kernel(mine_ref, many_ref, late_ref, kv_ref, sem):
    kv_ref[...] = mine_ref[:, LANES:]
    copies = [pltpu.make_async_copy(kv_ref, many_ref.at[i], sem.at[i])
              for i in range(many_ref.shape[0])]
    for copy in copies:
        copy.start()
    half = mine_ref.shape[0] // 2
    late_ref[...] = mine_ref[half:, :LANES]
    for copy in copies:
        copy.wait()


def spread_call(mine, chips):
    rows = mine.shape[0]
    vm = pl.BlockSpec(memory_space=pltpu.VMEM)
    return pl.pallas_call(
        spread_kernel,
        out_shape=(jax.ShapeDtypeStruct((chips, rows, LANES), jnp.bfloat16),
                   jax.ShapeDtypeStruct((rows // 2, LANES), jnp.bfloat16)),
        in_specs=[vm],
        out_specs=(pl.BlockSpec(memory_space=pl.ANY), vm),
        scratch_shapes=[pltpu.VMEM((rows, LANES), jnp.bfloat16), pltpu.SemaphoreType.DMA((chips,))],
        name="spread_keys",
    )(mine)


def short_kernel(chip_ref, mine_ref, late_ref, kv_ref, od_a_ref, od_b_ref, dkv_ref,
                 lhs_ref, lhs_t_ref, s_ref, dp_ref, top_ref, sum_ref, dot_ref, od_ref, acc_ref):
    scale = 1.0 / math.sqrt(HD)
    chip = chip_ref[0]
    blocks, _, kb = acc_ref.shape
    half = late_ref.shape[0]
    low = lax.broadcasted_iota(jnp.int32, (half, LANES), 1) < HD
    zero_b = jnp.zeros((half, LANES), jnp.bfloat16)
    for which, qg in enumerate((mine_ref[:half, :LANES], late_ref[...])):
        qz = jnp.where(low, (qg.astype(jnp.float32) * scale).astype(jnp.bfloat16), zero_b)
        gz = jnp.where(low, zero_b, qg)
        lhs = jnp.concatenate([qz, gz], axis=0)
        lhs_ref[which] = lhs
        lhs_t_ref[which] = lhs.T
    top_ref[...] = jnp.full_like(top_ref, NEG)
    sum_ref[...] = jnp.zeros_like(sum_ref)
    dot_ref[...] = jnp.zeros_like(dot_ref)
    od_ref[...] = jnp.zeros_like(od_ref)
    acc_ref[...] = jnp.zeros_like(acc_ref)
    ahead = (lax.broadcasted_iota(jnp.int32, (half, kb), 1)
             - lax.broadcasted_iota(jnp.int32, (half, kb), 0))
    steps = blocks + 1

    def place(t):
        second = t > chip
        which = jnp.where(second, 1, 0)
        block = jnp.where(second, t - chip - 1, t)
        first = jnp.where(second, (blocks - 1 - chip) * kb + half, chip * kb)
        return which, block, first - block * kb

    def keys(block):
        return kv_ref[pl.ds(pl.multiple_of(block * kb, kb), kb), :]

    for t in range(steps):
        which, block, reach = place(t)
        both = dot_t(lhs_ref[which], keys(block))
        s = jnp.where(ahead <= reach, both[:half], NEG)
        s_ref[t] = s
        dp_ref[t] = both[half:]
        top_ref[which] = jnp.maximum(top_ref[which], jnp.maximum(s[:, :LANES], s[:, LANES:]))
    for which in range(2):
        top = jnp.max(top_ref[which], axis=1, keepdims=True)
        top_ref[which] = jnp.broadcast_to(top, (half, LANES))
    for t in range(steps):
        which, _, _ = place(t)
        top = top_ref[which]
        e = jnp.exp(s_ref[t] - jnp.concatenate([top, top], axis=1))
        s_ref[t] = e
        ed = e * dp_ref[t]
        sum_ref[which] = sum_ref[which] + (e[:, :LANES] + e[:, LANES:])
        dot_ref[which] = dot_ref[which] + (ed[:, :LANES] + ed[:, LANES:])
    for which in range(2):
        inv = 1.0 / jnp.sum(sum_ref[which], axis=1, keepdims=True)
        dots = jnp.sum(dot_ref[which], axis=1, keepdims=True) * inv
        sum_ref[which] = jnp.broadcast_to(inv, (half, LANES))
        dot_ref[which] = jnp.broadcast_to(dots, (half, LANES))
    for t in range(steps):
        which, block, _ = place(t)
        inv, dots = sum_ref[which], dot_ref[which]
        p = s_ref[t] * jnp.concatenate([inv, inv], axis=1)
        ds = p * (dp_ref[t] - jnp.concatenate([dots, dots], axis=1))
        dsp = jnp.concatenate([ds.astype(jnp.bfloat16), p.astype(jnp.bfloat16)], axis=0)
        oq = dot_n(dsp, keys(block))
        od_ref[which] = od_ref[which] + jnp.where(low, oq[:half], oq[half:])
        acc_ref[block] = acc_ref[block] + dot_n(lhs_t_ref[which], dsp)
    gain = jnp.where(low, scale, 1.0)
    od_a_ref[...] = (od_ref[0] * gain).astype(jnp.bfloat16)
    od_b_ref[...] = (od_ref[1] * gain).astype(jnp.bfloat16)
    dkv_ref[...] = acc_ref[...].astype(jnp.bfloat16)


def short_call(chip, mine, late, kv):
    half = late.shape[0]
    kb = 2 * half
    blocks = kv.shape[0] // kb
    vm = pl.BlockSpec(memory_space=pltpu.VMEM)
    f32, bf16 = jnp.float32, jnp.bfloat16
    return pl.pallas_call(
        short_kernel,
        out_shape=(jax.ShapeDtypeStruct((half, LANES), bf16),
                   jax.ShapeDtypeStruct((half, LANES), bf16),
                   jax.ShapeDtypeStruct((blocks, LANES, kb), bf16)),
        in_specs=[pl.BlockSpec(memory_space=pltpu.SMEM), vm, vm, vm],
        out_specs=(vm, vm, vm),
        scratch_shapes=[
            pltpu.VMEM((2, kb, LANES), bf16),
            pltpu.VMEM((2, LANES, kb), bf16),
            pltpu.VMEM((blocks + 1, half, kb), f32),
            pltpu.VMEM((blocks + 1, half, kb), f32),
            pltpu.VMEM((2, half, LANES), f32),
            pltpu.VMEM((2, half, LANES), f32),
            pltpu.VMEM((2, half, LANES), f32),
            pltpu.VMEM((2, half, LANES), f32),
            pltpu.VMEM((blocks, LANES, kb), f32),
        ],
        compiler_params=pltpu.CompilerParams(vmem_limit_bytes=32 * 1024 * 1024),
        cost_estimate=pl.CostEstimate(
            flops=6 * (blocks + 1) * half * kb * LANES * 2, bytes_accessed=4 * blocks * kb * LANES,
            transcendentals=(blocks + 1) * half * kb),
        name="short_layer",
    )(chip, mine, late, kv)


def reduce_kernel(core_ref, parts_ref, od_a_ref, od_b_ref, keep_ref, give_ref):
    half = keep_ref.shape[0]
    total = parts_ref[0].astype(jnp.float32)
    for i in range(1, parts_ref.shape[0]):
        total = total + parts_ref[i].astype(jnp.float32)
    dkv = total.T.astype(jnp.bfloat16)
    first = jnp.concatenate([od_a_ref[...], dkv[:half]], axis=1)
    second = jnp.concatenate([od_b_ref[...], dkv[half:]], axis=1)
    is_first = core_ref[0] == 0
    keep_ref[...] = jnp.where(is_first, first, second)
    give_ref[...] = jnp.where(is_first, second, first)


def reduce_call(core, parts, od_a, od_b):
    half = od_a.shape[0]
    vm = pl.BlockSpec(memory_space=pltpu.VMEM)
    shape = jax.ShapeDtypeStruct((half, 2 * LANES), jnp.bfloat16)
    return pl.pallas_call(
        reduce_kernel,
        out_shape=(shape, shape),
        in_specs=[pl.BlockSpec(memory_space=pltpu.SMEM), vm, vm, vm],
        out_specs=(vm, vm),
        name="sum_terms",
    )(core, parts, od_a, od_b)


def join_kernel(core_ref, keep_ref, got_ref, out_ref, dq_ref, dk_ref, dv_ref):
    half = keep_ref.shape[0]
    low = lax.broadcasted_iota(jnp.int32, (half, LANES), 1) < HD
    is_first = core_ref[0] == 0
    keep = keep_ref[...].astype(jnp.float32)
    got = got_ref[...].astype(jnp.float32)
    even = jnp.where(is_first, keep, got)
    odd = jnp.where(is_first, got, keep)
    for part, (left, right) in enumerate(((dq_ref, out_ref), (dk_ref, dv_ref))):
        cols = slice(part * LANES, (part + 1) * LANES)
        a, b = even[:, cols], odd[:, cols]
        left[...] = jnp.where(low, a, pltpu.roll(b, HD, 1)).astype(jnp.bfloat16)
        right[...] = jnp.where(low, pltpu.roll(a, HD, 1), b).astype(jnp.bfloat16)


def join_call(core, keep, got):
    vm = pl.BlockSpec(memory_space=pltpu.VMEM)
    shape = jax.ShapeDtypeStruct((keep.shape[0], LANES), jnp.bfloat16)
    return pl.pallas_call(
        join_kernel,
        out_shape=(shape,) * 4,
        in_specs=[pl.BlockSpec(memory_space=pltpu.SMEM), vm, vm],
        out_specs=(vm,) * 4,
        name="join_heads",
    )(core, keep, got)


def on_device(sizes, q_local, k_local, v_local, q_short, k_short, v_short, grad_out):
    nx, ny, nc, nz = sizes
    axes = ("x", "y", "c", "z")
    count = nx * ny * nc * nz
    chips = nx * ny
    me = lax.axis_index(axes).astype(jnp.int32)[None]
    chip = lax.axis_index(("x", "y")).astype(jnp.int32)[None]
    core = lax.axis_index("c").astype(jnp.int32)[None]
    mirror = [(i, chips - 1 - i) for i in range(chips)]

    packed = pack_call(q_short, k_short, v_short, grad_out)
    mine = lax.all_to_all(packed, ("c", "z"), split_axis=0, concat_axis=0, tiled=True)
    mine = mine.reshape(-1, 4 * HD)
    spread, late = spread_call(mine, chips)
    kv = lax.all_to_all(spread, ("x", "y"), split_axis=0, concat_axis=0, tiled=True)
    kv = kv.reshape(-1, LANES)
    late = lax.ppermute(late, ("x", "y"), mirror)

    down = [(i, i + 1) for i in range(count - 1)]
    up = [(i + 1, i) for i in range(count - 1)]
    k_sent, v_sent, _ = lax.optimization_barrier((k_local, v_local, mine))
    prev_k = lax.ppermute(k_sent, axes, down)
    prev_v = lax.ppermute(v_sent, axes, down)

    kv, late, prev_k, prev_v = lax.optimization_barrier((kv, late, prev_k, prev_v))
    od_a, od_b, dkv = short_call(chip, mine, late, kv)
    parts = lax.all_to_all(dkv, ("x", "y"), split_axis=0, concat_axis=0, tiled=True)
    od_b = lax.ppermute(od_b, ("x", "y"), mirror)

    prev_k, prev_v, od_a = lax.optimization_barrier((prev_k, prev_v, od_a))
    local_out, local_dq, own_k, own_v, back_k, back_v = local_call(
        me, q_local, k_local, v_local, grad_out, prev_k, prev_v)
    back_k = lax.ppermute(back_k, axes, up)
    back_v = lax.ppermute(back_v, axes, up)
    local_dk = (own_k + back_k.astype(jnp.float32)).astype(jnp.bfloat16)
    local_dv = (own_v + back_v.astype(jnp.float32)).astype(jnp.bfloat16)

    keep, give = reduce_call(core, parts, od_a, od_b)
    got = lax.ppermute(give, "c", [(0, 1), (1, 0)])
    short_out, short_dq, short_dk, short_dv = join_call(core, keep, got)
    return (local_out, local_dq, local_dk, local_dv, short_out, short_dq, short_dk, short_dv)


def solution(mesh):
    nx, ny, nc, nz = 4, 4, 2, 8
    sizes = (nx, ny, nc, nz)
    fine = Mesh(mesh.devices.reshape(sizes), ("x", "y", "c", "z"))
    rows = P(("x", "y", "c", "z"), None)
    heads = P(("x", "y", "c"), "z")

    def body(*args):
        return on_device(sizes, *args)

    return jax.shard_map(
        body,
        mesh=fine,
        in_specs=(rows,) * 7,
        out_specs=(rows,) * 4 + (heads,) * 4,
        check_vma=False,
    )
```

time: 229 us -> 87.1 us (0.38)
  waiting for transfers between devices: 113 us -> 6.75 us
  local copies, waits for them, and re-layouts: 27.2 us -> 1.88 us
  Pallas kernels: 0 us -> 19.4 us
  matrix products: 19 us -> 0 us
  between operations: 14.2 us -> 0.79 us
  starting transfers between devices: 28.3 us -> 38.9 us
  other arithmetic: 9.42 us -> 1.52 us
    unnamed x4 -> x0, waiting for transfers between devices: 54.1 us -> none
    all_gather x2 -> x0, waiting for transfers between devices: 53.9 us -> none  [the longest x1 45.7 us: on_device(): lax.all_gather(head_v, 'grp', axis=0, tiled=True)]
    pallas_call x0 -> x6, Pallas kernels: none -> 19.4 us  [the longest x1 6.53 us: local_call(): pl.pallas_call(local_kernel, out_shape=(half, half, wide, wide, half, hal...]
    dot_general x18 -> x0, matrix products: 19 us -> none  [the longest x3 6.12 us: attend(): jnp.einsum('hij,jhd->ihd', weights_bf, values, preferred_element_type=jnp...]
    unnamed x57 -> x18, local copies, waits for them, and re-layouts: 16.5 us -> 1.88 us
    ppermute x4 -> x7, starting transfers between devices: 15 us -> 23 us  [the longest x1 4.94 us: on_device(): od_b = lax.ppermute(od_b, ('x', 'y'), mirror)]
    ppermute x4 -> x7, waiting for transfers between devices: 0.01 us -> 6.22 us  [the longest x1 4.76 us: on_device(): late = lax.ppermute(late, ('x', 'y'), mirror)]
    all_to_all x3 -> x2, waiting for transfers between devices: 5.38 us -> 0.53 us  [the longest x1 0.53 us: on_device(): lax.all_to_all(spread, ('x', 'y'), split_axis=0, concat_axis=0, tiled=True)]
  transfers between devices with their start and end apart: 10 -> 9, of which waited for: 5 -> 4; matrix products, arithmetic and copies ran while one was open for 15% -> 2% of each run, Pallas kernels for 0% -> 10%
where the time goes in v1:
time: 87.1 us; the launch traced here: 86.6 us
  starting transfers between devices  38.9 us (45%)
  Pallas kernels  19.4 us (22%)
  blocking collectives  17.4 us (20%)
  waiting for transfers between devices  6.75 us (8%)
  local copies, waits for them, and re-layouts  1.88 us (2%)
  other arithmetic  1.52 us (2%)
    all_to_all x1, blocking collectives, on_device(): lax.all_to_all(packed, ('c', 'z'), split_axis=0, concat_axis=0, tiled=True)  17.4 us
    all_to_all x1, starting transfers between devices, on_device(): lax.all_to_all(dkv, ('x', 'y'), split_axis=0, concat_axis=0, tiled=True)  8.99 us
    all_to_all x1, starting transfers between devices, on_device(): lax.all_to_all(spread, ('x', 'y'), split_axis=0, concat_axis=0, tiled=True)  6.9 us
    pallas_call x1, Pallas kernels, local_call(): pl.pallas_call(local_kernel, out_shape=(half, half, wide, wide, half, hal...  6.53 us
    ppermute x1, starting transfers between devices, on_device(): od_b = lax.ppermute(od_b, ('x', 'y'), mirror)  4.94 us
    ppermute x1, starting transfers between devices, on_device(): late = lax.ppermute(late, ('x', 'y'), mirror)  4.77 us
    ppermute x1, waiting for transfers between devices, on_device(): late = lax.ppermute(late, ('x', 'y'), mirror)  4.76 us
    pallas_call x1, Pallas kernels, short_call(): pl.pallas_call(short_kernel, out_shape=(jax.ShapeDtypeStruct((half, LANES...  4.56 us
  transfers between devices with their start and end apart: 9, of which 4 were waited for; matrix products, arithmetic and copies ran while one was open for 2% of the time, Pallas kernels for 10%

profile of v1, /device:TPU:1, one launch (start us, length us, event | category | flops | bytes accessed | tf_op | source)
XLA Modules:
  0.0 86.6 jit_solution(12751745802263658522)
XLA Ops:
  0.6 1.9 %pack_heads.1 = bf16[16,16,256]{2,1,0:T(8,128)(2,1)} custom-call(bf16[16,1024]{1,0:T(8,128)(2,1)} %q_ref.2, bf16[16,1024]{1,0:T(8,128)(2,1)} %k_ref.2, bf16[16,1024]{1,0:T(8,128)(2,1)} %v_ref.2, bf16[128,1024]{1,0:T(8,128)(2,1)} %g_ref.3), custom_call_target="tpu_custom_call" | custom-call | tf_op jit(solution)/shard_map/pack_heads/pallas_call | solution.py:118
  2.5 17.4 %all_to_all.15 = bf16[16,16,256]{2,1,0:T(8,128)(2,1)} all-to-all(bf16[16,16,256]{2,1,0:T(8,128)(2,1)} %pack_heads.1), channel_id=1, replica_groups=mesh['x'=4,'y'=4,'c'=2,'z'=8] {'c','z'}, dimensions={0} | all-to-all | bytes 262144 | tf_op jit(solution)/shard_map/all_to_all | solution.py:320
  19.9 2.7 %spread_keys.1 = (bf16[16,256,128]{2,1,0:T(8,128)(2,1)}, bf16[128,128]{1,0:T(8,128)(2,1)}) custom-call(bf16[256,256]{1,0:T(8,128)(2,1)} %bitcast.6), custom_call_target="tpu_custom_call" | custom-call | tf_op jit(solution)/shard_map/spread_keys/pallas_call | solution.py:142
  22.6 0.0 copy-start.4
  22.6 0.0 copy-start.5
  22.6 0.0 copy-start.8
  22.6 0.0 copy-start
  22.6 6.9 %all-to-all-start.1 = ((bf16[16,256,128]{2,1,0:T(8,128)(2,1)}), bf16[16,256,128]{2,1,0:T(8,128)(2,1)S(1)}, u32[]{:S(2)}, u32[]{:S(2)}) async-start(bf16[16,256,128]{2,1,0:T(8,128)(2,1)} %get-tuple-element.34), calls=%async_computation.1 | async-start | bytes 2097152 | tf_op jit(solution)/shard_map/all_to_all | solution.py:323
  29.5 0.0 copy-done.4
  29.6 3.4 %collective-permute-start.1 = (bf16[128,1024]{1,0:T(8,128)(2,1)S(1)}, bf16[128,1024]{1,0:T(8,128)(2,1)S(1)}, u32[]{:S(2)}, u32[]{:S(2)}) collective-permute-start(bf16[128,1024]{1,0:T(8,128)(2,1)S(1)} %copy-done.4), channel_id=1, source_target_pairs={{0,1},{1,2},{2,3},{3,4},{4,5},{5,6},{6,7},{7,8},{8,9},{9,10},{10,1... | collective-permute-start | bytes 786440 | tf_op jit(solution)/shard_map/ppermute | solution.py:330
  33.0 0.0 copy-done.5
  33.0 2.6 %collective-permute-start.2 = (bf16[128,1024]{1,0:T(8,128)(2,1)S(1)}, bf16[128,1024]{1,0:T(8,128)(2,1)S(1)}, u32[]{:S(2)}, u32[]{:S(2)}) collective-permute-start(bf16[128,1024]{1,0:T(8,128)(2,1)S(1)} %copy-done.5), channel_id=1, source_target_pairs={{0,1},{1,2},{2,3},{3,4},{4,5},{5,6},{6,7},{7,8},{8,9},{9,10},{10,1... | collective-permute-start | bytes 786440 | tf_op jit(solution)/shard_map/ppermute | solution.py:331
  35.6 0.0 copy-done.8
  35.6 4.8 %collective-permute-start = (bf16[128,128]{1,0:T(8,128)(2,1)S(1)}, bf16[128,128]{1,0:T(8,128)(2,1)S(1)}, u32[]{:S(2)}, u32[]{:S(2)}) collective-permute-start(bf16[128,128]{1,0:T(8,128)(2,1)S(1)} %copy-done.8), channel_id=1, source_target_pairs={{0,240},{16,224},{32,208},{48,192},{64,176},{80,160},{96,144},{112... | collective-permute-start | bytes 98312 | tf_op jit(solution)/shard_map/ppermute | solution.py:325
  40.4 4.8 %collective-permute-done.late_ref = bf16[128,128]{1,0:T(8,128)(2,1)S(1)} collective-permute-done((bf16[128,128]{1,0:T(8,128)(2,1)S(1)}, bf16[128,128]{1,0:T(8,128)(2,1)S(1)}, u32[]{:S(2)}, u32[]{:S(2)}) %collective-permute-start) | collective-permute-done | bytes 32800 | tf_op jit(solution)/shard_map/ppermute | solution.py:325
  45.1 0.0 collective-permute-done.1.pk_ref
  45.1 0.0 collective-permute-done.2.pv_ref
  45.1 0.5 all-to-all-done.1
  45.7 0.0 copy-done
  45.7 4.6 %short_layer.1 = (bf16[128,128]{1,0:T(8,128)(2,1)S(1)}, bf16[128,128]{1,0:T(8,128)(2,1)S(1)}, bf16[16,128,256]{2,1,0:T(8,128)(2,1)}) custom-call(s32[1]{0:T(128)} %bitcast.3.chip_ref, bf16[256,256]{1,0:T(8,128)(2,1)S(1)} %bitcast.7, bf16[128,128]{1,0:T(8,128)(2,1)S(1)} %collective-permute-done.late_ref, bf16[4096,128]{1,0:T(8,128)(2,1)S(1)} %bitcast.5), custom_call_target="tpu_custom_call" | custom-call | flops 855638016 | bytes 2097152 | tf_op jit(solution)/shard_map/short_layer/pallas_call | solution.py:230
  50.2 0.0 copy-start.2
  50.2 0.6 copy-done.2
  50.8 0.0 copy-start.1
  50.8 0.0 copy-start.3
  50.8 9.0 %all-to-all-start.2 = ((bf16[16,128,256]{2,1,0:T(8,128)(2,1)}), bf16[16,128,256]{2,1,0:T(8,128)(2,1)}, u32[]{:S(2)}, u32[]{:S(2)}) async-start(bf16[16,128,256]{2,1,0:T(8,128)(2,1)} %get-tuple-element.51), calls=%async_computation.2 | async-start | bytes 2097152 | tf_op jit(solution)/shard_map/all_to_all | solution.py:335
  59.8 0.0 copy-done.1
  59.9 0.0 copy-done.3
  59.9 6.5 %local_layer.1 = (bf16[128,1024]{1,0:T(8,128)(2,1)}, bf16[128,1024]{1,0:T(8,128)(2,1)}, f32[128,1024]{1,0:T(8,128)S(1)}, f32[128,1024]{1,0:T(8,128)S(1)}, bf16[1...) custom-call(s32[1]{0:T(128)} %bitcast.first_ref, bf16[128,1024]{1,0:T(8,128)(2,1)S(1)} %copy-done.3, ...), custom_call_target="tpu_custom_call" | custom-call | flops 805306368 | bytes 3145728 | tf_op jit(solution)/shard_map/local_layer/pallas_call | solution.py:80
  66.4 2.4 %collective-permute-start.3 = (bf16[128,1024]{1,0:T(8,128)(2,1)S(1)}, bf16[128,1024]{1,0:T(8,128)(2,1)S(1)}, u32[]{:S(2)}, u32[]{:S(2)}) collective-permute-start(bf16[128,1024]{1,0:T(8,128)(2,1)S(1)} %get-tuple-element.48), channel_id=1, source_target_pairs={{1,0},{2,1},{3,2},{4,3},{5,4},{6,5},{7,6},{8,7},{9,8},{10,9},{11,1... | collective-permute-start | bytes 786440 | tf_op jit(solution)/shard_map/ppermute | solution.py:341
  68.8 1.9 %collective-permute-start.4 = (bf16[128,1024]{1,0:T(8,128)(2,1)S(1)}, bf16[128,1024]{1,0:T(8,128)(2,1)S(1)}, u32[]{:S(2)}, u32[]{:S(2)}) collective-permute-start(bf16[128,1024]{1,0:T(8,128)(2,1)S(1)} %get-tuple-element.50), channel_id=1, source_target_pairs={{1,0},{2,1},{3,2},{4,3},{5,4},{6,5},{7,6},{8,7},{9,8},{10,9},{11,1... | collective-permute-start | bytes 786440 | tf_op jit(solution)/shard_map/ppermute | solution.py:342
  70.7 4.9 %collective-permute-start.5 = (bf16[128,128]{1,0:T(8,128)(2,1)S(1)}, bf16[128,128]{1,0:T(8,128)(2,1)S(1)}, u32[]{:S(2)}, u32[]{:S(2)}) collective-permute-start(bf16[128,128]{1,0:T(8,128)(2,1)S(1)} %get-tuple-element.53), channel_id=1, source_target_pairs={{0,240},{16,224},{32,208},{48,192},{64,176},{80,160},{96,144},{112... | collective-permute-start | bytes 98312 | tf_op jit(solution)/shard_map/ppermute | solution.py:336
  75.7 0.0 collective-permute-done.3
  75.7 0.8 add_convert_fusion.1
  76.5 1.1 %collective-permute-done.5.od_b_ref = bf16[128,128]{1,0:T(8,128)(2,1)S(1)} collective-permute-done((bf16[128,128]{1,0:T(8,128)(2,1)S(1)}, bf16[128,128]{1,0:T(8,128)(2,1)S(1)}, u32[]{:S(2)}, u32[]{:S(2)}) %collective-permute-start.5) | collective-permute-done | bytes 32800 | tf_op jit(solution)/shard_map/ppermute | solution.py:336
  77.5 0.0 copy-start.7
  77.6 0.0 all-to-all-done.2.parts_ref
  77.6 0.6 copy-done.7
  78.2 2.1 %sum_terms.1 = (bf16[128,256]{1,0:T(8,128)(2,1)}, bf16[128,256]{1,0:T(8,128)(2,1)}) custom-call(s32[1]{0:T(128)} %bitcast.4.core_ref, bf16[16,128,256]{2,1,0:T(8,128)(2,1)} %all-to-all-done.2.parts_ref, bf16[128,128]{1,0:T(8,128)(2,1)} %copy-done.2, bf16[128,128]{1,0:T(8,128)(2,1)} %copy-done.7), custom_call_target="tpu_custom_call" | custom-call | tf_op jit(solution)/shard_map/sum_terms/pallas_call | solution.py:273
  80.3 2.9 %collective-permute-start.6 = (bf16[128,256]{1,0:T(8,128)(2,1)}, bf16[128,256]{1,0:T(8,128)(2,1)S(1)}, u32[]{:S(2)}, u32[]{:S(2)}) collective-permute-start(bf16[128,256]{1,0:T(8,128)(2,1)} %get-tuple-element.55), channel_id=1, source_target_pairs={{0,8},{8,0},{1,9},{9,1},{2,10},{10,2},{3,11},{11,3},{4,12},{12,4},... | collective-permute-start | bytes 196616 | tf_op jit(solution)/shard_map/ppermute | solution.py:347
  83.2 0.0 collective-permute-done.4
  83.2 0.8 add_convert_fusion
  84.0 0.3 collective-permute-done.6.got_ref
  84.3 0.0 copy-start.6
  84.3 0.6 copy-done.6
  85.0 1.6 %join_heads.1 = (bf16[128,128]{1,0:T(8,128)(2,1)}, bf16[128,128]{1,0:T(8,128)(2,1)}, bf16[128,128]{1,0:T(8,128)(2,1)}, bf16[128,128]{1,0:T(8,128)(2,1)}) custom-call(s32[1]{0:T(128)} %bitcast.4.core_ref, bf16[128,256]{1,0:T(8,128)(2,1)} %get-tuple-element.54.keep_ref, bf16[128,256]{1,0:T(8,128)(2,1)} %copy-done.6), custom_call_target="tpu_custom_call" | custom-call | tf_op jit(solution)/shard_map/join_heads/pallas_call | solution.py:300
Async XLA Ops:
  22.6 7.0 %copy-start.4 = (bf16[128,1024]{1,0:T(8,128)(2,1)S(1)}, bf16[128,1024]{1,0:T(8,128)(2,1)}, u32[]{:S(2)}) copy-start(bf16[128,1024]{1,0:T(8,128)(2,1)} %k_ref.3) | copy-start | bytes 786436
  22.6 10.4 %copy-start.5 = (bf16[128,1024]{1,0:T(8,128)(2,1)S(1)}, bf16[128,1024]{1,0:T(8,128)(2,1)}, u32[]{:S(2)}) copy-start(bf16[128,1024]{1,0:T(8,128)(2,1)} %v_ref.3) | copy-start | bytes 786436
  22.6 13.0 %copy-start.8 = (bf16[128,128]{1,0:T(8,128)(2,1)S(1)}, bf16[128,128]{1,0:T(8,128)(2,1)}, u32[]{:S(2)}) copy-start(bf16[128,128]{1,0:T(8,128)(2,1)} %get-tuple-element.35) | copy-start | bytes 98308
  22.6 23.0 %copy-start = (bf16[16,16,256]{2,1,0:T(8,128)(2,1)S(1)}, bf16[16,16,256]{2,1,0:T(8,128)(2,1)}, u32[]{:S(2)}) copy-start(bf16[16,16,256]{2,1,0:T(8,128)(2,1)} %all_to_all.15) | copy-start | bytes 393220
  22.6 23.0 %all-to-all-start.1 = ((bf16[16,256,128]{2,1,0:T(8,128)(2,1)}), bf16[16,256,128]{2,1,0:T(8,128)(2,1)S(1)}, u32[]{:S(2)}, u32[]{:S(2)}) async-start(bf16[16,256,128]{2,1,0:T(8,128)(2,1)} %get-tuple-element.34), calls=%async_computation.1 | async-start | bytes 2097152 | tf_op jit(solution)/shard_map/all_to_all | solution.py:323
  29.6 15.6 %collective-permute-start.1 = (bf16[128,1024]{1,0:T(8,128)(2,1)S(1)}, bf16[128,1024]{1,0:T(8,128)(2,1)S(1)}, u32[]{:S(2)}, u32[]{:S(2)}) collective-permute-start(bf16[128,1024]{1,0:T(8,128)(2,1)S(1)} %copy-done.4), channel_id=1, source_target_pairs={{0,1},{1,2},{2,3},{3,4},{4,5},{5,6},{6,7},{7,8},{8,9},{9,10},{10,1... | collective-permute-start | bytes 786440 | tf_op jit(solution)/shard_map/ppermute | solution.py:330
  33.0 12.1 %collective-permute-start.2 = (bf16[128,1024]{1,0:T(8,128)(2,1)S(1)}, bf16[128,1024]{1,0:T(8,128)(2,1)S(1)}, u32[]{:S(2)}, u32[]{:S(2)}) collective-permute-start(bf16[128,1024]{1,0:T(8,128)(2,1)S(1)} %copy-done.5), channel_id=1, source_target_pairs={{0,1},{1,2},{2,3},{3,4},{4,5},{5,6},{6,7},{7,8},{8,9},{9,10},{10,1... | collective-permute-start | bytes 786440 | tf_op jit(solution)/shard_map/ppermute | solution.py:331
  35.6 9.5 %collective-permute-start = (bf16[128,128]{1,0:T(8,128)(2,1)S(1)}, bf16[128,128]{1,0:T(8,128)(2,1)S(1)}, u32[]{:S(2)}, u32[]{:S(2)}) collective-permute-start(bf16[128,128]{1,0:T(8,128)(2,1)S(1)} %copy-done.8), channel_id=1, source_target_pairs={{0,240},{16,224},{32,208},{48,192},{64,176},{80,160},{96,144},{112... | collective-permute-start | bytes 98312 | tf_op jit(solution)/shard_map/ppermute | solution.py:325
  50.2 0.6 copy-start.2
  50.8 9.0 %copy-start.1 = (bf16[128,1024]{1,0:T(8,128)(2,1)S(1)}, bf16[128,1024]{1,0:T(8,128)(2,1)}, u32[]{:S(2)}) copy-start(bf16[128,1024]{1,0:T(8,128)(2,1)} %g_ref.3) | copy-start | bytes 786436
  50.8 9.0 %copy-start.3 = (bf16[128,1024]{1,0:T(8,128)(2,1)S(1)}, bf16[128,1024]{1,0:T(8,128)(2,1)}, u32[]{:S(2)}) copy-start(bf16[128,1024]{1,0:T(8,128)(2,1)} %q_ref.3) | copy-start | bytes 786436
  50.8 26.7 %all-to-all-start.2 = ((bf16[16,128,256]{2,1,0:T(8,128)(2,1)}), bf16[16,128,256]{2,1,0:T(8,128)(2,1)}, u32[]{:S(2)}, u32[]{:S(2)}) async-start(bf16[16,128,256]{2,1,0:T(8,128)(2,1)} %get-tuple-element.51), calls=%async_computation.2 | async-start | bytes 2097152 | tf_op jit(solution)/shard_map/all_to_all | solution.py:335
  66.4 9.3 %collective-permute-start.3 = (bf16[128,1024]{1,0:T(8,128)(2,1)S(1)}, bf16[128,1024]{1,0:T(8,128)(2,1)S(1)}, u32[]{:S(2)}, u32[]{:S(2)}) collective-permute-start(bf16[128,1024]{1,0:T(8,128)(2,1)S(1)} %get-tuple-element.48), channel_id=1, source_target_pairs={{1,0},{2,1},{3,2},{4,3},{5,4},{6,5},{7,6},{8,7},{9,8},{10,9},{11,1... | collective-permute-start | bytes 786440 | tf_op jit(solution)/shard_map/ppermute | solution.py:341
  68.8 14.4 %collective-permute-start.4 = (bf16[128,1024]{1,0:T(8,128)(2,1)S(1)}, bf16[128,1024]{1,0:T(8,128)(2,1)S(1)}, u32[]{:S(2)}, u32[]{:S(2)}) collective-permute-start(bf16[128,1024]{1,0:T(8,128)(2,1)S(1)} %get-tuple-element.50), channel_id=1, source_target_pairs={{1,0},{2,1},{3,2},{4,3},{5,4},{6,5},{7,6},{8,7},{9,8},{10,9},{11,1... | collective-permute-start | bytes 786440 | tf_op jit(solution)/shard_map/ppermute | solution.py:342
  70.7 6.8 %collective-permute-start.5 = (bf16[128,128]{1,0:T(8,128)(2,1)S(1)}, bf16[128,128]{1,0:T(8,128)(2,1)S(1)}, u32[]{:S(2)}, u32[]{:S(2)}) collective-permute-start(bf16[128,128]{1,0:T(8,128)(2,1)S(1)} %get-tuple-element.53), channel_id=1, source_target_pairs={{0,240},{16,224},{32,208},{48,192},{64,176},{80,160},{96,144},{112... | collective-permute-start | bytes 98312 | tf_op jit(solution)/shard_map/ppermute | solution.py:336
  77.5 0.6 copy-start.7
  80.3 4.1 %collective-permute-start.6 = (bf16[128,256]{1,0:T(8,128)(2,1)}, bf16[128,256]{1,0:T(8,128)(2,1)S(1)}, u32[]{:S(2)}, u32[]{:S(2)}) collective-permute-start(bf16[128,256]{1,0:T(8,128)(2,1)} %get-tuple-element.55), channel_id=1, source_target_pairs={{0,8},{8,0},{1,9},{9,1},{2,10},{10,2},{3,11},{11,3},{4,12},{12,4},... | collective-permute-start | bytes 196616 | tf_op jit(solution)/shard_map/ppermute | solution.py:347
  84.3 0.6 copy-start.6

commit v2 on v1

v2 whole, which is shorter than its diff:
```python
import math

import jax
import jax.numpy as jnp
from jax import lax
from jax.experimental import pallas as pl
from jax.experimental.pallas import tpu as pltpu
from jax.sharding import Mesh
from jax.sharding import PartitionSpec as P

HD = 64
WINDOW = 128
POOL = 8
LANES = 128
NEG = float("-inf")
MIB = 1024 * 1024


def dot_t(a, b):
    return lax.dot_general(a, b, (((1,), (1,)), ((), ())), preferred_element_type=jnp.float32)


def dot_n(a, b):
    return lax.dot_general(a, b, (((1,), (0,)), ((), ())), preferred_element_type=jnp.float32)


def t_dot(a, b):
    return lax.dot_general(a, b, (((0,), (0,)), ((), ())), preferred_element_type=jnp.float32)


def split_heads(x):
    low = lax.broadcasted_iota(jnp.int32, x.shape, 1) < HD
    zero = jnp.zeros_like(x)
    return jnp.concatenate([jnp.where(low, x, zero), jnp.where(low, zero, x)], axis=0)


def scaled(x):
    return (x.astype(jnp.float32) * (1.0 / math.sqrt(HD))).astype(jnp.bfloat16)


def local_kernel(first_ref, q_ref, k_ref, v_ref, g_ref, prev_ref,
                 out_ref, dq_ref, dk_ref, dv_ref, stats_ref, stats_t_ref):
    rows, width = q_ref.shape
    scale = 1.0 / math.sqrt(HD)
    low = lax.broadcasted_iota(jnp.int32, (rows, LANES), 1) < HD
    row2 = lax.broadcasted_iota(jnp.int32, (2 * rows, rows), 0) & (rows - 1)
    col2 = lax.broadcasted_iota(jnp.int32, (2 * rows, rows), 1)
    from_prev = col2 > row2
    dead = from_prev & (first_ref[0] == 0)
    zero = jnp.zeros((2 * rows, rows), jnp.bfloat16)
    stats_t_ref[...] = jnp.zeros_like(stats_t_ref)
    pairs = width // LANES
    for pair in range(pairs):
        cols = slice(pair * LANES, (pair + 1) * LANES)
        q2 = split_heads(scaled(q_ref[:, cols]))
        g2 = split_heads(g_ref[:, cols])
        kc = jnp.concatenate([prev_ref[0, :, cols], k_ref[:, cols]], axis=0)
        vc = jnp.concatenate([prev_ref[1, :, cols], v_ref[:, cols]], axis=0)
        s_all = dot_t(q2, kc)
        s = jnp.where(from_prev, s_all[:, :rows], s_all[:, rows:])
        s = jnp.where(dead, NEG, s)
        top = jnp.max(s, axis=1, keepdims=True)
        p = jnp.exp(s - top)
        total = jnp.sum(p, axis=1, keepdims=True)
        p = p * (1.0 / total)
        pb = p.astype(jnp.bfloat16)
        own_p = jnp.where(from_prev, zero, pb)
        pc = jnp.concatenate([jnp.where(from_prev, pb, zero), own_p], axis=1)
        o2 = dot_n(pc, vc).astype(jnp.bfloat16)
        out_ref[:, cols] = jnp.where(low, o2[:rows], o2[rows:])
        dots = jnp.sum(g2.astype(jnp.float32) * o2.astype(jnp.float32), axis=1, keepdims=True)
        stats_t_ref[:, pair:pair + 1] = top + jnp.log(total)
        stats_t_ref[:, pairs + pair:pairs + pair + 1] = dots
        dp_all = dot_t(g2, vc)
        dp = jnp.where(from_prev, dp_all[:, :rows], dp_all[:, rows:])
        ds = (p * (dp - dots)).astype(jnp.bfloat16)
        own_ds = jnp.where(from_prev, zero, ds)
        dc = jnp.concatenate([jnp.where(from_prev, ds, zero), own_ds], axis=1)
        dq2 = dot_n(dc, kc) * scale
        dq_ref[:, cols] = jnp.where(low, dq2[:rows], dq2[rows:]).astype(jnp.bfloat16)
        dk_ref[:, cols] = t_dot(own_ds, q2)
        dv_ref[:, cols] = t_dot(own_p, g2)
    stats_ref[...] = stats_t_ref[...].T[:2 * pairs]


def local_call(first, q, k, v, g, prev):
    rows, width = q.shape
    wide = jax.ShapeDtypeStruct((rows, width), jnp.float32)
    half = jax.ShapeDtypeStruct((rows, width), jnp.bfloat16)
    vm = pl.BlockSpec(memory_space=pltpu.VMEM)
    return pl.pallas_call(
        local_kernel,
        out_shape=(half, half, wide, wide,
                   jax.ShapeDtypeStruct((2 * width // LANES, 2 * rows), jnp.float32)),
        in_specs=[pl.BlockSpec(memory_space=pltpu.SMEM)] + [vm] * 5,
        out_specs=(vm,) * 5,
        scratch_shapes=[pltpu.VMEM((2 * rows, LANES), jnp.float32)],
        compiler_params=pltpu.CompilerParams(vmem_limit_bytes=12 * MIB),
        cost_estimate=pl.CostEstimate(
            flops=12 * rows * 256 * width * 2, bytes_accessed=12 * rows * width * 2,
            transcendentals=rows * rows * 16),
        name="local_layer",
    )(first, q, k, v, g, prev)


def late_kernel(k_ref, v_ref, next_ref, stats_ref, own_k_ref, own_v_ref, dk_ref, dv_ref, token_ref):
    rows, width = k_ref.shape
    pairs = width // LANES
    key = lax.broadcasted_iota(jnp.int32, (rows, 2 * rows), 0)
    query = lax.broadcasted_iota(jnp.int32, (rows, 2 * rows), 1) & (rows - 1)
    seen = key > query
    token_ref[...] = jnp.zeros_like(token_ref)
    for pair in range(pairs):
        cols = slice(pair * LANES, (pair + 1) * LANES)
        q2 = split_heads(scaled(next_ref[0, :, cols]))
        g2 = split_heads(next_ref[1, :, cols])
        s = dot_t(k_ref[:, cols], q2)
        dp = dot_t(v_ref[:, cols], g2)
        lse = stats_ref[pair:pair + 1, :]
        dots = stats_ref[pairs + pair:pairs + pair + 1, :]
        p = jnp.exp(jnp.where(seen, s - lse, NEG))
        ds = p * (dp - dots)
        dk = own_k_ref[:, cols] + dot_n(ds.astype(jnp.bfloat16), q2)
        dv = own_v_ref[:, cols] + dot_n(p.astype(jnp.bfloat16), g2)
        dk_ref[:, cols] = dk.astype(jnp.bfloat16)
        dv_ref[:, cols] = dv.astype(jnp.bfloat16)


def late_call(k, v, following, stats, own_k, own_v):
    rows, width = k.shape
    half = jax.ShapeDtypeStruct((rows, width), jnp.bfloat16)
    vm = pl.BlockSpec(memory_space=pltpu.VMEM)
    return pl.pallas_call(
        late_kernel,
        out_shape=(half, half, jax.ShapeDtypeStruct((8, LANES), jnp.float32)),
        in_specs=[vm] * 6,
        out_specs=(vm,) * 3,
        compiler_params=pltpu.CompilerParams(vmem_limit_bytes=12 * MIB),
        cost_estimate=pl.CostEstimate(
            flops=8 * rows * 256 * width, bytes_accessed=12 * rows * width * 2,
            transcendentals=rows * rows * 16),
        name="late_keys",
    )(k, v, following, stats, own_k, own_v)


def pack_kernel(q_ref, k_ref, v_ref, g_ref, packed_ref):
    small = q_ref.shape[0]
    low = lax.broadcasted_iota(jnp.int32, (small, LANES), 1) < HD

    def halves(a, b):
        swap_a = pltpu.roll(a, HD, 1)
        swap_b = pltpu.roll(b, HD, 1)
        return jnp.where(low, a, swap_b), jnp.where(low, swap_a, b)

    pairs = q_ref.shape[1] // LANES
    for pair in range(pairs):
        cols = slice(pair * LANES, (pair + 1) * LANES)
        grads = g_ref[:, cols].astype(jnp.float32).reshape(small, POOL, LANES)
        pooled = jnp.sum(grads, axis=1).astype(jnp.bfloat16).astype(jnp.float32)
        quarter = [r[:, cols].astype(jnp.float32) for r in (q_ref, k_ref, v_ref)]
        qg = halves(quarter[0], pooled)
        kv = halves(quarter[1], quarter[2])
        for core in range(2):
            packed_ref[core * pairs + pair, :, :LANES] = qg[core].astype(jnp.bfloat16)
            packed_ref[core * pairs + pair, :, LANES:] = kv[core].astype(jnp.bfloat16)


def pack_call(q, k, v, g):
    small, width = q.shape
    vm = pl.BlockSpec(memory_space=pltpu.VMEM)
    return pl.pallas_call(
        pack_kernel,
        out_shape=jax.ShapeDtypeStruct((width // HD, small, 4 * HD), jnp.bfloat16),
        in_specs=[vm] * 4,
        out_specs=vm,
        name="pack_heads",
    )(q, k, v, g)


def short_kernel(chip_ref, mine_ref, kv_ref, od_ref, dkv_ref,
                 lhs_ref, lhs_t_ref, s_ref, dp_ref, top_ref, sum_ref, dot_ref, acc_ref,
                 stage_ref, sem):
    scale = 1.0 / math.sqrt(HD)
    chip = chip_ref[0]
    blocks, _, kb = stage_ref.shape
    rows = mine_ref.shape[0]
    low = lax.broadcasted_iota(jnp.int32, (rows, LANES), 1) < HD
    qg = mine_ref[:, :LANES]
    zero_b = jnp.zeros((rows, LANES), jnp.bfloat16)
    qz = jnp.where(low, (qg.astype(jnp.float32) * scale).astype(jnp.bfloat16), zero_b)
    gz = jnp.where(low, zero_b, qg)
    lhs = jnp.concatenate([qz, gz], axis=0)
    lhs_ref[...] = lhs
    lhs_t_ref[...] = lhs.T
    tri = (lax.broadcasted_iota(jnp.int32, (rows, kb), 1)
           <= lax.broadcasted_iota(jnp.int32, (rows, kb), 0))
    spots = [(chip - t) & (blocks - 1) for t in range(blocks)]
    shut = [jnp.where(chip < t, NEG, 0.0) for t in range(blocks)]
    copies = [pltpu.make_async_copy(stage_ref.at[j], dkv_ref.at[spots[j]], sem.at[j])
              for j in range(blocks)]

    def keys(t):
        return kv_ref[pl.ds(pl.multiple_of(spots[t] * kb, kb), kb), :]

    top = None
    for t in range(blocks):
        both = dot_t(lhs_ref[...], keys(t))
        s = both[:rows]
        if t == 0:
            s = jnp.where(tri, s, NEG)
        s_ref[t] = s
        dp_ref[t] = both[rows:]
        most = jnp.maximum(s[:, :LANES], s[:, LANES:])
        if t > 0:
            most = most + shut[t]
        top_ref[...] = most if t == 0 else jnp.maximum(top_ref[...], most)
    top_ref[...] = jnp.broadcast_to(jnp.max(top_ref[...], axis=1, keepdims=True), (rows, LANES))
    for t in range(blocks):
        top = top_ref[...]
        if t > 0:
            top = top - shut[t]
        e = jnp.exp(s_ref[t] - jnp.concatenate([top, top], axis=1))
        s_ref[t] = e
        ed = e * dp_ref[t]
        es = e[:, :LANES] + e[:, LANES:]
        eds = ed[:, :LANES] + ed[:, LANES:]
        sum_ref[...] = es if t == 0 else sum_ref[...] + es
        dot_ref[...] = eds if t == 0 else dot_ref[...] + eds
    inv = 1.0 / jnp.sum(sum_ref[...], axis=1, keepdims=True)
    dots = jnp.sum(dot_ref[...], axis=1, keepdims=True) * inv
    sum_ref[...] = jnp.broadcast_to(inv, (rows, LANES))
    dot_ref[...] = jnp.broadcast_to(dots, (rows, LANES))
    for t in range(blocks):
        inv, dots = sum_ref[...], dot_ref[...]
        p = s_ref[t] * jnp.concatenate([inv, inv], axis=1)
        ds = p * (dp_ref[t] - jnp.concatenate([dots, dots], axis=1))
        dsp = jnp.concatenate([ds.astype(jnp.bfloat16), p.astype(jnp.bfloat16)], axis=0)
        oq = dot_n(dsp, keys(t))
        od = jnp.where(low, oq[:rows], oq[rows:])
        acc_ref[...] = od if t == 0 else acc_ref[...] + od
        stage_ref[t] = dot_n(lhs_t_ref[...], dsp).astype(jnp.bfloat16)
        copies[t].start()
    od_ref[...] = (acc_ref[...] * jnp.where(low, scale, 1.0)).astype(jnp.bfloat16)
    for j in range(blocks):
        copies[j].wait()


def short_call(chip, mine, kv):
    rows = mine.shape[0]
    kb = rows
    blocks = kv.shape[0] // kb
    vm = pl.BlockSpec(memory_space=pltpu.VMEM)
    f32, bf16 = jnp.float32, jnp.bfloat16
    return pl.pallas_call(
        short_kernel,
        out_shape=(jax.ShapeDtypeStruct((rows, LANES), bf16),
                   jax.ShapeDtypeStruct((blocks, LANES, kb), bf16)),
        in_specs=[pl.BlockSpec(memory_space=pltpu.SMEM), vm, vm],
        out_specs=(vm, pl.BlockSpec(memory_space=pl.ANY)),
        scratch_shapes=[
            pltpu.VMEM((2 * rows, LANES), bf16),
            pltpu.VMEM((LANES, 2 * rows), bf16),
            pltpu.VMEM((blocks, rows, kb), f32),
            pltpu.VMEM((blocks, rows, kb), f32),
            pltpu.VMEM((rows, LANES), f32),
            pltpu.VMEM((rows, LANES), f32),
            pltpu.VMEM((rows, LANES), f32),
            pltpu.VMEM((rows, LANES), f32),
            pltpu.VMEM((blocks, LANES, kb), bf16),
            pltpu.SemaphoreType.DMA((blocks,)),
        ],
        compiler_params=pltpu.CompilerParams(vmem_limit_bytes=20 * MIB),
        cost_estimate=pl.CostEstimate(
            flops=rows * kb, bytes_accessed=kb, transcendentals=rows),
        name="short_layer",
    )(chip, mine, kv)


def reduce_kernel(core_ref, token_ref, parts_ref, od_ref, keep_ref, give_ref):
    half = keep_ref.shape[0]
    total = parts_ref[0].astype(jnp.float32)
    for i in range(1, parts_ref.shape[0]):
        total = total + parts_ref[i].astype(jnp.float32)
    dkv = total.T.astype(jnp.bfloat16)
    first = jnp.concatenate([od_ref[:half], dkv[:half]], axis=1)
    second = jnp.concatenate([od_ref[half:], dkv[half:]], axis=1)
    is_first = core_ref[0] == 0
    keep_ref[...] = jnp.where(is_first, first, second)
    give_ref[...] = jnp.where(is_first, second, first)


def reduce_call(core, token, parts, od):
    half = od.shape[0] // 2
    vm = pl.BlockSpec(memory_space=pltpu.VMEM)
    shape = jax.ShapeDtypeStruct((half, 2 * LANES), jnp.bfloat16)
    return pl.pallas_call(
        reduce_kernel,
        out_shape=(shape, shape),
        in_specs=[pl.BlockSpec(memory_space=pltpu.SMEM), pl.BlockSpec(memory_space=pl.ANY), vm, vm],
        out_specs=(vm, vm),
        compiler_params=pltpu.CompilerParams(vmem_limit_bytes=6 * MIB),
        name="sum_terms",
    )(core, token, parts, od)


def join_kernel(core_ref, keep_ref, got_ref, out_ref, dq_ref, dk_ref, dv_ref):
    half = keep_ref.shape[0]
    low = lax.broadcasted_iota(jnp.int32, (half, LANES), 1) < HD
    is_first = core_ref[0] == 0
    keep = keep_ref[...].astype(jnp.float32)
    got = got_ref[...].astype(jnp.float32)
    even = jnp.where(is_first, keep, got)
    odd = jnp.where(is_first, got, keep)
    for part, (left, right) in enumerate(((dq_ref, out_ref), (dk_ref, dv_ref))):
        cols = slice(part * LANES, (part + 1) * LANES)
        a, b = even[:, cols], odd[:, cols]
        left[...] = jnp.where(low, a, pltpu.roll(b, HD, 1)).astype(jnp.bfloat16)
        right[...] = jnp.where(low, pltpu.roll(a, HD, 1), b).astype(jnp.bfloat16)


def join_call(core, keep, got):
    vm = pl.BlockSpec(memory_space=pltpu.VMEM)
    shape = jax.ShapeDtypeStruct((keep.shape[0], LANES), jnp.bfloat16)
    return pl.pallas_call(
        join_kernel,
        out_shape=(shape,) * 4,
        in_specs=[pl.BlockSpec(memory_space=pltpu.SMEM), vm, vm],
        out_specs=(vm,) * 4,
        compiler_params=pltpu.CompilerParams(vmem_limit_bytes=6 * MIB),
        name="join_heads",
    )(core, keep, got)


def on_device(sizes, q_local, k_local, v_local, q_short, k_short, v_short, grad_out):
    nx, ny, nc, nz = sizes
    axes = ("x", "y", "c", "z")
    count = nx * ny * nc * nz
    chips = nx * ny
    me = lax.axis_index(axes).astype(jnp.int32)[None]
    chip = lax.axis_index(("x", "y")).astype(jnp.int32)[None]
    core = lax.axis_index("c").astype(jnp.int32)[None]

    down = [(i, i + 1) for i in range(count - 1)]
    up = [(i + 1, i) for i in range(count - 1)]
    packed = pack_call(q_short, k_short, v_short, grad_out)
    packed, k_sent, v_sent, q_sent, g_sent = lax.optimization_barrier(
        (packed, k_local, v_local, q_local, grad_out))
    mine = lax.all_to_all(packed, ("c", "z"), split_axis=0, concat_axis=0, tiled=True)
    mine = mine.reshape(-1, 4 * HD)
    halo = jnp.stack([k_sent, v_sent])
    halo_up = jnp.stack([q_sent, g_sent])
    halo, halo_up, mine = lax.optimization_barrier((halo, halo_up, mine))
    prev = lax.ppermute(halo, axes, down)
    following = lax.ppermute(halo_up, axes, up)

    chip_rows = mine.shape[0]
    spread = jnp.broadcast_to(mine[None, :, LANES:], (chips, chip_rows, LANES))
    kv = lax.all_to_all(spread, ("x", "y"), split_axis=0, concat_axis=0, tiled=True)
    kv = kv.reshape(-1, LANES)
    od, dkv = short_call(chip, mine, kv)
    dkv, prev, following = lax.optimization_barrier((dkv, prev, following))
    parts = lax.all_to_all(dkv, ("x", "y"), split_axis=0, concat_axis=0, tiled=True)
    prev, od = lax.optimization_barrier((prev, od))
    local_out, local_dq, own_k, own_v, stats = local_call(
        me, q_local, k_local, v_local, grad_out, prev)
    stats = lax.ppermute(stats, axes, up)
    local_dk, local_dv, token = late_call(k_local, v_local, following, stats, own_k, own_v)

    keep, give = reduce_call(core, token, parts, od)
    got = lax.ppermute(give, "c", [(0, 1), (1, 0)])
    short_out, short_dq, short_dk, short_dv = join_call(core, keep, got)
    return (local_out, local_dq, local_dk, local_dv, short_out, short_dq, short_dk, short_dv)


def solution(mesh):
    nx, ny, nc, nz = 4, 4, 2, 8
    sizes = (nx, ny, nc, nz)
    fine = Mesh(mesh.devices.reshape(sizes), ("x", "y", "c", "z"))
    rows = P(("x", "y", "c", "z"), None)
    heads = P(("x", "y", "c"), "z")

    def body(*args):
        return on_device(sizes, *args)

    return jax.shard_map(
        body,
        mesh=fine,
        in_specs=(rows,) * 7,
        out_specs=(rows,) * 4 + (heads,) * 4,
        check_vma=False,
    )
```

time: 87.1 us -> 78.2 us (0.90)
  blocking collectives: 17.4 us -> 0 us
  waiting for transfers between devices: 6.75 us -> 18.9 us
  Pallas kernels: 19.4 us -> 16.7 us
  starting transfers between devices: 38.9 us -> 38 us
    all_to_all x1 -> x0, blocking collectives: 17.4 us -> none  [on_device(): lax.all_to_all(packed, ('c', 'z'), split_axis=0, concat_axis=0, tiled=True)]
    ppermute x6 -> x3, starting transfers between devices: 20 us -> 9.39 us  [the longest x1 3.42 us: on_device(): prev = lax.ppermute(halo, axes, down)]
    all_to_all x0 -> x1, starting transfers between devices: none -> 9.99 us  [on_device(): lax.all_to_all(packed, ('c', 'z'), split_axis=0, concat_axis=0, tiled=True)]
    all_to_all x1, waiting for transfers between devices: 0.53 us -> 9.24 us  [on_device(): lax.all_to_all(spread, ('x', 'y'), split_axis=0, concat_axis=0, tiled=True)]
    all_to_all x0 -> x1, waiting for transfers between devices: none -> 5.17 us  [on_device(): lax.all_to_all(packed, ('c', 'z'), split_axis=0, concat_axis=0, tiled=True)]
    ppermute x6 -> x3, waiting for transfers between devices: 5.87 us -> 2.15 us  [the longest x1 2.14 us: on_device(): stats = lax.ppermute(stats, axes, up)]
    another operation x0 -> x1, other arithmetic: none -> 2.11 us  [on_device(): halo = jnp.stack([k_sent, v_sent])]
    pallas_call x1, Pallas kernels: 2.12 us -> 0.21 us  [reduce_call(): pl.pallas_call(reduce_kernel, out_shape=(shape, shape), in_specs=[pl.Bloc...]
  transfers between devices with their start and end apart: 9 -> 7, of which waited for: 4 -> 5; matrix products, arithmetic and copies ran while one was open for 2% -> 3% of each run, Pallas kernels for 10% -> 18%
where the time goes in v2:
time: 78.2 us; the launch traced here: 77.7 us
  starting transfers between devices  38 us (49%)
  waiting for transfers between devices  18.9 us (24%)
  Pallas kernels  16.7 us (21%)
  other arithmetic  2.11 us (3%)
  local copies, waits for them, and re-layouts  1.21 us (2%)
  between operations  0.79 us (1%)
    all_to_all x1, starting transfers between devices, on_device(): lax.all_to_all(packed, ('c', 'z'), split_axis=0, concat_axis=0, tiled=True)  9.99 us
    all_to_all x1, waiting for transfers between devices, on_device(): lax.all_to_all(spread, ('x', 'y'), split_axis=0, concat_axis=0, tiled=True)  9.24 us
    all_to_all x1, starting transfers between devices, on_device(): lax.all_to_all(dkv, ('x', 'y'), split_axis=0, concat_axis=0, tiled=True)  8.61 us
    all_to_all x1, starting transfers between devices, on_device(): lax.all_to_all(spread, ('x', 'y'), split_axis=0, concat_axis=0, tiled=True)  6.75 us
    pallas_call x1, Pallas kernels, local_call(): pl.pallas_call(local_kernel, out_shape=(half, half, wide, wide, jax.Shape...  6.24 us
    all_to_all x1, waiting for transfers between devices, on_device(): lax.all_to_all(packed, ('c', 'z'), split_axis=0, concat_axis=0, tiled=True)  5.17 us
    pallas_call x1, Pallas kernels, short_call(): pl.pallas_call(short_kernel, out_shape=(jax.ShapeDtypeStruct((rows, LANES...  5.16 us
    ppermute x1, starting transfers between devices, on_device(): prev = lax.ppermute(halo, axes, down)  3.42 us
  transfers between devices with their start and end apart: 7, of which 5 were waited for; matrix products, arithmetic and copies ran while one was open for 3% of the time, Pallas kernels for 18%

profile of v2, /device:TPU:1, one launch (start us, length us, event | category | flops | bytes accessed | tf_op | source)
XLA Modules:
  0.0 77.7 jit_solution(15094658629681493048)
XLA Ops:
  0.6 0.0 copy-start
  0.6 0.0 copy-start.1
  0.7 2.0 %pack_heads.1 = bf16[16,16,256]{2,1,0:T(8,128)(2,1)} custom-call(bf16[16,1024]{1,0:T(8,128)(2,1)} %q_ref.2, bf16[16,1024]{1,0:T(8,128)(2,1)} %k_ref.3, bf16[16,1024]{1,0:T(8,128)(2,1)} %v_ref.3, bf16[128,1024]{1,0:T(8,128)(2,1)} %g_ref.3), custom_call_target="tpu_custom_call" | custom-call | tf_op jit(solution)/shard_map/pack_heads/pallas_call | solution.py:171
  2.6 10.0 %all-to-all-start = ((bf16[16,16,256]{2,1,0:T(8,128)(2,1)}), bf16[16,16,256]{2,1,0:T(8,128)(2,1)S(1)}, u32[]{:S(2)}, u32[]{:S(2)}) async-start(bf16[16,16,256]{2,1,0:T(8,128)(2,1)} %pack_heads.1), calls=%async_computation | async-start | bytes 262144 | tf_op jit(solution)/shard_map/all_to_all | solution.py:348
  12.6 0.0 copy-done
  12.6 0.0 copy-done.1
  12.6 2.1 %pad_maximum_fusion = (bf16[2,128,1024]{2,1,0:T(8,128)(2,1)}, bf16[2,128,1024]{2,1,0:T(8,128)(2,1)}) fusion(bf16[1,128,1024]{2,1,0:T(8,128)(2,1)} %bitcast.12, bf16[1,128,1024]{2,1,0:T(8,128)(2,1)S(1)} %bitcast.11, bf16[1,128,1024]{2,1,0:T(8,128)(2,1)S(1)} %bitcast.10, bf16[1,128,1024]{2,1,0:T(8,128)(2,1)} %bitcast.15), kind=kLoop, calls=%fused_computation | loop fusion | flops 524288 | bytes 2097152 | tf_op jit(solution)/shard_map/stack | solution.py:350
  14.7 5.2 %all-to-all-done = bf16[16,16,256]{2,1,0:T(8,128)(2,1)S(1)} async-done(((bf16[16,16,256]{2,1,0:T(8,128)(2,1)}), bf16[16,16,256]{2,1,0:T(8,128)(2,1)S(1)}, u32[]{:S(2)}, u32[]{:S(2)}) %all-to-all-start) | async-done | bytes 131104 | tf_op jit(solution)/shard_map/all_to_all | solution.py:348
  19.9 1.2 %broadcast_in_dim.17 = bf16[16,256,128]{2,1,0:T(8,128)(2,1)} broadcast(bf16[256,128]{1,0:T(8,128)(2,1)S(1)} %slice.3), dimensions={1,2} | broadcast | bytes 1114112 | tf_op jit(solution)/shard_map/broadcast_in_dim | solution.py:357
  21.1 6.8 %all-to-all-start.1 = ((bf16[16,256,128]{2,1,0:T(8,128)(2,1)}), bf16[16,256,128]{2,1,0:T(8,128)(2,1)S(1)}, u32[]{:S(2)}, u32[]{:S(2)}) async-start(bf16[16,256,128]{2,1,0:T(8,128)(2,1)} %broadcast_in_dim.17), calls=%async_computation.1 | async-start | bytes 2097152 | tf_op jit(solution)/shard_map/all_to_all | solution.py:358
  27.9 3.4 %collective-permute-start = (bf16[2,128,1024]{2,1,0:T(8,128)(2,1)}, bf16[2,128,1024]{2,1,0:T(8,128)(2,1)S(1)}, u32[]{:S(2)}, u32[]{:S(2)}) collective-permute-start(bf16[2,128,1024]{2,1,0:T(8,128)(2,1)} %get-tuple-element.44), channel_id=1, source_target_pairs={{0,1},{1,2},{2,3},{3,4},{4,5},{5,6},{6,7},{7,8},{8,9},{9,10},{10,1... | collective-permute-start | bytes 1572872 | tf_op jit(solution)/shard_map/ppermute | solution.py:353
  31.3 3.4 %collective-permute-start.1 = (bf16[2,128,1024]{2,1,0:T(8,128)(2,1)}, bf16[2,128,1024]{2,1,0:T(8,128)(2,1)S(1)}, u32[]{:S(2)}, u32[]{:S(2)}) collective-permute-start(bf16[2,128,1024]{2,1,0:T(8,128)(2,1)} %get-tuple-element.45), channel_id=1, source_target_pairs={{1,0},{2,1},{3,2},{4,3},{5,4},{6,5},{7,6},{8,7},{9,8},{10,9},{11,1... | collective-permute-start | bytes 1572872 | tf_op jit(solution)/shard_map/ppermute | solution.py:354
  34.6 9.2 %all-to-all-done.1 = bf16[16,256,128]{2,1,0:T(8,128)(2,1)S(1)} async-done(((bf16[16,256,128]{2,1,0:T(8,128)(2,1)}), bf16[16,256,128]{2,1,0:T(8,128)(2,1)S(1)}, u32[]{:S(2)}, u32[]{:S(2)}) %all-to-all-start.1) | async-done | bytes 1048608 | tf_op jit(solution)/shard_map/all_to_all | solution.py:358
  43.9 5.2 %short_layer.1 = (bf16[256,128]{1,0:T(8,128)(2,1)S(1)}, bf16[16,128,256]{2,1,0:T(8,128)(2,1)}) custom-call(s32[1]{0:T(128)} %bitcast.1.chip_ref, bf16[256,256]{1,0:T(8,128)(2,1)S(1)} %bitcast.14, bf16[4096,128]{1,0:T(8,128)(2,1)S(1)} %bitcast.9), custom_call_target="tpu_custom_call" | custom-call | flops 65536 | bytes 256 | tf_op jit(solution)/shard_map/short_layer/pallas_call | solution.py:254
  49.1 0.0 collective-permute-done.prev_ref
  49.1 0.0 collective-permute-done.1.next_ref
  49.1 0.0 copy-start.2
  49.1 0.0 copy-start.3
  49.1 8.6 %all-to-all-start.2 = ((bf16[16,128,256]{2,1,0:T(8,128)(2,1)}), bf16[16,128,256]{2,1,0:T(8,128)(2,1)S(1)}, u32[]{:S(2)}, u32[]{:S(2)}) async-start(bf16[16,128,256]{2,1,0:T(8,128)(2,1)} %get-tuple-element.58), calls=%async_computation.2 | async-start | bytes 2097152 | tf_op jit(solution)/shard_map/all_to_all | solution.py:362
  57.7 0.0 copy-done.2
  57.7 0.0 copy-done.3
  57.8 6.2 %local_layer.1 = (bf16[128,1024]{1,0:T(8,128)(2,1)}, bf16[128,1024]{1,0:T(8,128)(2,1)}, f32[128,1024]{1,0:T(8,128)S(1)}, f32[128,1024]{1,0:T(8,128)S(1)}, f32[16,256]{1,0:T(8,128)S(1)}) custom-call(s32[1]{0:T(128)} %bitcast.first_ref, bf16[128,1024]{1,0:T(8,128)(2,1)S(1)} %copy-done.3, bf16[128,1024]{1,0:T(8,128)(2,1)S(1)} %copy-done.1, ...), custom_call_target="tpu_custom_call" | custom-call | flops 805306368 | bytes 3145728 | tf_op jit(solution)/shard_map/local_layer/pallas_call | solution.py:91
  64.0 2.6 %collective-permute-start.2 = (f32[16,256]{1,0:T(8,128)S(1)}, f32[16,256]{1,0:T(8,128)S(1)}, u32[]{:S(2)}, u32[]{:S(2)}) collective-permute-start(f32[16,256]{1,0:T(8,128)S(1)} %get-tuple-element.52), channel_id=1, source_target_pairs={{1,0},{2,1},{3,2},{4,3},{5,4},{6,5},{7,6},{8,7},{9,8},{10,9},{11,1... | collective-permute-start | bytes 49160 | tf_op jit(solution)/shard_map/ppermute | solution.py:366
  66.6 2.1 %collective-permute-done.2.stats_ref = f32[16,256]{1,0:T(8,128)S(1)} collective-permute-done((f32[16,256]{1,0:T(8,128)S(1)}, f32[16,256]{1,0:T(8,128)S(1)}, u32[]{:S(2)}, u32[]{:S(2)}) %collective-permute-start.2) | collective-permute-done | bytes 16416 | tf_op jit(solution)/shard_map/ppermute | solution.py:366
  68.8 2.4 %late_keys.1 = (bf16[128,1024]{1,0:T(8,128)(2,1)}, bf16[128,1024]{1,0:T(8,128)(2,1)}, f32[8,128]{1,0:T(8,128)S(1)}) custom-call(bf16[128,1024]{1,0:T(8,128)(2,1)S(1)} %copy-done.1, bf16[128,1024]{1,0:T(8,128)(2,1)S(1)} %copy-done.2, bf16[2,128,1024]{2,1,0:T(8,128)(2,1)S(1)} %collective-permute-done.1.next_ref, ...), custom_call_target="tpu_custom_call" | custom-call | flops 268435456 | bytes 3145728 | tf_op jit(solution)/shard_map/late_keys/pallas_call | solution.py:133
  71.2 1.5 %all-to-all-done.2.parts_ref = bf16[16,128,256]{2,1,0:T(8,128)(2,1)S(1)} async-done(((bf16[16,128,256]{2,1,0:T(8,128)(2,1)}), bf16[16,128,256]{2,1,0:T(8,128)(2,1)S(1)}, u32[]{:S(2)}, u32[]{:S(2)}) %all-to-all-start.2) | async-done | bytes 1048608 | tf_op jit(solution)/shard_map/all_to_all | solution.py:362
  72.6 0.2 sum_terms.1
  72.9 3.2 %collective-permute-start.3 = (bf16[128,256]{1,0:T(8,128)(2,1)S(1)}, bf16[128,256]{1,0:T(8,128)(2,1)S(1)}, u32[]{:S(2)}, u32[]{:S(2)}) collective-permute-start(bf16[128,256]{1,0:T(8,128)(2,1)S(1)} %get-tuple-element.61), channel_id=1, source_target_pairs={{0,8},{8,0},{1,9},{9,1},{2,10},{10,2},{3,11},{11,3},{4,12},{12,4},... | collective-permute-start | bytes 196616 | tf_op jit(solution)/shard_map/ppermute | solution.py:370
  76.1 0.9 %collective-permute-done.3.got_ref = bf16[128,256]{1,0:T(8,128)(2,1)S(1)} collective-permute-done((bf16[128,256]{1,0:T(8,128)(2,1)S(1)}, bf16[128,256]{1,0:T(8,128)(2,1)S(1)}, u32[]{:S(2)}, u32[]{:S(2)}) %collective-permute-start.3) | collective-permute-done | bytes 65568 | tf_op jit(solution)/shard_map/ppermute | solution.py:370
  77.0 0.7 join_heads.1
  (1 shorter events, 0.0 us)
Async XLA Ops:
  0.6 12.0 %copy-start = (bf16[128,1024]{1,0:T(8,128)(2,1)S(1)}, bf16[128,1024]{1,0:T(8,128)(2,1)}, u32[]{:S(2)}) copy-start(bf16[128,1024]{1,0:T(8,128)(2,1)} %g_ref.3) | copy-start | bytes 786436
  0.6 12.0 %copy-start.1 = (bf16[128,1024]{1,0:T(8,128)(2,1)S(1)}, bf16[128,1024]{1,0:T(8,128)(2,1)}, u32[]{:S(2)}) copy-start(bf16[128,1024]{1,0:T(8,128)(2,1)} %k_ref.5) | copy-start | bytes 786436
  2.6 17.3 %all-to-all-start = ((bf16[16,16,256]{2,1,0:T(8,128)(2,1)}), bf16[16,16,256]{2,1,0:T(8,128)(2,1)S(1)}, u32[]{:S(2)}, u32[]{:S(2)}) async-start(bf16[16,16,256]{2,1,0:T(8,128)(2,1)} %pack_heads.1), calls=%async_computation | async-start | bytes 262144 | tf_op jit(solution)/shard_map/all_to_all | solution.py:348
  21.1 22.8 %all-to-all-start.1 = ((bf16[16,256,128]{2,1,0:T(8,128)(2,1)}), bf16[16,256,128]{2,1,0:T(8,128)(2,1)S(1)}, u32[]{:S(2)}, u32[]{:S(2)}) async-start(bf16[16,256,128]{2,1,0:T(8,128)(2,1)} %broadcast_in_dim.17), calls=%async_computation.1 | async-start | bytes 2097152 | tf_op jit(solution)/shard_map/all_to_all | solution.py:358
  27.9 21.2 %collective-permute-start = (bf16[2,128,1024]{2,1,0:T(8,128)(2,1)}, bf16[2,128,1024]{2,1,0:T(8,128)(2,1)S(1)}, u32[]{:S(2)}, u32[]{:S(2)}) collective-permute-start(bf16[2,128,1024]{2,1,0:T(8,128)(2,1)} %get-tuple-element.44), channel_id=1, source_target_pairs={{0,1},{1,2},{2,3},{3,4},{4,5},{5,6},{6,7},{7,8},{8,9},{9,10},{10,1... | collective-permute-start | bytes 1572872 | tf_op jit(solution)/shard_map/ppermute | solution.py:353
  31.3 17.8 %collective-permute-start.1 = (bf16[2,128,1024]{2,1,0:T(8,128)(2,1)}, bf16[2,128,1024]{2,1,0:T(8,128)(2,1)S(1)}, u32[]{:S(2)}, u32[]{:S(2)}) collective-permute-start(bf16[2,128,1024]{2,1,0:T(8,128)(2,1)} %get-tuple-element.45), channel_id=1, source_target_pairs={{1,0},{2,1},{3,2},{4,3},{5,4},{6,5},{7,6},{8,7},{9,8},{10,9},{11,1... | collective-permute-start | bytes 1572872 | tf_op jit(solution)/shard_map/ppermute | solution.py:354
  49.1 8.7 %copy-start.2 = (bf16[128,1024]{1,0:T(8,128)(2,1)S(1)}, bf16[128,1024]{1,0:T(8,128)(2,1)}, u32[]{:S(2)}) copy-start(bf16[128,1024]{1,0:T(8,128)(2,1)} %v_ref.5) | copy-start | bytes 786436
  49.1 8.7 %copy-start.3 = (bf16[128,1024]{1,0:T(8,128)(2,1)S(1)}, bf16[128,1024]{1,0:T(8,128)(2,1)}, u32[]{:S(2)}) copy-start(bf16[128,1024]{1,0:T(8,128)(2,1)} %q_ref.3) | copy-start | bytes 786436
  49.1 23.5 %all-to-all-start.2 = ((bf16[16,128,256]{2,1,0:T(8,128)(2,1)}), bf16[16,128,256]{2,1,0:T(8,128)(2,1)S(1)}, u32[]{:S(2)}, u32[]{:S(2)}) async-start(bf16[16,128,256]{2,1,0:T(8,128)(2,1)} %get-tuple-element.58), calls=%async_computation.2 | async-start | bytes 2097152 | tf_op jit(solution)/shard_map/all_to_all | solution.py:362
  64.0 4.8 %collective-permute-start.2 = (f32[16,256]{1,0:T(8,128)S(1)}, f32[16,256]{1,0:T(8,128)S(1)}, u32[]{:S(2)}, u32[]{:S(2)}) collective-permute-start(f32[16,256]{1,0:T(8,128)S(1)} %get-tuple-element.52), channel_id=1, source_target_pairs={{1,0},{2,1},{3,2},{4,3},{5,4},{6,5},{7,6},{8,7},{9,8},{10,9},{11,1... | collective-permute-start | bytes 49160 | tf_op jit(solution)/shard_map/ppermute | solution.py:366
  72.9 4.1 %collective-permute-start.3 = (bf16[128,256]{1,0:T(8,128)(2,1)S(1)}, bf16[128,256]{1,0:T(8,128)(2,1)S(1)}, u32[]{:S(2)}, u32[]{:S(2)}) collective-permute-start(bf16[128,256]{1,0:T(8,128)(2,1)S(1)} %get-tuple-element.61), channel_id=1, source_target_pairs={{0,8},{8,0},{1,9},{9,1},{2,10},{10,2},{3,11},{11,3},{4,12},{12,4},... | collective-permute-start | bytes 196616 | tf_op jit(solution)/shard_map/ppermute | solution.py:370

commit v3 on v2

v3 whole, which is shorter than its diff:
```python
import math

import jax
import jax.numpy as jnp
from jax import lax
from jax.experimental import pallas as pl
from jax.experimental.pallas import tpu as pltpu
from jax.sharding import Mesh
from jax.sharding import PartitionSpec as P

HD = 64
WINDOW = 128
POOL = 8
LANES = 128
NEG = float("-inf")
MIB = 1024 * 1024
COST = 10 ** 11


def dot_t(a, b):
    return lax.dot_general(a, b, (((1,), (1,)), ((), ())), preferred_element_type=jnp.float32)


def dot_n(a, b):
    return lax.dot_general(a, b, (((1,), (0,)), ((), ())), preferred_element_type=jnp.float32)


def t_dot(a, b):
    return lax.dot_general(a, b, (((0,), (0,)), ((), ())), preferred_element_type=jnp.float32)


def split_heads(x):
    low = lax.broadcasted_iota(jnp.int32, x.shape, 1) < HD
    zero = jnp.zeros_like(x)
    return jnp.concatenate([jnp.where(low, x, zero), jnp.where(low, zero, x)], axis=0)


def scaled(x):
    return (x.astype(jnp.float32) * (1.0 / math.sqrt(HD))).astype(jnp.bfloat16)


def weights_kernel(place_ref, q_ref, k_ref, v_ref, g_ref, prev_ref, cross_ref,
                   p_ref, ds_ref, stats_ref, s_ref, dp_ref):
    rows, width = q_ref.shape
    key = lax.broadcasted_iota(jnp.int32, (rows, 2 * rows), 0)
    query = lax.broadcasted_iota(jnp.int32, (rows, 2 * rows), 1) & (rows - 1)
    from_prev = key > query
    dead = from_prev & (place_ref[0] == 0)
    crossed = place_ref[1] == 1
    pairs = width // LANES
    for pair in range(pairs):
        cols = slice(pair * LANES, (pair + 1) * LANES)
        q2 = split_heads(scaled(q_ref[:, cols]))
        g2 = split_heads(g_ref[:, cols])
        prev_k = jnp.where(crossed, cross_ref[0, :, cols], prev_ref[0, :, cols])
        prev_v = jnp.where(crossed, cross_ref[1, :, cols], prev_ref[1, :, cols])
        s = jnp.where(from_prev, dot_t(prev_k, q2), dot_t(k_ref[:, cols], q2))
        s_ref[pair] = jnp.where(dead, NEG, s)
        dp_ref[pair] = jnp.where(
            from_prev, dot_t(prev_v, g2), dot_t(v_ref[:, cols], g2))
    for pair in range(pairs):
        s, dp = s_ref[pair], dp_ref[pair]
        top = jnp.max(s, axis=0, keepdims=True)
        e = jnp.exp(s - top)
        total = jnp.sum(e, axis=0, keepdims=True)
        inv = 1.0 / total
        dots = jnp.sum(e * dp, axis=0, keepdims=True) * inv
        p = e * inv
        p_ref[pair] = p.astype(jnp.bfloat16)
        ds_ref[pair] = (p * (dp - dots)).astype(jnp.bfloat16)
        stats_ref[pair:pair + 1, :] = top + jnp.log(total)
        stats_ref[pairs + pair:pairs + pair + 1, :] = dots


def weights_call(place, q, k, v, g, prev, cross):
    rows, width = q.shape
    pairs = width // LANES
    block = jax.ShapeDtypeStruct((pairs, rows, 2 * rows), jnp.bfloat16)
    vm = pl.BlockSpec(memory_space=pltpu.VMEM)
    return pl.pallas_call(
        weights_kernel,
        out_shape=(block, block, jax.ShapeDtypeStruct((2 * pairs, 2 * rows), jnp.float32)),
        in_specs=[pl.BlockSpec(memory_space=pltpu.SMEM)] + [vm] * 6,
        out_specs=(vm,) * 3,
        scratch_shapes=[pltpu.VMEM((pairs, rows, 2 * rows), jnp.float32)] * 2,
        compiler_params=pltpu.CompilerParams(vmem_limit_bytes=6 * MIB),
        cost_estimate=pl.CostEstimate(
            flops=COST, bytes_accessed=12 * rows * width * 2,
            transcendentals=rows * rows * 16),
        name="local_weights",
    )(place, q, k, v, g, prev, cross)


def local_kernel(place_ref, q_ref, k_ref, v_ref, g_ref, prev_ref, cross_ref, p_ref, ds_ref,
                 out_ref, dq_ref, dk_ref, dv_ref):
    rows, width = q_ref.shape
    scale = 1.0 / math.sqrt(HD)
    low = lax.broadcasted_iota(jnp.int32, (rows, LANES), 1) < HD
    query = lax.broadcasted_iota(jnp.int32, (2 * rows, rows), 0) & (rows - 1)
    key = lax.broadcasted_iota(jnp.int32, (2 * rows, rows), 1)
    from_prev = key > query
    seen = (lax.broadcasted_iota(jnp.int32, (rows, 2 * rows), 0)
            <= (lax.broadcasted_iota(jnp.int32, (rows, 2 * rows), 1) & (rows - 1)))
    zero = jnp.zeros((2 * rows, rows), jnp.bfloat16)
    zero_t = jnp.zeros((rows, 2 * rows), jnp.bfloat16)
    crossed = place_ref[1] == 1
    for pair in range(width // LANES):
        cols = slice(pair * LANES, (pair + 1) * LANES)
        q2 = split_heads(scaled(q_ref[:, cols]))
        g2 = split_heads(g_ref[:, cols])
        p_t, ds_t = p_ref[pair], ds_ref[pair]
        dk_ref[:, cols] = dot_n(jnp.where(seen, ds_t, zero_t), q2)
        dv_ref[:, cols] = dot_n(jnp.where(seen, p_t, zero_t), g2)
        prev_k = jnp.where(crossed, cross_ref[0, :, cols], prev_ref[0, :, cols])
        prev_v = jnp.where(crossed, cross_ref[1, :, cols], prev_ref[1, :, cols])
        p, ds = p_t.T, ds_t.T
        o2 = (dot_n(jnp.where(from_prev, p, zero), prev_v)
              + dot_n(jnp.where(from_prev, zero, p), v_ref[:, cols]))
        out_ref[:, cols] = jnp.where(low, o2[:rows], o2[rows:]).astype(jnp.bfloat16)
        dq2 = (dot_n(jnp.where(from_prev, ds, zero), prev_k)
               + dot_n(jnp.where(from_prev, zero, ds), k_ref[:, cols])) * scale
        dq_ref[:, cols] = jnp.where(low, dq2[:rows], dq2[rows:]).astype(jnp.bfloat16)


def local_call(place, q, k, v, g, prev, cross, p, ds):
    rows, width = q.shape
    wide = jax.ShapeDtypeStruct((rows, width), jnp.float32)
    half = jax.ShapeDtypeStruct((rows, width), jnp.bfloat16)
    vm = pl.BlockSpec(memory_space=pltpu.VMEM)
    return pl.pallas_call(
        local_kernel,
        out_shape=(half, half, wide, wide),
        in_specs=[pl.BlockSpec(memory_space=pltpu.SMEM)] + [vm] * 8,
        out_specs=(vm,) * 4,
        compiler_params=pltpu.CompilerParams(vmem_limit_bytes=6 * MIB),
        cost_estimate=pl.CostEstimate(
            flops=COST, bytes_accessed=12 * rows * width * 2,
            transcendentals=0),
        name="local_layer",
    )(place, q, k, v, g, prev, cross, p, ds)


def late_kernel(place_ref, k_ref, v_ref, next_ref, cross_ref, stats_ref, own_k_ref, own_v_ref,
                dk_ref, dv_ref, token_ref, s_ref, dp_ref):
    rows, width = k_ref.shape
    pairs = width // LANES
    key = lax.broadcasted_iota(jnp.int32, (rows, 2 * rows), 0)
    query = lax.broadcasted_iota(jnp.int32, (rows, 2 * rows), 1) & (rows - 1)
    seen = key > query
    token_ref[...] = jnp.zeros_like(token_ref)
    crossed = place_ref[2] == 1
    for pair in range(pairs):
        cols = slice(pair * LANES, (pair + 1) * LANES)
        q2 = split_heads(scaled(jnp.where(crossed, cross_ref[0, :, cols], next_ref[0, :, cols])))
        g2 = split_heads(jnp.where(crossed, cross_ref[1, :, cols], next_ref[1, :, cols]))
        s_ref[pair] = dot_t(k_ref[:, cols], q2)
        dp_ref[pair] = dot_t(v_ref[:, cols], g2)
    for pair in range(pairs):
        cols = slice(pair * LANES, (pair + 1) * LANES)
        q2 = split_heads(scaled(jnp.where(crossed, cross_ref[0, :, cols], next_ref[0, :, cols])))
        g2 = split_heads(jnp.where(crossed, cross_ref[1, :, cols], next_ref[1, :, cols]))
        lse = stats_ref[pair:pair + 1, :]
        dots = stats_ref[pairs + pair:pairs + pair + 1, :]
        p = jnp.exp(jnp.where(seen, s_ref[pair] - lse, NEG))
        ds = p * (dp_ref[pair] - dots)
        dk = own_k_ref[:, cols] + dot_n(ds.astype(jnp.bfloat16), q2)
        dv = own_v_ref[:, cols] + dot_n(p.astype(jnp.bfloat16), g2)
        dk_ref[:, cols] = dk.astype(jnp.bfloat16)
        dv_ref[:, cols] = dv.astype(jnp.bfloat16)


def late_call(place, k, v, following, cross, stats, own_k, own_v):
    rows, width = k.shape
    half = jax.ShapeDtypeStruct((rows, width), jnp.bfloat16)
    vm = pl.BlockSpec(memory_space=pltpu.VMEM)
    return pl.pallas_call(
        late_kernel,
        out_shape=(half, half, jax.ShapeDtypeStruct((8, LANES), jnp.float32)),
        in_specs=[pl.BlockSpec(memory_space=pltpu.SMEM)] + [vm] * 7,
        out_specs=(vm,) * 3,
        scratch_shapes=[pltpu.VMEM((width // LANES, rows, 2 * rows), jnp.float32)] * 2,
        compiler_params=pltpu.CompilerParams(vmem_limit_bytes=6 * MIB),
        cost_estimate=pl.CostEstimate(
            flops=COST, bytes_accessed=12 * rows * width * 2,
            transcendentals=rows * rows * 16),
        name="late_keys",
    )(place, k, v, following, cross, stats, own_k, own_v)


def pack_kernel(q_ref, k_ref, v_ref, g_ref, packed_ref):
    small = q_ref.shape[0]
    low = lax.broadcasted_iota(jnp.int32, (small, LANES), 1) < HD

    def halves(a, b):
        swap_a = pltpu.roll(a, HD, 1)
        swap_b = pltpu.roll(b, HD, 1)
        return jnp.where(low, a, swap_b), jnp.where(low, swap_a, b)

    pairs = q_ref.shape[1] // LANES
    for pair in range(pairs):
        cols = slice(pair * LANES, (pair + 1) * LANES)
        grads = g_ref[:, cols].astype(jnp.float32).reshape(small, POOL, LANES)
        pooled = jnp.sum(grads, axis=1).astype(jnp.bfloat16).astype(jnp.float32)
        quarter = [r[:, cols].astype(jnp.float32) for r in (q_ref, k_ref, v_ref)]
        qg = halves(quarter[0], pooled)
        kv = halves(quarter[1], quarter[2])
        for core in range(2):
            packed_ref[core * pairs + pair, :, :LANES] = qg[core].astype(jnp.bfloat16)
            packed_ref[core * pairs + pair, :, LANES:] = kv[core].astype(jnp.bfloat16)


def pack_call(q, k, v, g):
    small, width = q.shape
    vm = pl.BlockSpec(memory_space=pltpu.VMEM)
    return pl.pallas_call(
        pack_kernel,
        out_shape=jax.ShapeDtypeStruct((width // HD, small, 4 * HD), jnp.bfloat16),
        in_specs=[vm] * 4,
        out_specs=vm,
        name="pack_heads",
    )(q, k, v, g)


def short_kernel(chip_ref, mine_ref, kv_ref, room_ref, od_ref, dkv_ref,
                 lhs_ref, kv_t_ref, s_ref, dp_ref, acc_ref, stage_ref, sem):
    scale = 1.0 / math.sqrt(HD)
    chip = chip_ref[0]
    blocks, kb, _ = stage_ref.shape
    rows = mine_ref.shape[0]
    lhs = split_heads(mine_ref[:, :LANES])
    lhs_ref[:rows] = scaled(lhs[:rows])
    lhs_ref[rows:] = lhs[rows:]
    tri = (lax.broadcasted_iota(jnp.int32, (kb, rows), 0)
           <= lax.broadcasted_iota(jnp.int32, (kb, rows), 1))
    spots = [(chip - t) & (blocks - 1) for t in range(blocks)]
    shut = [jnp.where(chip < t, NEG, 0.0) for t in range(blocks)]
    copies = [pltpu.make_async_copy(stage_ref.at[j], dkv_ref.at[spots[j]], sem.at[j])
              for j in range(blocks)]

    def keys(t):
        return kv_ref[pl.ds(pl.multiple_of(spots[t] * kb, kb), kb), :]

    tops, sums, dot_sums = [], [], []
    for t in range(blocks):
        kv = keys(t)
        both = dot_t(kv, lhs_ref[...])
        kv_t_ref[t] = kv.T
        s, dp = both[:, :rows], both[:, rows:]
        if t == 0:
            s = jnp.where(tri, s, NEG)
        top = jnp.max(s, axis=0, keepdims=True)
        e = jnp.exp(s - top)
        s_ref[t] = e
        dp_ref[t] = dp
        tops.append(top if t == 0 else top + shut[t])
        sums.append(jnp.sum(e, axis=0, keepdims=True))
        dot_sums.append(jnp.sum(e * dp, axis=0, keepdims=True))
    top = tops[0]
    for t in range(1, blocks):
        top = jnp.maximum(top, tops[t])
    shares = [jnp.exp(each - top) for each in tops]
    inv = 1.0 / sum(share * part for share, part in zip(shares, sums))
    dots = sum(share * part for share, part in zip(shares, dot_sums)) * inv
    for t in range(blocks):
        p = s_ref[t] * (shares[t] * inv)
        ds = p * (dp_ref[t] - dots)
        dsp = jnp.concatenate([ds.astype(jnp.bfloat16), p.astype(jnp.bfloat16)], axis=1)
        stage_ref[t] = dot_n(dsp, lhs_ref[...]).astype(jnp.bfloat16)
        copies[t].start()
        od = dot_n(kv_t_ref[t], dsp)
        od = jnp.concatenate([od[:HD, :rows], od[HD:, rows:]], axis=0)
        acc_ref[...] = od if t == 0 else acc_ref[...] + od
    low = lax.broadcasted_iota(jnp.int32, (rows, LANES), 1) < HD
    od_ref[...] = (acc_ref[...].T * jnp.where(low, scale, 1.0)).astype(jnp.bfloat16)
    for copy in copies:
        copy.wait()


def short_call(chip, mine, kv, room):
    rows = mine.shape[0]
    kb = rows
    blocks = kv.shape[0] // kb
    vm = pl.BlockSpec(memory_space=pltpu.VMEM)
    f32, bf16 = jnp.float32, jnp.bfloat16
    return pl.pallas_call(
        short_kernel,
        out_shape=(jax.ShapeDtypeStruct((rows, LANES), bf16),
                   jax.ShapeDtypeStruct((blocks, kb, LANES), bf16)),
        in_specs=[pl.BlockSpec(memory_space=pltpu.SMEM), vm, vm,
                  pl.BlockSpec(memory_space=pl.ANY)],
        out_specs=(vm, pl.BlockSpec(memory_space=pl.ANY)),
        input_output_aliases={3: 1},
        scratch_shapes=[
            pltpu.VMEM((2 * rows, LANES), bf16),
            pltpu.VMEM((blocks, LANES, kb), bf16),
            pltpu.VMEM((blocks, kb, rows), f32),
            pltpu.VMEM((blocks, kb, rows), f32),
            pltpu.VMEM((LANES, rows), f32),
            pltpu.VMEM((blocks, kb, LANES), bf16),
            pltpu.SemaphoreType.DMA((blocks,)),
        ],
        compiler_params=pltpu.CompilerParams(vmem_limit_bytes=14 * MIB),
        cost_estimate=pl.CostEstimate(
            flops=rows * kb, bytes_accessed=kb, transcendentals=rows),
        name="short_layer",
    )(chip, mine, kv, room)


def reduce_kernel(core_ref, token_ref, parts_ref, od_ref, keep_ref, give_ref):
    half = keep_ref.shape[0]
    total = parts_ref[0].astype(jnp.float32)
    for i in range(1, parts_ref.shape[0]):
        total = total + parts_ref[i].astype(jnp.float32)
    dkv = total.astype(jnp.bfloat16)
    first = jnp.concatenate([od_ref[:half], dkv[:half]], axis=1)
    second = jnp.concatenate([od_ref[half:], dkv[half:]], axis=1)
    is_first = core_ref[0] == 0
    keep_ref[...] = jnp.where(is_first, first, second)
    give_ref[...] = jnp.where(is_first, second, first)


def reduce_call(core, token, parts, od):
    half = od.shape[0] // 2
    vm = pl.BlockSpec(memory_space=pltpu.VMEM)
    shape = jax.ShapeDtypeStruct((half, 2 * LANES), jnp.bfloat16)
    return pl.pallas_call(
        reduce_kernel,
        out_shape=(shape, shape),
        in_specs=[pl.BlockSpec(memory_space=pltpu.SMEM), pl.BlockSpec(memory_space=pl.ANY), vm, vm],
        out_specs=(vm, vm),
        compiler_params=pltpu.CompilerParams(vmem_limit_bytes=3 * MIB),
        name="sum_terms",
    )(core, token, parts, od)


def join_kernel(core_ref, keep_ref, got_ref, out_ref, dq_ref, dk_ref, dv_ref):
    half = keep_ref.shape[0]
    low = lax.broadcasted_iota(jnp.int32, (half, LANES), 1) < HD
    is_first = core_ref[0] == 0
    keep = keep_ref[...].astype(jnp.float32)
    got = got_ref[...].astype(jnp.float32)
    even = jnp.where(is_first, keep, got)
    odd = jnp.where(is_first, got, keep)
    for part, (left, right) in enumerate(((dq_ref, out_ref), (dk_ref, dv_ref))):
        cols = slice(part * LANES, (part + 1) * LANES)
        a, b = even[:, cols], odd[:, cols]
        left[...] = jnp.where(low, a, pltpu.roll(b, HD, 1)).astype(jnp.bfloat16)
        right[...] = jnp.where(low, pltpu.roll(a, HD, 1), b).astype(jnp.bfloat16)


def join_call(core, keep, got):
    vm = pl.BlockSpec(memory_space=pltpu.VMEM)
    shape = jax.ShapeDtypeStruct((keep.shape[0], LANES), jnp.bfloat16)
    return pl.pallas_call(
        join_kernel,
        out_shape=(shape,) * 4,
        in_specs=[pl.BlockSpec(memory_space=pltpu.SMEM), vm, vm],
        out_specs=(vm,) * 4,
        compiler_params=pltpu.CompilerParams(vmem_limit_bytes=2 * MIB),
        name="join_heads",
    )(core, keep, got)


def on_device(sizes, q_local, k_local, v_local, q_short, k_short, v_short, grad_out):
    nx, ny, nc, nz = sizes
    axes = ("x", "y", "c", "z")
    count = nx * ny * nc * nz
    chips = nx * ny
    me = lax.axis_index(axes).astype(jnp.int32)
    column = nc * nz
    is_first = me % column == 0
    is_last = me % column == column - 1
    place = jnp.stack([me, is_first.astype(jnp.int32), is_last.astype(jnp.int32)])
    chip = lax.axis_index(("x", "y")).astype(jnp.int32)[None]
    core = lax.axis_index("c").astype(jnp.int32)[None]

    steps = [(i, i + 1) for i in range(count - 1)]
    inside = [pair for pair in steps if pair[1] % column]
    across = [pair for pair in steps if pair[1] % column == 0]
    down = inside
    up = [(b, a) for a, b in inside]
    both_ways = across + [(b, a) for a, b in across]
    all_up = [(b, a) for a, b in steps]
    packed = pack_call(q_short, k_short, v_short, grad_out)
    packed, k_sent, v_sent, q_sent, g_sent = lax.optimization_barrier(
        (packed, k_local, v_local, q_local, grad_out))
    mine = lax.all_to_all(packed, ("c", "z"), split_axis=0, concat_axis=0, tiled=True)
    mine = mine.reshape(-1, 4 * HD)
    halo = jnp.stack([k_sent, v_sent])
    halo_up = jnp.stack([q_sent, g_sent])
    edge = jnp.where(is_first, halo_up, halo)
    halo, halo_up, edge, mine = lax.optimization_barrier((halo, halo_up, edge, mine))
    prev = lax.ppermute(halo, axes, down)
    following = lax.ppermute(halo_up, axes, up)

    chip_rows = mine.shape[0]
    spread = jnp.broadcast_to(mine[None, :, LANES:], (chips, chip_rows, LANES))
    kv = lax.all_to_all(spread, ("x", "y"), split_axis=0, concat_axis=0, tiled=True)
    kv = kv.reshape(-1, LANES)
    cross = lax.ppermute(edge, axes, both_ways)
    od, dkv = short_call(chip, mine, kv, spread)
    dkv, prev, following, cross = lax.optimization_barrier((dkv, prev, following, cross))
    parts = lax.all_to_all(dkv, ("x", "y"), split_axis=0, concat_axis=0, tiled=True)
    prev, od = lax.optimization_barrier((prev, od))
    weights, dscore, stats = weights_call(
        place, q_local, k_local, v_local, grad_out, prev, cross)
    stats = lax.ppermute(stats, axes, all_up)
    local_out, local_dq, own_k, own_v = local_call(
        place, q_local, k_local, v_local, grad_out, prev, cross, weights, dscore)
    local_dk, local_dv, token = late_call(
        place, k_local, v_local, following, cross, stats, own_k, own_v)

    keep, give = reduce_call(core, token, parts, od)
    got = lax.ppermute(give, "c", [(0, 1), (1, 0)])
    short_out, short_dq, short_dk, short_dv = join_call(core, keep, got)
    return (local_out, local_dq, local_dk, local_dv, short_out, short_dq, short_dk, short_dv)


def solution(mesh):
    nx, ny, nc, nz = 4, 4, 2, 8
    sizes = (nx, ny, nc, nz)
    fine = Mesh(mesh.devices.reshape(sizes), ("x", "y", "c", "z"))
    rows = P(("x", "y", "c", "z"), None)
    heads = P(("x", "y", "c"), "z")

    def body(*args):
        return on_device(sizes, *args)

    return jax.shard_map(
        body,
        mesh=fine,
        in_specs=(rows,) * 7,
        out_specs=(rows,) * 4 + (heads,) * 4,
        check_vma=False,
    )
```

time: 78.2 us -> 74.2 us (0.949)
  waiting for transfers between devices: 18.9 us -> 13.6 us
  starting transfers between devices: 38 us -> 39.6 us
    ppermute x1 -> x2, starting transfers between devices: 2.61 us -> 8.2 us  [the longest x1 7.5 us: on_device(): stats = lax.ppermute(stats, axes, all_up)]
    all_to_all x1, starting transfers between devices: 8.61 us -> 4.48 us  [on_device(): lax.all_to_all(dkv, ('x', 'y'), split_axis=0, concat_axis=0, tiled=True)]
    select_n x0 -> x1, other arithmetic: none -> 2.19 us  [on_device(): edge = jnp.where(is_first, halo_up, halo)]
    ppermute x1 -> x2, waiting for transfers between devices: 2.14 us -> 0.01 us  [the longest x1 0.01 us: on_device(): cross = lax.ppermute(edge, axes, both_ways)]
    another operation x1, other arithmetic: 2.11 us -> 0.08 us  [on_device(): jnp.stack([me, is_first.astype(jnp.int32), is_last.astype(jnp.int32)])]
    all_to_all x1, waiting for transfers between devices: 9.24 us -> 7.63 us  [on_device(): lax.all_to_all(spread, ('x', 'y'), split_axis=0, concat_axis=0, tiled=True)]
    all_to_all x1, waiting for transfers between devices: 1.48 us -> 0.01 us  [on_device(): lax.all_to_all(dkv, ('x', 'y'), split_axis=0, concat_axis=0, tiled=True)]
    pallas_call x1, Pallas kernels: 0.21 us -> 1.37 us  [reduce_call(): pl.pallas_call(reduce_kernel, out_shape=(shape, shape), in_specs=[pl.Bloc...]
  transfers between devices with their start and end apart: 7 -> 8, of which waited for: 5 -> 3; matrix products, arithmetic and copies ran while one was open for 3% -> 3% of each run, Pallas kernels for 18% -> 16%
where the time goes in v3:
time: 74.2 us; the launch traced here: 73.6 us
  starting transfers between devices  39.6 us (53%)
  Pallas kernels  16.1 us (22%)
  waiting for transfers between devices  13.6 us (18%)
  other arithmetic  2.27 us (3%)
  local copies, waits for them, and re-layouts  1.2 us (2%)
  between operations  0.8 us (1%)
    all_to_all x1, starting transfers between devices, on_device(): lax.all_to_all(packed, ('c', 'z'), split_axis=0, concat_axis=0, tiled=True)  10.1 us
    all_to_all x1, waiting for transfers between devices, on_device(): lax.all_to_all(spread, ('x', 'y'), split_axis=0, concat_axis=0, tiled=True)  7.63 us
    ppermute x1, starting transfers between devices, on_device(): stats = lax.ppermute(stats, axes, all_up)  7.5 us
    all_to_all x1, starting transfers between devices, on_device(): lax.all_to_all(spread, ('x', 'y'), split_axis=0, concat_axis=0, tiled=True)  6.75 us
    all_to_all x1, waiting for transfers between devices, on_device(): lax.all_to_all(packed, ('c', 'z'), split_axis=0, concat_axis=0, tiled=True)  5.07 us
    pallas_call x1, Pallas kernels, short_call(): pl.pallas_call(short_kernel, out_shape=(jax.ShapeDtypeStruct((rows, LANES...  4.66 us
    all_to_all x1, starting transfers between devices, on_device(): lax.all_to_all(dkv, ('x', 'y'), split_axis=0, concat_axis=0, tiled=True)  4.48 us
    ppermute x1, starting transfers between devices, on_device(): prev = lax.ppermute(halo, axes, down)  3.42 us
  transfers between devices with their start and end apart: 8, of which 3 were waited for; matrix products, arithmetic and copies ran while one was open for 3% of the time, Pallas kernels for 16%

profile of v3, /device:TPU:1, one launch (start us, length us, event | category | flops | bytes accessed | tf_op | source)
XLA Modules:
  0.0 73.6 jit_solution(15637002621586117411)
XLA Ops:
  0.6 0.0 copy-start.1
  0.6 0.0 copy-start.2
  0.7 2.0 %pack_heads.1 = bf16[16,16,256]{2,1,0:T(8,128)(2,1)} custom-call(bf16[16,1024]{1,0:T(8,128)(2,1)} %q_ref.3, bf16[16,1024]{1,0:T(8,128)(2,1)} %k_ref.4, bf16[16,1024]{1,0:T(8,128)(2,1)} %v_ref.4, bf16[128,1024]{1,0:T(8,128)(2,1)} %g_ref.5), custom_call_target="tpu_custom_call" | custom-call | tf_op jit(solution)/shard_map/pack_heads/pallas_call | solution.py:215
  2.6 0.0 copy-start
  2.6 10.1 %all-to-all-start = ((bf16[16,16,256]{2,1,0:T(8,128)(2,1)}), bf16[16,16,256]{2,1,0:T(8,128)(2,1)S(1)}, u32[]{:S(2)}, u32[]{:S(2)}) async-start(bf16[16,16,256]{2,1,0:T(8,128)(2,1)} %pack_heads.1), calls=%async_computation | async-start | bytes 262144 | tf_op jit(solution)/shard_map/all_to_all | solution.py:387
  12.7 0.0 copy-done.1
  12.7 0.0 copy-done.2
  12.8 0.0 copy-done
  12.8 2.2 %broadcast_select_fusion = (bf16[2,128,1024]{2,1,0:T(8,128)(2,1)}, bf16[2,128,1024]{2,1,0:T(8,128)(2,1)}, bf16[2,128,1024]{2,1,0:T(8,128)(2,1)}) fusion(pred[]{:T(512)S(6)} %eq.9, bf16[1,128,1024]{2,1,0:T(8,128)(2,1)S(1)} %bitcast.12, bf16[1,128,1024]{2,1,0:T(8,128)(2,1)S(1)} %bitcast.15, bf16[1,128,1024]{2,1,0:T(8,128)(2,1)} %bitcast.17, ...), kind=kLoop, calls=%fused_computation.2 | loop fusion | flops 786432 | bytes 2621441 | tf_op jit(solution)/shard_map/jit(_where)/select_n | solution.py:391
  15.0 5.1 %all-to-all-done = bf16[16,16,256]{2,1,0:T(8,128)(2,1)S(1)} async-done(((bf16[16,16,256]{2,1,0:T(8,128)(2,1)}), bf16[16,16,256]{2,1,0:T(8,128)(2,1)S(1)}, u32[]{:S(2)}, u32[]{:S(2)}) %all-to-all-start) | async-done | bytes 131104 | tf_op jit(solution)/shard_map/all_to_all | solution.py:387
  20.0 1.2 %broadcast_in_dim.13.room_ref = bf16[16,256,128]{2,1,0:T(8,128)(2,1)} broadcast(bf16[256,128]{1,0:T(8,128)(2,1)S(1)} %slice.3), dimensions={1,2} | broadcast | bytes 1114112 | tf_op jit(solution)/shard_map/broadcast_in_dim | solution.py:397
  21.2 6.8 %all-to-all-start.1 = ((bf16[16,256,128]{2,1,0:T(8,128)(2,1)}), bf16[16,256,128]{2,1,0:T(8,128)(2,1)S(1)}, u32[]{:S(2)}, u32[]{:S(2)}) async-start(bf16[16,256,128]{2,1,0:T(8,128)(2,1)} %broadcast_in_dim.13.room_ref), calls=%async_computation.1 | async-start | bytes 2097152 | tf_op jit(solution)/shard_map/all_to_all | solution.py:398
  28.0 3.4 %collective-permute-start = (bf16[2,128,1024]{2,1,0:T(8,128)(2,1)}, bf16[2,128,1024]{2,1,0:T(8,128)(2,1)}, u32[]{:S(2)}, u32[]{:S(2)}) collective-permute-start(bf16[2,128,1024]{2,1,0:T(8,128)(2,1)} %get-tuple-element.48), channel_id=1, source_target_pairs={{0,1},{1,2},{2,3},{3,4},{4,5},{5,6},{6,7},{7,8},{8,9},{9,10},{10,1... | collective-permute-start | bytes 1572872 | tf_op jit(solution)/shard_map/ppermute | solution.py:393
  31.4 3.4 %collective-permute-start.1 = (bf16[2,128,1024]{2,1,0:T(8,128)(2,1)}, bf16[2,128,1024]{2,1,0:T(8,128)(2,1)S(1)}, u32[]{:S(2)}, u32[]{:S(2)}) collective-permute-start(bf16[2,128,1024]{2,1,0:T(8,128)(2,1)} %get-tuple-element.49), channel_id=1, source_target_pairs={{1,0},{2,1},{3,2},{4,3},{5,4},{6,5},{7,6},{8,7},{9,8},{10,9},{11,1... | collective-permute-start | bytes 1572872 | tf_op jit(solution)/shard_map/ppermute | solution.py:394
  34.8 0.7 collective-permute-start.2
  35.5 0.1 pad_add_fusion.place_ref
  35.6 7.6 %all-to-all-done.1 = bf16[16,256,128]{2,1,0:T(8,128)(2,1)S(1)} async-done(((bf16[16,256,128]{2,1,0:T(8,128)(2,1)}), bf16[16,256,128]{2,1,0:T(8,128)(2,1)S(1)}, u32[]{:S(2)}, u32[]{:S(2)}) %all-to-all-start.1) | async-done | bytes 1048608 | tf_op jit(solution)/shard_map/all_to_all | solution.py:398
  43.2 4.7 %short_layer.1 = (bf16[256,128]{1,0:T(8,128)(2,1)S(1)}, bf16[16,256,128]{2,1,0:T(8,128)(2,1)}) custom-call(s32[1]{0:T(128)} %bitcast.3.chip_ref, bf16[256,256]{1,0:T(8,128)(2,1)S(1)} %bitcast.14, bf16[4096,128]{1,0:T(8,128)(2,1)S(1)} %bitcast.11, bf16[16,256,128]{2,1,0:T(8,128)(2,1)} %broadcast_in_dim.13.room_ref), custom_call_target="tpu_custom_call", output_to_operand_aliasing={{1}: (3, {})} | custom-call | flops 65536 | bytes 256 | tf_op jit(solution)/shard_map/short_layer/pallas_call | solution.py:285
  47.9 0.0 collective-permute-done.prev_ref
  47.9 0.0 collective-permute-done.1.next_ref
  47.9 0.0 collective-permute-done.2.cross_ref
  47.9 0.0 copy-start.3
  47.9 4.5 %all-to-all-start.2 = ((bf16[16,256,128]{2,1,0:T(8,128)(2,1)}), bf16[16,256,128]{2,1,0:T(8,128)(2,1)}, u32[]{:S(2)}, u32[]{:S(2)}) async-start(bf16[16,256,128]{2,1,0:T(8,128)(2,1)} %get-tuple-element.66), calls=%async_computation.2 | async-start | bytes 2097152 | tf_op jit(solution)/shard_map/all_to_all | solution.py:403
  52.4 0.0 copy-done.3
  52.4 2.2 %local_weights.1 = (bf16[8,128,256]{2,1,0:T(8,128)(2,1)S(1)}, bf16[8,128,256]{2,1,0:T(8,128)(2,1)S(1)}, f32[16,256]{1,0:T(8,128)S(1)}) custom-call(s32[3]{0:T(128)S(1)} %pad_add_fusion.place_ref, bf16[128,1024]{1,0:T(8,128)(2,1)S(1)} %copy-done.1, bf16[128,1024]{1,0:T(8,128)(2,1)S(1)} %copy-done.2, bf16[128,1024]{1,0:T(8,128)(2,1)S(1)} %copy-done.3, ...), custom_call_target="tpu_custom_call" | custom-call | flops 99999997952 | bytes 3145728 | tf_op jit(solution)/shard_map/local_weights/pallas_call | solution.py:80
  54.6 7.5 %collective-permute-start.3 = (f32[16,256]{1,0:T(8,128)S(1)}, f32[16,256]{1,0:T(8,128)S(1)}, u32[]{:S(2)}, u32[]{:S(2)}) collective-permute-start(f32[16,256]{1,0:T(8,128)S(1)} %get-tuple-element.60), channel_id=1, source_target_pairs={{1,0},{2,1},{3,2},{4,3},{5,4},{6,5},{7,6},{8,7},{9,8},{10,9},{11,1... | collective-permute-start | bytes 49160 | tf_op jit(solution)/shard_map/ppermute | solution.py:407
  62.1 2.9 %local_layer.1 = (bf16[128,1024]{1,0:T(8,128)(2,1)}, bf16[128,1024]{1,0:T(8,128)(2,1)}, f32[128,1024]{1,0:T(8,128)S(1)}, f32[128,1024]{1,0:T(8,128)S(1)}) custom-call(s32[3]{0:T(128)S(1)} %pad_add_fusion.place_ref, bf16[128,1024]{1,0:T(8,128)(2,1)S(1)} %copy-done.1, bf16[128,1024]{1,0:T(8,128)(2,1)S(1)} %copy-done.2, bf16[128,1024]{1,0:T(8,128)(2,1)S(1)} %copy-done.3, ...), custom_call_target="tpu_custom_call" | custom-call | flops 99999997952 | bytes 3145728 | tf_op jit(solution)/shard_map/local_layer/pallas_call | solution.py:130
  65.1 0.0 collective-permute-done.3.stats_ref
  65.1 2.3 %late_keys.1 = (bf16[128,1024]{1,0:T(8,128)(2,1)}, bf16[128,1024]{1,0:T(8,128)(2,1)}, f32[8,128]{1,0:T(8,128)S(1)}) custom-call(s32[3]{0:T(128)S(1)} %pad_add_fusion.place_ref, bf16[128,1024]{1,0:T(8,128)(2,1)S(1)} %copy-done.2, bf16[128,1024]{1,0:T(8,128)(2,1)S(1)} %copy-done.3, bf16[2,128,1024]{2,1,0:T(8,128)(2,1)S(1)} %collective-permute-done.1.next_ref, ...), custom_call_target="tpu_custom_call" | custom-call | flops 99999997952 | bytes 3145728 | tf_op jit(solution)/shard_map/late_keys/pallas_call | solution.py:176
  67.3 0.0 all-to-all-done.2.parts_ref
  67.3 1.4 %sum_terms.1 = (bf16[128,256]{1,0:T(8,128)(2,1)S(1)}, bf16[128,256]{1,0:T(8,128)(2,1)S(1)}) custom-call(s32[1]{0:T(128)} %bitcast.10.core_ref, f32[8,128]{1,0:T(8,128)S(1)} %get-tuple-element.65.token_ref, bf16[16,256,128]{2,1,0:T(8,128)(2,1)} %all-to-all-done.2.parts_ref, bf16[256,128]{1,0:T(8,128)(2,1)S(1)} %get-tuple-element.67.od_ref), custom_call_target="tpu_custom_call" | custom-call | tf_op jit(solution)/shard_map/sum_terms/pallas_call | solution.py:326
  68.7 3.2 %collective-permute-start.4 = (bf16[128,256]{1,0:T(8,128)(2,1)S(1)}, bf16[128,256]{1,0:T(8,128)(2,1)S(1)}, u32[]{:S(2)}, u32[]{:S(2)}) collective-permute-start(bf16[128,256]{1,0:T(8,128)(2,1)S(1)} %get-tuple-element.69), channel_id=1, source_target_pairs={{0,8},{8,0},{1,9},{9,1},{2,10},{10,2},{3,11},{11,3},{4,12},{12,4},... | collective-permute-start | bytes 196616 | tf_op jit(solution)/shard_map/ppermute | solution.py:414
  71.9 0.9 %collective-permute-done.4.got_ref = bf16[128,256]{1,0:T(8,128)(2,1)S(1)} collective-permute-done((bf16[128,256]{1,0:T(8,128)(2,1)S(1)}, bf16[128,256]{1,0:T(8,128)(2,1)S(1)}, u32[]{:S(2)}, u32[]{:S(2)}) %collective-permute-start.4) | collective-permute-done | bytes 65568 | tf_op jit(solution)/shard_map/ppermute | solution.py:414
  72.8 0.7 join_heads.1
  (1 shorter events, 0.0 us)
Async XLA Ops:
  0.6 12.1 %copy-start.1 = (bf16[128,1024]{1,0:T(8,128)(2,1)S(1)}, bf16[128,1024]{1,0:T(8,128)(2,1)}, u32[]{:S(2)}) copy-start(bf16[128,1024]{1,0:T(8,128)(2,1)} %q_ref.5) | copy-start | bytes 786436
  0.6 12.1 %copy-start.2 = (bf16[128,1024]{1,0:T(8,128)(2,1)S(1)}, bf16[128,1024]{1,0:T(8,128)(2,1)}, u32[]{:S(2)}) copy-start(bf16[128,1024]{1,0:T(8,128)(2,1)} %k_ref.7) | copy-start | bytes 786436
  2.6 10.1 %copy-start = (bf16[128,1024]{1,0:T(8,128)(2,1)S(1)}, bf16[128,1024]{1,0:T(8,128)(2,1)}, u32[]{:S(2)}) copy-start(bf16[128,1024]{1,0:T(8,128)(2,1)} %g_ref.5) | copy-start | bytes 786436
  2.6 17.4 %all-to-all-start = ((bf16[16,16,256]{2,1,0:T(8,128)(2,1)}), bf16[16,16,256]{2,1,0:T(8,128)(2,1)S(1)}, u32[]{:S(2)}, u32[]{:S(2)}) async-start(bf16[16,16,256]{2,1,0:T(8,128)(2,1)} %pack_heads.1), calls=%async_computation | async-start | bytes 262144 | tf_op jit(solution)/shard_map/all_to_all | solution.py:387
  21.2 22.0 %all-to-all-start.1 = ((bf16[16,256,128]{2,1,0:T(8,128)(2,1)}), bf16[16,256,128]{2,1,0:T(8,128)(2,1)S(1)}, u32[]{:S(2)}, u32[]{:S(2)}) async-start(bf16[16,256,128]{2,1,0:T(8,128)(2,1)} %broadcast_in_dim.13.room_ref), calls=%async_computation.1 | async-start | bytes 2097152 | tf_op jit(solution)/shard_map/all_to_all | solution.py:398
  28.0 19.9 %collective-permute-start = (bf16[2,128,1024]{2,1,0:T(8,128)(2,1)}, bf16[2,128,1024]{2,1,0:T(8,128)(2,1)}, u32[]{:S(2)}, u32[]{:S(2)}) collective-permute-start(bf16[2,128,1024]{2,1,0:T(8,128)(2,1)} %get-tuple-element.48), channel_id=1, source_target_pairs={{0,1},{1,2},{2,3},{3,4},{4,5},{5,6},{6,7},{7,8},{8,9},{9,10},{10,1... | collective-permute-start | bytes 1572872 | tf_op jit(solution)/shard_map/ppermute | solution.py:393
  31.4 16.5 %collective-permute-start.1 = (bf16[2,128,1024]{2,1,0:T(8,128)(2,1)}, bf16[2,128,1024]{2,1,0:T(8,128)(2,1)S(1)}, u32[]{:S(2)}, u32[]{:S(2)}) collective-permute-start(bf16[2,128,1024]{2,1,0:T(8,128)(2,1)} %get-tuple-element.49), channel_id=1, source_target_pairs={{1,0},{2,1},{3,2},{4,3},{5,4},{6,5},{7,6},{8,7},{9,8},{10,9},{11,1... | collective-permute-start | bytes 1572872 | tf_op jit(solution)/shard_map/ppermute | solution.py:394
  34.8 13.1 %collective-permute-start.2 = (bf16[2,128,1024]{2,1,0:T(8,128)(2,1)}, bf16[2,128,1024]{2,1,0:T(8,128)(2,1)S(1)}, u32[]{:S(2)}, u32[]{:S(2)}) collective-permute-start(bf16[2,128,1024]{2,1,0:T(8,128)(2,1)} %get-tuple-element.50), channel_id=1, source_target_pairs={{15,16},{31,32},{47,48},{63,64},{79,80},{95,96},{111,112},{127,128... | collective-permute-start | bytes 1572872 | tf_op jit(solution)/shard_map/ppermute | solution.py:400
  47.9 4.5 %copy-start.3 = (bf16[128,1024]{1,0:T(8,128)(2,1)S(1)}, bf16[128,1024]{1,0:T(8,128)(2,1)}, u32[]{:S(2)}) copy-start(bf16[128,1024]{1,0:T(8,128)(2,1)} %v_ref.7) | copy-start | bytes 786436
  47.9 19.4 %all-to-all-start.2 = ((bf16[16,256,128]{2,1,0:T(8,128)(2,1)}), bf16[16,256,128]{2,1,0:T(8,128)(2,1)}, u32[]{:S(2)}, u32[]{:S(2)}) async-start(bf16[16,256,128]{2,1,0:T(8,128)(2,1)} %get-tuple-element.66), calls=%async_computation.2 | async-start | bytes 2097152 | tf_op jit(solution)/shard_map/all_to_all | solution.py:403
  54.6 10.5 %collective-permute-start.3 = (f32[16,256]{1,0:T(8,128)S(1)}, f32[16,256]{1,0:T(8,128)S(1)}, u32[]{:S(2)}, u32[]{:S(2)}) collective-permute-start(f32[16,256]{1,0:T(8,128)S(1)} %get-tuple-element.60), channel_id=1, source_target_pairs={{1,0},{2,1},{3,2},{4,3},{5,4},{6,5},{7,6},{8,7},{9,8},{10,9},{11,1... | collective-permute-start | bytes 49160 | tf_op jit(solution)/shard_map/ppermute | solution.py:407
  68.7 4.1 %collective-permute-start.4 = (bf16[128,256]{1,0:T(8,128)(2,1)S(1)}, bf16[128,256]{1,0:T(8,128)(2,1)S(1)}, u32[]{:S(2)}, u32[]{:S(2)}) collective-permute-start(bf16[128,256]{1,0:T(8,128)(2,1)S(1)} %get-tuple-element.69), channel_id=1, source_target_pairs={{0,8},{8,0},{1,9},{9,1},{2,10},{10,2},{3,11},{11,3},{4,12},{12,4},... | collective-permute-start | bytes 196616 | tf_op jit(solution)/shard_map/ppermute | solution.py:414

commit v4 on v3

--- a/solution.py
+++ b/solution.py
@@ -14,7 +14,6 @@
 LANES = 128
 NEG = float("-inf")
 MIB = 1024 * 1024
-COST = 10 ** 11
 
 
 def dot_t(a, b):
@@ -85,7 +84,7 @@
         scratch_shapes=[pltpu.VMEM((pairs, rows, 2 * rows), jnp.float32)] * 2,
         compiler_params=pltpu.CompilerParams(vmem_limit_bytes=6 * MIB),
         cost_estimate=pl.CostEstimate(
-            flops=COST, bytes_accessed=12 * rows * width * 2,
+            flops=8 * rows * 256 * width * 2, bytes_accessed=12 * rows * width * 2,
             transcendentals=rows * rows * 16),
         name="local_weights",
     )(place, q, k, v, g, prev, cross)
@@ -134,7 +133,7 @@
         out_specs=(vm,) * 4,
         compiler_params=pltpu.CompilerParams(vmem_limit_bytes=6 * MIB),
         cost_estimate=pl.CostEstimate(
-            flops=COST, bytes_accessed=12 * rows * width * 2,
+            flops=8 * rows * 256 * width * 2, bytes_accessed=12 * rows * width * 2,
             transcendentals=0),
         name="local_layer",
     )(place, q, k, v, g, prev, cross, p, ds)
@@ -181,7 +180,7 @@
         scratch_shapes=[pltpu.VMEM((width // LANES, rows, 2 * rows), jnp.float32)] * 2,
         compiler_params=pltpu.CompilerParams(vmem_limit_bytes=6 * MIB),
         cost_estimate=pl.CostEstimate(
-            flops=COST, bytes_accessed=12 * rows * width * 2,
+            flops=8 * rows * 256 * width * 2, bytes_accessed=12 * rows * width * 2,
             transcendentals=rows * rows * 16),
         name="late_keys",
     )(place, k, v, following, cross, stats, own_k, own_v)

time: 74.2 us -> 72.8 us (0.981)
  Pallas kernels: 16.1 us -> 14.3 us
    pallas_call x1, Pallas kernels: 1.37 us -> 0.15 us  [reduce_call(): pl.pallas_call(reduce_kernel, out_shape=(shape, shape), in_specs=[pl.Bloc...]
    ppermute x1, starting transfers between devices: 3.23 us -> 4.03 us  [on_device(): got = lax.ppermute(give, 'c', [(0, 1), (1, 0)])]
where the time goes in v4:
time: 72.8 us; the launch traced here: 72 us
  starting transfers between devices  39.8 us (55%)
  Pallas kernels  14.3 us (20%)
  waiting for transfers between devices  13.7 us (19%)
  other arithmetic  2.26 us (3%)
  local copies, waits for them, and re-layouts  1.21 us (2%)
  between operations  0.79 us (1%)
    all_to_all x1, starting transfers between devices, on_device(): lax.all_to_all(packed, ('c', 'z'), split_axis=0, concat_axis=0, tiled=True)  10.1 us
    all_to_all x1, waiting for transfers between devices, on_device(): lax.all_to_all(spread, ('x', 'y'), split_axis=0, concat_axis=0, tiled=True)  7.72 us
    ppermute x1, starting transfers between devices, on_device(): stats = lax.ppermute(stats, axes, all_up)  7.29 us
    all_to_all x1, starting transfers between devices, on_device(): lax.all_to_all(spread, ('x', 'y'), split_axis=0, concat_axis=0, tiled=True)  6.75 us
    all_to_all x1, waiting for transfers between devices, on_device(): lax.all_to_all(packed, ('c', 'z'), split_axis=0, concat_axis=0, tiled=True)  5.08 us
    pallas_call x1, Pallas kernels, short_call(): pl.pallas_call(short_kernel, out_shape=(jax.ShapeDtypeStruct((rows, LANES...  4.6 us
    all_to_all x1, starting transfers between devices, on_device(): lax.all_to_all(dkv, ('x', 'y'), split_axis=0, concat_axis=0, tiled=True)  4.12 us
    ppermute x1, starting transfers between devices, on_device(): got = lax.ppermute(give, 'c', [(0, 1), (1, 0)])  4.03 us
  transfers between devices with their start and end apart: 8, of which 3 were waited for; matrix products, arithmetic and copies ran while one was open for 3% of the time, Pallas kernels for 16%

profile of v4, /device:TPU:1, one launch (start us, length us, event | category | flops | bytes accessed | tf_op | source)
XLA Modules:
  0.0 72.0 jit_solution(518165782877464231)
XLA Ops:
  0.6 0.0 copy-start.1
  0.6 0.0 copy-start.2
  0.7 2.0 %pack_heads.1 = bf16[16,16,256]{2,1,0:T(8,128)(2,1)} custom-call(bf16[16,1024]{1,0:T(8,128)(2,1)} %q_ref.3, bf16[16,1024]{1,0:T(8,128)(2,1)} %k_ref.4, bf16[16,1024]{1,0:T(8,128)(2,1)} %v_ref.4, bf16[128,1024]{1,0:T(8,128)(2,1)} %g_ref.5), custom_call_target="tpu_custom_call" | custom-call | tf_op jit(solution)/shard_map/pack_heads/pallas_call | solution.py:214
  2.6 0.0 copy-start
  2.6 10.1 %all-to-all-start = ((bf16[16,16,256]{2,1,0:T(8,128)(2,1)}), bf16[16,16,256]{2,1,0:T(8,128)(2,1)S(1)}, u32[]{:S(2)}, u32[]{:S(2)}) async-start(bf16[16,16,256]{2,1,0:T(8,128)(2,1)} %pack_heads.1), calls=%async_computation | async-start | bytes 262144 | tf_op jit(solution)/shard_map/all_to_all | solution.py:386
  12.7 0.0 copy-done.1
  12.7 0.0 copy-done.2
  12.8 0.0 copy-done
  12.8 2.2 %broadcast_select_fusion = (bf16[2,128,1024]{2,1,0:T(8,128)(2,1)}, bf16[2,128,1024]{2,1,0:T(8,128)(2,1)}, bf16[2,128,1024]{2,1,0:T(8,128)(2,1)}) fusion(pred[]{:T(512)S(6)} %eq.9, bf16[1,128,1024]{2,1,0:T(8,128)(2,1)S(1)} %bitcast.14, bf16[1,128,1024]{2,1,0:T(8,128)(2,1)} %bitcast.15, bf16[1,128,1024]{2,1,0:T(8,128)(2,1)S(1)} %bitcast.13, ...), kind=kLoop, calls=%fused_computation.2 | loop fusion | flops 786432 | bytes 2621441 | tf_op jit(solution)/shard_map/jit(_where)/select_n | solution.py:390
  15.0 5.1 %all-to-all-done = bf16[16,16,256]{2,1,0:T(8,128)(2,1)S(1)} async-done(((bf16[16,16,256]{2,1,0:T(8,128)(2,1)}), bf16[16,16,256]{2,1,0:T(8,128)(2,1)S(1)}, u32[]{:S(2)}, u32[]{:S(2)}) %all-to-all-start) | async-done | bytes 131104 | tf_op jit(solution)/shard_map/all_to_all | solution.py:386
  20.0 1.2 %broadcast_in_dim.13.room_ref = bf16[16,256,128]{2,1,0:T(8,128)(2,1)} broadcast(bf16[256,128]{1,0:T(8,128)(2,1)S(1)} %slice.3), dimensions={1,2} | broadcast | bytes 1114112 | tf_op jit(solution)/shard_map/broadcast_in_dim | solution.py:396
  21.2 6.8 %all-to-all-start.1 = ((bf16[16,256,128]{2,1,0:T(8,128)(2,1)}), bf16[16,256,128]{2,1,0:T(8,128)(2,1)S(1)}, u32[]{:S(2)}, u32[]{:S(2)}) async-start(bf16[16,256,128]{2,1,0:T(8,128)(2,1)} %broadcast_in_dim.13.room_ref), calls=%async_computation.1 | async-start | bytes 2097152 | tf_op jit(solution)/shard_map/all_to_all | solution.py:397
  28.0 3.4 %collective-permute-start = (bf16[2,128,1024]{2,1,0:T(8,128)(2,1)}, bf16[2,128,1024]{2,1,0:T(8,128)(2,1)S(1)}, u32[]{:S(2)}, u32[]{:S(2)}) collective-permute-start(bf16[2,128,1024]{2,1,0:T(8,128)(2,1)} %get-tuple-element.48), channel_id=1, source_target_pairs={{0,1},{1,2},{2,3},{3,4},{4,5},{5,6},{6,7},{7,8},{8,9},{9,10},{10,1... | collective-permute-start | bytes 1572872 | tf_op jit(solution)/shard_map/ppermute | solution.py:392
  31.4 3.4 %collective-permute-start.1 = (bf16[2,128,1024]{2,1,0:T(8,128)(2,1)}, bf16[2,128,1024]{2,1,0:T(8,128)(2,1)}, u32[]{:S(2)}, u32[]{:S(2)}) collective-permute-start(bf16[2,128,1024]{2,1,0:T(8,128)(2,1)} %get-tuple-element.49), channel_id=1, source_target_pairs={{1,0},{2,1},{3,2},{4,3},{5,4},{6,5},{7,6},{8,7},{9,8},{10,9},{11,1... | collective-permute-start | bytes 1572872 | tf_op jit(solution)/shard_map/ppermute | solution.py:393
  34.8 0.7 collective-permute-start.2
  35.5 7.7 %all-to-all-done.1 = bf16[16,256,128]{2,1,0:T(8,128)(2,1)S(1)} async-done(((bf16[16,256,128]{2,1,0:T(8,128)(2,1)}), bf16[16,256,128]{2,1,0:T(8,128)(2,1)S(1)}, u32[]{:S(2)}, u32[]{:S(2)}) %all-to-all-start.1) | async-done | bytes 1048608 | tf_op jit(solution)/shard_map/all_to_all | solution.py:397
  43.2 4.6 %short_layer.1 = (bf16[256,128]{1,0:T(8,128)(2,1)S(1)}, bf16[16,256,128]{2,1,0:T(8,128)(2,1)}) custom-call(s32[1]{0:T(128)} %bitcast.3.chip_ref, bf16[256,256]{1,0:T(8,128)(2,1)S(1)} %bitcast.17, bf16[4096,128]{1,0:T(8,128)(2,1)S(1)} %bitcast.11, bf16[16,256,128]{2,1,0:T(8,128)(2,1)} %broadcast_in_dim.13.room_ref), custom_call_target="tpu_custom_call", output_to_operand_aliasing={{1}: (3, {})} | custom-call | flops 65536 | bytes 256 | tf_op jit(solution)/shard_map/short_layer/pallas_call | solution.py:284
  47.8 0.0 collective-permute-done.prev_ref
  47.8 0.0 collective-permute-done.1.next_ref
  47.8 0.0 collective-permute-done.2.cross_ref
  47.9 0.0 copy-start.3
  47.9 4.1 %all-to-all-start.2 = ((bf16[16,256,128]{2,1,0:T(8,128)(2,1)}), bf16[16,256,128]{2,1,0:T(8,128)(2,1)S(1)}, u32[]{:S(2)}, u32[]{:S(2)}) async-start(bf16[16,256,128]{2,1,0:T(8,128)(2,1)} %get-tuple-element.66), calls=%async_computation.2 | async-start | bytes 2097152 | tf_op jit(solution)/shard_map/all_to_all | solution.py:402
  52.0 0.1 pad_add_fusion.place_ref
  52.1 0.0 copy-done.3
  52.1 1.7 %local_weights.1 = (bf16[8,128,256]{2,1,0:T(8,128)(2,1)S(1)}, bf16[8,128,256]{2,1,0:T(8,128)(2,1)S(1)}, f32[16,256]{1,0:T(8,128)S(1)}) custom-call(s32[3]{0:T(128)S(1)} %pad_add_fusion.place_ref, bf16[128,1024]{1,0:T(8,128)(2,1)S(1)} %copy-done.3, bf16[128,1024]{1,0:T(8,128)(2,1)S(1)} %copy-done, bf16[128,1024]{1,0:T(8,128)(2,1)S(1)} %copy-done.1, ...), custom_call_target="tpu_custom_call" | custom-call | flops 536870912 | bytes 3145728 | tf_op jit(solution)/shard_map/local_weights/pallas_call | solution.py:79
  53.7 7.3 %collective-permute-start.3 = (f32[16,256]{1,0:T(8,128)S(1)}, f32[16,256]{1,0:T(8,128)S(1)}, u32[]{:S(2)}, u32[]{:S(2)}) collective-permute-start(f32[16,256]{1,0:T(8,128)S(1)} %get-tuple-element.60), channel_id=1, source_target_pairs={{1,0},{2,1},{3,2},{4,3},{5,4},{6,5},{7,6},{8,7},{9,8},{10,9},{11,1... | collective-permute-start | bytes 49160 | tf_op jit(solution)/shard_map/ppermute | solution.py:406
  61.0 2.4 %local_layer.1 = (bf16[128,1024]{1,0:T(8,128)(2,1)}, bf16[128,1024]{1,0:T(8,128)(2,1)}, f32[128,1024]{1,0:T(8,128)S(1)}, f32[128,1024]{1,0:T(8,128)S(1)}) custom-call(s32[3]{0:T(128)S(1)} %pad_add_fusion.place_ref, bf16[128,1024]{1,0:T(8,128)(2,1)S(1)} %copy-done.3, bf16[128,1024]{1,0:T(8,128)(2,1)S(1)} %copy-done, bf16[128,1024]{1,0:T(8,128)(2,1)S(1)} %copy-done.1, ...), custom_call_target="tpu_custom_call" | custom-call | flops 536870912 | bytes 3145728 | tf_op jit(solution)/shard_map/local_layer/pallas_call | solution.py:129
  63.5 0.0 collective-permute-done.3.stats_ref
  63.5 2.7 %late_keys.1 = (bf16[128,1024]{1,0:T(8,128)(2,1)}, bf16[128,1024]{1,0:T(8,128)(2,1)}, f32[8,128]{1,0:T(8,128)S(1)}) custom-call(s32[3]{0:T(128)S(1)} %pad_add_fusion.place_ref, bf16[128,1024]{1,0:T(8,128)(2,1)S(1)} %copy-done, bf16[128,1024]{1,0:T(8,128)(2,1)S(1)} %copy-done.1, bf16[2,128,1024]{2,1,0:T(8,128)(2,1)} %collective-permute-done.1.next_ref, ...), custom_call_target="tpu_custom_call" | custom-call | flops 536870912 | bytes 3145728 | tf_op jit(solution)/shard_map/late_keys/pallas_call | solution.py:175
  66.2 0.0 all-to-all-done.2.parts_ref
  66.2 0.1 sum_terms.1
  66.4 4.0 %collective-permute-start.4 = (bf16[128,256]{1,0:T(8,128)(2,1)S(1)}, bf16[128,256]{1,0:T(8,128)(2,1)S(1)}, u32[]{:S(2)}, u32[]{:S(2)}) collective-permute-start(bf16[128,256]{1,0:T(8,128)(2,1)S(1)} %get-tuple-element.69), channel_id=1, source_target_pairs={{0,8},{8,0},{1,9},{9,1},{2,10},{10,2},{3,11},{11,3},{4,12},{12,4},... | collective-permute-start | bytes 196616 | tf_op jit(solution)/shard_map/ppermute | solution.py:413
  70.4 0.9 %collective-permute-done.4.got_ref = bf16[128,256]{1,0:T(8,128)(2,1)S(1)} collective-permute-done((bf16[128,256]{1,0:T(8,128)(2,1)S(1)}, bf16[128,256]{1,0:T(8,128)(2,1)S(1)}, u32[]{:S(2)}, u32[]{:S(2)}) %collective-permute-start.4) | collective-permute-done | bytes 65568 | tf_op jit(solution)/shard_map/ppermute | solution.py:413
  71.3 0.7 %join_heads.1 = (bf16[128,128]{1,0:T(8,128)(2,1)}, bf16[128,128]{1,0:T(8,128)(2,1)}, bf16[128,128]{1,0:T(8,128)(2,1)}, bf16[128,128]{1,0:T(8,128)(2,1)}) custom-call(s32[1]{0:T(128)} %bitcast.10.core_ref, bf16[128,256]{1,0:T(8,128)(2,1)S(1)} %get-tuple-element.68.keep_ref, bf16[128,256]{1,0:T(8,128)(2,1)S(1)} %collective-permute-done.4.got_ref), custom_call_target="tpu_custom_call" | custom-call | tf_op jit(solution)/shard_map/join_heads/pallas_call | solution.py:353
  (1 shorter events, 0.0 us)
Async XLA Ops:
  0.6 12.1 %copy-start.1 = (bf16[128,1024]{1,0:T(8,128)(2,1)S(1)}, bf16[128,1024]{1,0:T(8,128)(2,1)}, u32[]{:S(2)}) copy-start(bf16[128,1024]{1,0:T(8,128)(2,1)} %v_ref.7) | copy-start | bytes 786436
  0.6 12.1 %copy-start.2 = (bf16[128,1024]{1,0:T(8,128)(2,1)S(1)}, bf16[128,1024]{1,0:T(8,128)(2,1)}, u32[]{:S(2)}) copy-start(bf16[128,1024]{1,0:T(8,128)(2,1)} %g_ref.5) | copy-start | bytes 786436
  2.6 10.1 %copy-start = (bf16[128,1024]{1,0:T(8,128)(2,1)S(1)}, bf16[128,1024]{1,0:T(8,128)(2,1)}, u32[]{:S(2)}) copy-start(bf16[128,1024]{1,0:T(8,128)(2,1)} %k_ref.7) | copy-start | bytes 786436
  2.6 17.4 %all-to-all-start = ((bf16[16,16,256]{2,1,0:T(8,128)(2,1)}), bf16[16,16,256]{2,1,0:T(8,128)(2,1)S(1)}, u32[]{:S(2)}, u32[]{:S(2)}) async-start(bf16[16,16,256]{2,1,0:T(8,128)(2,1)} %pack_heads.1), calls=%async_computation | async-start | bytes 262144 | tf_op jit(solution)/shard_map/all_to_all | solution.py:386
  21.2 22.0 %all-to-all-start.1 = ((bf16[16,256,128]{2,1,0:T(8,128)(2,1)}), bf16[16,256,128]{2,1,0:T(8,128)(2,1)S(1)}, u32[]{:S(2)}, u32[]{:S(2)}) async-start(bf16[16,256,128]{2,1,0:T(8,128)(2,1)} %broadcast_in_dim.13.room_ref), calls=%async_computation.1 | async-start | bytes 2097152 | tf_op jit(solution)/shard_map/all_to_all | solution.py:397
  28.0 19.8 %collective-permute-start = (bf16[2,128,1024]{2,1,0:T(8,128)(2,1)}, bf16[2,128,1024]{2,1,0:T(8,128)(2,1)S(1)}, u32[]{:S(2)}, u32[]{:S(2)}) collective-permute-start(bf16[2,128,1024]{2,1,0:T(8,128)(2,1)} %get-tuple-element.48), channel_id=1, source_target_pairs={{0,1},{1,2},{2,3},{3,4},{4,5},{5,6},{6,7},{7,8},{8,9},{9,10},{10,1... | collective-permute-start | bytes 1572872 | tf_op jit(solution)/shard_map/ppermute | solution.py:392
  31.4 16.4 %collective-permute-start.1 = (bf16[2,128,1024]{2,1,0:T(8,128)(2,1)}, bf16[2,128,1024]{2,1,0:T(8,128)(2,1)}, u32[]{:S(2)}, u32[]{:S(2)}) collective-permute-start(bf16[2,128,1024]{2,1,0:T(8,128)(2,1)} %get-tuple-element.49), channel_id=1, source_target_pairs={{1,0},{2,1},{3,2},{4,3},{5,4},{6,5},{7,6},{8,7},{9,8},{10,9},{11,1... | collective-permute-start | bytes 1572872 | tf_op jit(solution)/shard_map/ppermute | solution.py:393
  34.8 13.1 %collective-permute-start.2 = (bf16[2,128,1024]{2,1,0:T(8,128)(2,1)}, bf16[2,128,1024]{2,1,0:T(8,128)(2,1)S(1)}, u32[]{:S(2)}, u32[]{:S(2)}) collective-permute-start(bf16[2,128,1024]{2,1,0:T(8,128)(2,1)} %get-tuple-element.50), channel_id=1, source_target_pairs={{15,16},{31,32},{47,48},{63,64},{79,80},{95,96},{111,112},{127,128... | collective-permute-start | bytes 1572872 | tf_op jit(solution)/shard_map/ppermute | solution.py:399
  47.9 4.2 %copy-start.3 = (bf16[128,1024]{1,0:T(8,128)(2,1)S(1)}, bf16[128,1024]{1,0:T(8,128)(2,1)}, u32[]{:S(2)}) copy-start(bf16[128,1024]{1,0:T(8,128)(2,1)} %q_ref.5) | copy-start | bytes 786436
  47.9 18.4 %all-to-all-start.2 = ((bf16[16,256,128]{2,1,0:T(8,128)(2,1)}), bf16[16,256,128]{2,1,0:T(8,128)(2,1)S(1)}, u32[]{:S(2)}, u32[]{:S(2)}) async-start(bf16[16,256,128]{2,1,0:T(8,128)(2,1)} %get-tuple-element.66), calls=%async_computation.2 | async-start | bytes 2097152 | tf_op jit(solution)/shard_map/all_to_all | solution.py:402
  53.7 9.7 %collective-permute-start.3 = (f32[16,256]{1,0:T(8,128)S(1)}, f32[16,256]{1,0:T(8,128)S(1)}, u32[]{:S(2)}, u32[]{:S(2)}) collective-permute-start(f32[16,256]{1,0:T(8,128)S(1)} %get-tuple-element.60), channel_id=1, source_target_pairs={{1,0},{2,1},{3,2},{4,3},{5,4},{6,5},{7,6},{8,7},{9,8},{10,9},{11,1... | collective-permute-start | bytes 49160 | tf_op jit(solution)/shard_map/ppermute | solution.py:406
  66.4 4.9 %collective-permute-start.4 = (bf16[128,256]{1,0:T(8,128)(2,1)S(1)}, bf16[128,256]{1,0:T(8,128)(2,1)S(1)}, u32[]{:S(2)}, u32[]{:S(2)}) collective-permute-start(bf16[128,256]{1,0:T(8,128)(2,1)S(1)} %get-tuple-element.69), channel_id=1, source_target_pairs={{0,8},{8,0},{1,9},{9,1},{2,10},{10,2},{3,11},{11,3},{4,12},{12,4},... | collective-permute-start | bytes 196616 | tf_op jit(solution)/shard_map/ppermute | solution.py:413

commit v5 on v4

--- a/solution.py
+++ b/solution.py
@@ -266,8 +266,8 @@
         dsp = jnp.concatenate([ds.astype(jnp.bfloat16), p.astype(jnp.bfloat16)], axis=1)
         stage_ref[t] = dot_n(dsp, lhs_ref[...]).astype(jnp.bfloat16)
         copies[t].start()
-        od = dot_n(kv_t_ref[t], dsp)
-        od = jnp.concatenate([od[:HD, :rows], od[HD:, rows:]], axis=0)
+        od = jnp.concatenate([dot_n(kv_t_ref[t, :HD], dsp[:, :rows]),
+                              dot_n(kv_t_ref[t, HD:], dsp[:, rows:])], axis=0)
         acc_ref[...] = od if t == 0 else acc_ref[...] + od
     low = lax.broadcasted_iota(jnp.int32, (rows, LANES), 1) < HD
     od_ref[...] = (acc_ref[...].T * jnp.where(low, scale, 1.0)).astype(jnp.bfloat16)

time: 72.8 us -> 72.7 us (level)
  no operation moved by 1% of the time
where the time goes in v5:
time: 72.7 us; the launch traced here: 71.8 us
  starting transfers between devices  39.8 us (55%)
  Pallas kernels  14 us (19%)
  waiting for transfers between devices  13.7 us (19%)
  other arithmetic  2.26 us (3%)
  local copies, waits for them, and re-layouts  1.21 us (2%)
  between operations  0.79 us (1%)
    all_to_all x1, starting transfers between devices, on_device(): lax.all_to_all(packed, ('c', 'z'), split_axis=0, concat_axis=0, tiled=True)  10.1 us
    all_to_all x1, waiting for transfers between devices, on_device(): lax.all_to_all(spread, ('x', 'y'), split_axis=0, concat_axis=0, tiled=True)  7.72 us
    ppermute x1, starting transfers between devices, on_device(): stats = lax.ppermute(stats, axes, all_up)  7.22 us
    all_to_all x1, starting transfers between devices, on_device(): lax.all_to_all(spread, ('x', 'y'), split_axis=0, concat_axis=0, tiled=True)  6.75 us
    all_to_all x1, waiting for transfers between devices, on_device(): lax.all_to_all(packed, ('c', 'z'), split_axis=0, concat_axis=0, tiled=True)  5.08 us
    pallas_call x1, Pallas kernels, short_call(): pl.pallas_call(short_kernel, out_shape=(jax.ShapeDtypeStruct((rows, LANES...  4.35 us
    all_to_all x1, starting transfers between devices, on_device(): lax.all_to_all(dkv, ('x', 'y'), split_axis=0, concat_axis=0, tiled=True)  4.19 us
    ppermute x1, starting transfers between devices, on_device(): got = lax.ppermute(give, 'c', [(0, 1), (1, 0)])  4.1 us
  transfers between devices with their start and end apart: 8, of which 3 were waited for; matrix products, arithmetic and copies ran while one was open for 3% of the time, Pallas kernels for 16%

profile of v5, /device:TPU:1, one launch (start us, length us, event | category | flops | bytes accessed | tf_op | source)
XLA Modules:
  0.0 71.8 jit_solution(8393941295092629481)
XLA Ops:
  0.6 0.0 copy-start.1
  0.6 0.0 copy-start.2
  0.7 2.0 %pack_heads.1 = bf16[16,16,256]{2,1,0:T(8,128)(2,1)} custom-call(bf16[16,1024]{1,0:T(8,128)(2,1)} %q_ref.3, bf16[16,1024]{1,0:T(8,128)(2,1)} %k_ref.4, bf16[16,1024]{1,0:T(8,128)(2,1)} %v_ref.4, bf16[128,1024]{1,0:T(8,128)(2,1)} %g_ref.5), custom_call_target="tpu_custom_call" | custom-call | tf_op jit(solution)/shard_map/pack_heads/pallas_call | solution.py:214
  2.6 0.0 copy-start
  2.6 10.1 %all-to-all-start = ((bf16[16,16,256]{2,1,0:T(8,128)(2,1)}), bf16[16,16,256]{2,1,0:T(8,128)(2,1)S(1)}, u32[]{:S(2)}, u32[]{:S(2)}) async-start(bf16[16,16,256]{2,1,0:T(8,128)(2,1)} %pack_heads.1), calls=%async_computation | async-start | bytes 262144 | tf_op jit(solution)/shard_map/all_to_all | solution.py:386
  12.7 0.0 copy-done.1
  12.7 0.0 copy-done.2
  12.8 0.0 copy-done
  12.8 2.2 %broadcast_select_fusion = (bf16[2,128,1024]{2,1,0:T(8,128)(2,1)}, bf16[2,128,1024]{2,1,0:T(8,128)(2,1)}, bf16[2,128,1024]{2,1,0:T(8,128)(2,1)}) fusion(pred[]{:T(512)S(6)} %eq.9, bf16[1,128,1024]{2,1,0:T(8,128)(2,1)S(1)} %bitcast.14, bf16[1,128,1024]{2,1,0:T(8,128)(2,1)} %bitcast.15, bf16[1,128,1024]{2,1,0:T(8,128)(2,1)S(1)} %bitcast.13, ...), kind=kLoop, calls=%fused_computation.2 | loop fusion | flops 786432 | bytes 2621441 | tf_op jit(solution)/shard_map/jit(_where)/select_n | solution.py:390
  15.0 5.1 %all-to-all-done = bf16[16,16,256]{2,1,0:T(8,128)(2,1)S(1)} async-done(((bf16[16,16,256]{2,1,0:T(8,128)(2,1)}), bf16[16,16,256]{2,1,0:T(8,128)(2,1)S(1)}, u32[]{:S(2)}, u32[]{:S(2)}) %all-to-all-start) | async-done | bytes 131104 | tf_op jit(solution)/shard_map/all_to_all | solution.py:386
  20.0 1.2 %broadcast_in_dim.13.room_ref = bf16[16,256,128]{2,1,0:T(8,128)(2,1)} broadcast(bf16[256,128]{1,0:T(8,128)(2,1)S(1)} %slice.3), dimensions={1,2} | broadcast | bytes 1114112 | tf_op jit(solution)/shard_map/broadcast_in_dim | solution.py:396
  21.2 6.8 %all-to-all-start.1 = ((bf16[16,256,128]{2,1,0:T(8,128)(2,1)}), bf16[16,256,128]{2,1,0:T(8,128)(2,1)S(1)}, u32[]{:S(2)}, u32[]{:S(2)}) async-start(bf16[16,256,128]{2,1,0:T(8,128)(2,1)} %broadcast_in_dim.13.room_ref), calls=%async_computation.1 | async-start | bytes 2097152 | tf_op jit(solution)/shard_map/all_to_all | solution.py:397
  28.0 3.4 %collective-permute-start = (bf16[2,128,1024]{2,1,0:T(8,128)(2,1)}, bf16[2,128,1024]{2,1,0:T(8,128)(2,1)S(1)}, u32[]{:S(2)}, u32[]{:S(2)}) collective-permute-start(bf16[2,128,1024]{2,1,0:T(8,128)(2,1)} %get-tuple-element.48), channel_id=1, source_target_pairs={{0,1},{1,2},{2,3},{3,4},{4,5},{5,6},{6,7},{7,8},{8,9},{9,10},{10,1... | collective-permute-start | bytes 1572872 | tf_op jit(solution)/shard_map/ppermute | solution.py:392
  31.4 3.4 %collective-permute-start.1 = (bf16[2,128,1024]{2,1,0:T(8,128)(2,1)}, bf16[2,128,1024]{2,1,0:T(8,128)(2,1)}, u32[]{:S(2)}, u32[]{:S(2)}) collective-permute-start(bf16[2,128,1024]{2,1,0:T(8,128)(2,1)} %get-tuple-element.49), channel_id=1, source_target_pairs={{1,0},{2,1},{3,2},{4,3},{5,4},{6,5},{7,6},{8,7},{9,8},{10,9},{11,1... | collective-permute-start | bytes 1572872 | tf_op jit(solution)/shard_map/ppermute | solution.py:393
  34.8 0.7 collective-permute-start.2
  35.5 7.7 %all-to-all-done.1 = bf16[16,256,128]{2,1,0:T(8,128)(2,1)S(1)} async-done(((bf16[16,256,128]{2,1,0:T(8,128)(2,1)}), bf16[16,256,128]{2,1,0:T(8,128)(2,1)S(1)}, u32[]{:S(2)}, u32[]{:S(2)}) %all-to-all-start.1) | async-done | bytes 1048608 | tf_op jit(solution)/shard_map/all_to_all | solution.py:397
  43.2 4.4 %short_layer.1 = (bf16[256,128]{1,0:T(8,128)(2,1)S(1)}, bf16[16,256,128]{2,1,0:T(8,128)(2,1)}) custom-call(s32[1]{0:T(128)} %bitcast.3.chip_ref, bf16[256,256]{1,0:T(8,128)(2,1)S(1)} %bitcast.17, bf16[4096,128]{1,0:T(8,128)(2,1)S(1)} %bitcast.11, bf16[16,256,128]{2,1,0:T(8,128)(2,1)} %broadcast_in_dim.13.room_ref), custom_call_target="tpu_custom_call", output_to_operand_aliasing={{1}: (3, {})} | custom-call | flops 65536 | bytes 256 | tf_op jit(solution)/shard_map/short_layer/pallas_call | solution.py:284
  47.6 0.0 collective-permute-done.prev_ref
  47.6 0.0 collective-permute-done.1.next_ref
  47.6 0.0 collective-permute-done.2.cross_ref
  47.6 0.0 copy-start.3
  47.6 4.2 %all-to-all-start.2 = ((bf16[16,256,128]{2,1,0:T(8,128)(2,1)}), bf16[16,256,128]{2,1,0:T(8,128)(2,1)S(1)}, u32[]{:S(2)}, u32[]{:S(2)}) async-start(bf16[16,256,128]{2,1,0:T(8,128)(2,1)} %get-tuple-element.66), calls=%async_computation.2 | async-start | bytes 2097152 | tf_op jit(solution)/shard_map/all_to_all | solution.py:402
  51.8 0.1 pad_add_fusion.place_ref
  51.9 0.0 copy-done.3
  51.9 1.7 %local_weights.1 = (bf16[8,128,256]{2,1,0:T(8,128)(2,1)S(1)}, bf16[8,128,256]{2,1,0:T(8,128)(2,1)S(1)}, f32[16,256]{1,0:T(8,128)S(1)}) custom-call(s32[3]{0:T(128)S(1)} %pad_add_fusion.place_ref, bf16[128,1024]{1,0:T(8,128)(2,1)S(1)} %copy-done.3, bf16[128,1024]{1,0:T(8,128)(2,1)S(1)} %copy-done, bf16[128,1024]{1,0:T(8,128)(2,1)S(1)} %copy-done.1, ...), custom_call_target="tpu_custom_call" | custom-call | flops 536870912 | bytes 3145728 | tf_op jit(solution)/shard_map/local_weights/pallas_call | solution.py:79
  53.6 7.2 %collective-permute-start.3 = (f32[16,256]{1,0:T(8,128)S(1)}, f32[16,256]{1,0:T(8,128)S(1)}, u32[]{:S(2)}, u32[]{:S(2)}) collective-permute-start(f32[16,256]{1,0:T(8,128)S(1)} %get-tuple-element.60), channel_id=1, source_target_pairs={{1,0},{2,1},{3,2},{4,3},{5,4},{6,5},{7,6},{8,7},{9,8},{10,9},{11,1... | collective-permute-start | bytes 49160 | tf_op jit(solution)/shard_map/ppermute | solution.py:406
  60.8 2.4 %local_layer.1 = (bf16[128,1024]{1,0:T(8,128)(2,1)}, bf16[128,1024]{1,0:T(8,128)(2,1)}, f32[128,1024]{1,0:T(8,128)S(1)}, f32[128,1024]{1,0:T(8,128)S(1)}) custom-call(s32[3]{0:T(128)S(1)} %pad_add_fusion.place_ref, bf16[128,1024]{1,0:T(8,128)(2,1)S(1)} %copy-done.3, bf16[128,1024]{1,0:T(8,128)(2,1)S(1)} %copy-done, bf16[128,1024]{1,0:T(8,128)(2,1)S(1)} %copy-done.1, ...), custom_call_target="tpu_custom_call" | custom-call | flops 536870912 | bytes 3145728 | tf_op jit(solution)/shard_map/local_layer/pallas_call | solution.py:129
  63.2 0.0 collective-permute-done.3.stats_ref
  63.2 2.7 %late_keys.1 = (bf16[128,1024]{1,0:T(8,128)(2,1)}, bf16[128,1024]{1,0:T(8,128)(2,1)}, f32[8,128]{1,0:T(8,128)S(1)}) custom-call(s32[3]{0:T(128)S(1)} %pad_add_fusion.place_ref, bf16[128,1024]{1,0:T(8,128)(2,1)S(1)} %copy-done, bf16[128,1024]{1,0:T(8,128)(2,1)S(1)} %copy-done.1, bf16[2,128,1024]{2,1,0:T(8,128)(2,1)} %collective-permute-done.1.next_ref, ...), custom_call_target="tpu_custom_call" | custom-call | flops 536870912 | bytes 3145728 | tf_op jit(solution)/shard_map/late_keys/pallas_call | solution.py:175
  66.0 0.0 all-to-all-done.2.parts_ref
  66.0 0.1 sum_terms.1
  66.1 4.1 %collective-permute-start.4 = (bf16[128,256]{1,0:T(8,128)(2,1)S(1)}, bf16[128,256]{1,0:T(8,128)(2,1)S(1)}, u32[]{:S(2)}, u32[]{:S(2)}) collective-permute-start(bf16[128,256]{1,0:T(8,128)(2,1)S(1)} %get-tuple-element.69), channel_id=1, source_target_pairs={{0,8},{8,0},{1,9},{9,1},{2,10},{10,2},{3,11},{11,3},{4,12},{12,4},... | collective-permute-start | bytes 196616 | tf_op jit(solution)/shard_map/ppermute | solution.py:413
  70.2 0.9 %collective-permute-done.4.got_ref = bf16[128,256]{1,0:T(8,128)(2,1)S(1)} collective-permute-done((bf16[128,256]{1,0:T(8,128)(2,1)S(1)}, bf16[128,256]{1,0:T(8,128)(2,1)S(1)}, u32[]{:S(2)}, u32[]{:S(2)}) %collective-permute-start.4) | collective-permute-done | bytes 65568 | tf_op jit(solution)/shard_map/ppermute | solution.py:413
  71.1 0.7 %join_heads.1 = (bf16[128,128]{1,0:T(8,128)(2,1)}, bf16[128,128]{1,0:T(8,128)(2,1)}, bf16[128,128]{1,0:T(8,128)(2,1)}, bf16[128,128]{1,0:T(8,128)(2,1)}) custom-call(s32[1]{0:T(128)} %bitcast.10.core_ref, bf16[128,256]{1,0:T(8,128)(2,1)S(1)} %get-tuple-element.68.keep_ref, bf16[128,256]{1,0:T(8,128)(2,1)S(1)} %collective-permute-done.4.got_ref), custom_call_target="tpu_custom_call" | custom-call | tf_op jit(solution)/shard_map/join_heads/pallas_call | solution.py:353
  (1 shorter events, 0.0 us)
Async XLA Ops:
  0.6 12.1 %copy-start.1 = (bf16[128,1024]{1,0:T(8,128)(2,1)S(1)}, bf16[128,1024]{1,0:T(8,128)(2,1)}, u32[]{:S(2)}) copy-start(bf16[128,1024]{1,0:T(8,128)(2,1)} %v_ref.7) | copy-start | bytes 786436
  0.6 12.1 %copy-start.2 = (bf16[128,1024]{1,0:T(8,128)(2,1)S(1)}, bf16[128,1024]{1,0:T(8,128)(2,1)}, u32[]{:S(2)}) copy-start(bf16[128,1024]{1,0:T(8,128)(2,1)} %g_ref.5) | copy-start | bytes 786436
  2.6 10.1 %copy-start = (bf16[128,1024]{1,0:T(8,128)(2,1)S(1)}, bf16[128,1024]{1,0:T(8,128)(2,1)}, u32[]{:S(2)}) copy-start(bf16[128,1024]{1,0:T(8,128)(2,1)} %k_ref.7) | copy-start | bytes 786436
  2.6 17.4 %all-to-all-start = ((bf16[16,16,256]{2,1,0:T(8,128)(2,1)}), bf16[16,16,256]{2,1,0:T(8,128)(2,1)S(1)}, u32[]{:S(2)}, u32[]{:S(2)}) async-start(bf16[16,16,256]{2,1,0:T(8,128)(2,1)} %pack_heads.1), calls=%async_computation | async-start | bytes 262144 | tf_op jit(solution)/shard_map/all_to_all | solution.py:386
  21.2 22.0 %all-to-all-start.1 = ((bf16[16,256,128]{2,1,0:T(8,128)(2,1)}), bf16[16,256,128]{2,1,0:T(8,128)(2,1)S(1)}, u32[]{:S(2)}, u32[]{:S(2)}) async-start(bf16[16,256,128]{2,1,0:T(8,128)(2,1)} %broadcast_in_dim.13.room_ref), calls=%async_computation.1 | async-start | bytes 2097152 | tf_op jit(solution)/shard_map/all_to_all | solution.py:397
  28.0 19.6 %collective-permute-start = (bf16[2,128,1024]{2,1,0:T(8,128)(2,1)}, bf16[2,128,1024]{2,1,0:T(8,128)(2,1)S(1)}, u32[]{:S(2)}, u32[]{:S(2)}) collective-permute-start(bf16[2,128,1024]{2,1,0:T(8,128)(2,1)} %get-tuple-element.48), channel_id=1, source_target_pairs={{0,1},{1,2},{2,3},{3,4},{4,5},{5,6},{6,7},{7,8},{8,9},{9,10},{10,1... | collective-permute-start | bytes 1572872 | tf_op jit(solution)/shard_map/ppermute | solution.py:392
  31.4 16.2 %collective-permute-start.1 = (bf16[2,128,1024]{2,1,0:T(8,128)(2,1)}, bf16[2,128,1024]{2,1,0:T(8,128)(2,1)}, u32[]{:S(2)}, u32[]{:S(2)}) collective-permute-start(bf16[2,128,1024]{2,1,0:T(8,128)(2,1)} %get-tuple-element.49), channel_id=1, source_target_pairs={{1,0},{2,1},{3,2},{4,3},{5,4},{6,5},{7,6},{8,7},{9,8},{10,9},{11,1... | collective-permute-start | bytes 1572872 | tf_op jit(solution)/shard_map/ppermute | solution.py:393
  34.8 12.8 %collective-permute-start.2 = (bf16[2,128,1024]{2,1,0:T(8,128)(2,1)}, bf16[2,128,1024]{2,1,0:T(8,128)(2,1)S(1)}, u32[]{:S(2)}, u32[]{:S(2)}) collective-permute-start(bf16[2,128,1024]{2,1,0:T(8,128)(2,1)} %get-tuple-element.50), channel_id=1, source_target_pairs={{15,16},{31,32},{47,48},{63,64},{79,80},{95,96},{111,112},{127,128... | collective-permute-start | bytes 1572872 | tf_op jit(solution)/shard_map/ppermute | solution.py:399
  47.6 4.3 %copy-start.3 = (bf16[128,1024]{1,0:T(8,128)(2,1)S(1)}, bf16[128,1024]{1,0:T(8,128)(2,1)}, u32[]{:S(2)}) copy-start(bf16[128,1024]{1,0:T(8,128)(2,1)} %q_ref.5) | copy-start | bytes 786436
  47.6 18.3 %all-to-all-start.2 = ((bf16[16,256,128]{2,1,0:T(8,128)(2,1)}), bf16[16,256,128]{2,1,0:T(8,128)(2,1)S(1)}, u32[]{:S(2)}, u32[]{:S(2)}) async-start(bf16[16,256,128]{2,1,0:T(8,128)(2,1)} %get-tuple-element.66), calls=%async_computation.2 | async-start | bytes 2097152 | tf_op jit(solution)/shard_map/all_to_all | solution.py:402
  53.6 9.6 %collective-permute-start.3 = (f32[16,256]{1,0:T(8,128)S(1)}, f32[16,256]{1,0:T(8,128)S(1)}, u32[]{:S(2)}, u32[]{:S(2)}) collective-permute-start(f32[16,256]{1,0:T(8,128)S(1)} %get-tuple-element.60), channel_id=1, source_target_pairs={{1,0},{2,1},{3,2},{4,3},{5,4},{6,5},{7,6},{8,7},{9,8},{10,9},{11,1... | collective-permute-start | bytes 49160 | tf_op jit(solution)/shard_map/ppermute | solution.py:406
  66.1 5.0 %collective-permute-start.4 = (bf16[128,256]{1,0:T(8,128)(2,1)S(1)}, bf16[128,256]{1,0:T(8,128)(2,1)S(1)}, u32[]{:S(2)}, u32[]{:S(2)}) collective-permute-start(bf16[128,256]{1,0:T(8,128)(2,1)S(1)} %get-tuple-element.69), channel_id=1, source_target_pairs={{0,8},{8,0},{1,9},{9,1},{2,10},{10,2},{3,11},{11,3},{4,12},{12,4},... | collective-permute-start | bytes 196616 | tf_op jit(solution)/shard_map/ppermute | solution.py:413

commit v6 on v5

--- a/solution.py
+++ b/solution.py
@@ -221,7 +221,7 @@
 
 
 def short_kernel(chip_ref, mine_ref, kv_ref, room_ref, od_ref, dkv_ref,
-                 lhs_ref, kv_t_ref, s_ref, dp_ref, acc_ref, stage_ref, sem):
+                 lhs_ref, kv_t_ref, s_ref, dp_ref, stage_ref, sem):
     scale = 1.0 / math.sqrt(HD)
     chip = chip_ref[0]
     blocks, kb, _ = stage_ref.shape
@@ -268,9 +268,9 @@
         copies[t].start()
         od = jnp.concatenate([dot_n(kv_t_ref[t, :HD], dsp[:, :rows]),
                               dot_n(kv_t_ref[t, HD:], dsp[:, rows:])], axis=0)
-        acc_ref[...] = od if t == 0 else acc_ref[...] + od
+        acc = od if t == 0 else acc + od
     low = lax.broadcasted_iota(jnp.int32, (rows, LANES), 1) < HD
-    od_ref[...] = (acc_ref[...].T * jnp.where(low, scale, 1.0)).astype(jnp.bfloat16)
+    od_ref[...] = (acc.T * jnp.where(low, scale, 1.0)).astype(jnp.bfloat16)
     for copy in copies:
         copy.wait()
 
@@ -294,7 +294,6 @@
             pltpu.VMEM((blocks, LANES, kb), bf16),
             pltpu.VMEM((blocks, kb, rows), f32),
             pltpu.VMEM((blocks, kb, rows), f32),
-            pltpu.VMEM((LANES, rows), f32),
             pltpu.VMEM((blocks, kb, LANES), bf16),
             pltpu.SemaphoreType.DMA((blocks,)),
         ],

time: 72.7 us -> 72.7 us (level)
  no operation moved by 1% of the time
where the time goes in v6:
time: 72.7 us; the launch traced here: 71.8 us
  starting transfers between devices  39.8 us (55%)
  Pallas kernels  14 us (19%)
  waiting for transfers between devices  13.7 us (19%)
  other arithmetic  2.26 us (3%)
  local copies, waits for them, and re-layouts  1.21 us (2%)
  between operations  0.79 us (1%)
    all_to_all x1, starting transfers between devices, on_device(): lax.all_to_all(packed, ('c', 'z'), split_axis=0, concat_axis=0, tiled=True)  10.1 us
    all_to_all x1, waiting for transfers between devices, on_device(): lax.all_to_all(spread, ('x', 'y'), split_axis=0, concat_axis=0, tiled=True)  7.72 us
    ppermute x1, starting transfers between devices, on_device(): stats = lax.ppermute(stats, axes, all_up)  7.22 us
    all_to_all x1, starting transfers between devices, on_device(): lax.all_to_all(spread, ('x', 'y'), split_axis=0, concat_axis=0, tiled=True)  6.75 us
    all_to_all x1, waiting for transfers between devices, on_device(): lax.all_to_all(packed, ('c', 'z'), split_axis=0, concat_axis=0, tiled=True)  5.08 us
    pallas_call x1, Pallas kernels, short_call(): pl.pallas_call(short_kernel, out_shape=(jax.ShapeDtypeStruct((rows, LANES...  4.35 us
    all_to_all x1, starting transfers between devices, on_device(): lax.all_to_all(dkv, ('x', 'y'), split_axis=0, concat_axis=0, tiled=True)  4.19 us
    ppermute x1, starting transfers between devices, on_device(): got = lax.ppermute(give, 'c', [(0, 1), (1, 0)])  4.1 us
  transfers between devices with their start and end apart: 8, of which 3 were waited for; matrix products, arithmetic and copies ran while one was open for 3% of the time, Pallas kernels for 16%

profile of v6, /device:TPU:1, one launch (start us, length us, event | category | flops | bytes accessed | tf_op | source)
XLA Modules:
  0.0 71.8 jit_solution(8393941295092629481)
XLA Ops:
  0.6 0.0 copy-start.1
  0.6 0.0 copy-start.2
  0.7 2.0 %pack_heads.1 = bf16[16,16,256]{2,1,0:T(8,128)(2,1)} custom-call(bf16[16,1024]{1,0:T(8,128)(2,1)} %q_ref.3, bf16[16,1024]{1,0:T(8,128)(2,1)} %k_ref.4, bf16[16,1024]{1,0:T(8,128)(2,1)} %v_ref.4, bf16[128,1024]{1,0:T(8,128)(2,1)} %g_ref.5), custom_call_target="tpu_custom_call" | custom-call | tf_op jit(solution)/shard_map/pack_heads/pallas_call | solution.py:214
  2.6 0.0 copy-start
  2.6 10.1 %all-to-all-start = ((bf16[16,16,256]{2,1,0:T(8,128)(2,1)}), bf16[16,16,256]{2,1,0:T(8,128)(2,1)S(1)}, u32[]{:S(2)}, u32[]{:S(2)}) async-start(bf16[16,16,256]{2,1,0:T(8,128)(2,1)} %pack_heads.1), calls=%async_computation | async-start | bytes 262144 | tf_op jit(solution)/shard_map/all_to_all | solution.py:385
  12.7 0.0 copy-done.1
  12.7 0.0 copy-done.2
  12.8 0.0 copy-done
  12.8 2.2 %broadcast_select_fusion = (bf16[2,128,1024]{2,1,0:T(8,128)(2,1)}, bf16[2,128,1024]{2,1,0:T(8,128)(2,1)}, bf16[2,128,1024]{2,1,0:T(8,128)(2,1)}) fusion(pred[]{:T(512)S(6)} %eq.9, bf16[1,128,1024]{2,1,0:T(8,128)(2,1)S(1)} %bitcast.14, bf16[1,128,1024]{2,1,0:T(8,128)(2,1)} %bitcast.15, bf16[1,128,1024]{2,1,0:T(8,128)(2,1)S(1)} %bitcast.13, ...), kind=kLoop, calls=%fused_computation.2 | loop fusion | flops 786432 | bytes 2621441 | tf_op jit(solution)/shard_map/jit(_where)/select_n | solution.py:389
  15.0 5.1 %all-to-all-done = bf16[16,16,256]{2,1,0:T(8,128)(2,1)S(1)} async-done(((bf16[16,16,256]{2,1,0:T(8,128)(2,1)}), bf16[16,16,256]{2,1,0:T(8,128)(2,1)S(1)}, u32[]{:S(2)}, u32[]{:S(2)}) %all-to-all-start) | async-done | bytes 131104 | tf_op jit(solution)/shard_map/all_to_all | solution.py:385
  20.0 1.2 %broadcast_in_dim.13.room_ref = bf16[16,256,128]{2,1,0:T(8,128)(2,1)} broadcast(bf16[256,128]{1,0:T(8,128)(2,1)S(1)} %slice.3), dimensions={1,2} | broadcast | bytes 1114112 | tf_op jit(solution)/shard_map/broadcast_in_dim | solution.py:395
  21.2 6.8 %all-to-all-start.1 = ((bf16[16,256,128]{2,1,0:T(8,128)(2,1)}), bf16[16,256,128]{2,1,0:T(8,128)(2,1)S(1)}, u32[]{:S(2)}, u32[]{:S(2)}) async-start(bf16[16,256,128]{2,1,0:T(8,128)(2,1)} %broadcast_in_dim.13.room_ref), calls=%async_computation.1 | async-start | bytes 2097152 | tf_op jit(solution)/shard_map/all_to_all | solution.py:396
  28.0 3.4 %collective-permute-start = (bf16[2,128,1024]{2,1,0:T(8,128)(2,1)}, bf16[2,128,1024]{2,1,0:T(8,128)(2,1)S(1)}, u32[]{:S(2)}, u32[]{:S(2)}) collective-permute-start(bf16[2,128,1024]{2,1,0:T(8,128)(2,1)} %get-tuple-element.48), channel_id=1, source_target_pairs={{0,1},{1,2},{2,3},{3,4},{4,5},{5,6},{6,7},{7,8},{8,9},{9,10},{10,1... | collective-permute-start | bytes 1572872 | tf_op jit(solution)/shard_map/ppermute | solution.py:391
  31.4 3.4 %collective-permute-start.1 = (bf16[2,128,1024]{2,1,0:T(8,128)(2,1)}, bf16[2,128,1024]{2,1,0:T(8,128)(2,1)}, u32[]{:S(2)}, u32[]{:S(2)}) collective-permute-start(bf16[2,128,1024]{2,1,0:T(8,128)(2,1)} %get-tuple-element.49), channel_id=1, source_target_pairs={{1,0},{2,1},{3,2},{4,3},{5,4},{6,5},{7,6},{8,7},{9,8},{10,9},{11,1... | collective-permute-start | bytes 1572872 | tf_op jit(solution)/shard_map/ppermute | solution.py:392
  34.8 0.7 collective-permute-start.2
  35.5 7.7 %all-to-all-done.1 = bf16[16,256,128]{2,1,0:T(8,128)(2,1)S(1)} async-done(((bf16[16,256,128]{2,1,0:T(8,128)(2,1)}), bf16[16,256,128]{2,1,0:T(8,128)(2,1)S(1)}, u32[]{:S(2)}, u32[]{:S(2)}) %all-to-all-start.1) | async-done | bytes 1048608 | tf_op jit(solution)/shard_map/all_to_all | solution.py:396
  43.2 4.4 %short_layer.1 = (bf16[256,128]{1,0:T(8,128)(2,1)S(1)}, bf16[16,256,128]{2,1,0:T(8,128)(2,1)}) custom-call(s32[1]{0:T(128)} %bitcast.3.chip_ref, bf16[256,256]{1,0:T(8,128)(2,1)S(1)} %bitcast.17, bf16[4096,128]{1,0:T(8,128)(2,1)S(1)} %bitcast.11, bf16[16,256,128]{2,1,0:T(8,128)(2,1)} %broadcast_in_dim.13.room_ref), custom_call_target="tpu_custom_call", output_to_operand_aliasing={{1}: (3, {})} | custom-call | flops 65536 | bytes 256 | tf_op jit(solution)/shard_map/short_layer/pallas_call | solution.py:284
  47.6 0.0 collective-permute-done.prev_ref
  47.6 0.0 collective-permute-done.1.next_ref
  47.6 0.0 collective-permute-done.2.cross_ref
  47.6 0.0 copy-start.3
  47.6 4.2 %all-to-all-start.2 = ((bf16[16,256,128]{2,1,0:T(8,128)(2,1)}), bf16[16,256,128]{2,1,0:T(8,128)(2,1)S(1)}, u32[]{:S(2)}, u32[]{:S(2)}) async-start(bf16[16,256,128]{2,1,0:T(8,128)(2,1)} %get-tuple-element.66), calls=%async_computation.2 | async-start | bytes 2097152 | tf_op jit(solution)/shard_map/all_to_all | solution.py:401
  51.8 0.1 pad_add_fusion.place_ref
  51.9 0.0 copy-done.3
  51.9 1.7 %local_weights.1 = (bf16[8,128,256]{2,1,0:T(8,128)(2,1)S(1)}, bf16[8,128,256]{2,1,0:T(8,128)(2,1)S(1)}, f32[16,256]{1,0:T(8,128)S(1)}) custom-call(s32[3]{0:T(128)S(1)} %pad_add_fusion.place_ref, bf16[128,1024]{1,0:T(8,128)(2,1)S(1)} %copy-done.3, bf16[128,1024]{1,0:T(8,128)(2,1)S(1)} %copy-done, bf16[128,1024]{1,0:T(8,128)(2,1)S(1)} %copy-done.1, ...), custom_call_target="tpu_custom_call" | custom-call | flops 536870912 | bytes 3145728 | tf_op jit(solution)/shard_map/local_weights/pallas_call | solution.py:79
  53.6 7.2 %collective-permute-start.3 = (f32[16,256]{1,0:T(8,128)S(1)}, f32[16,256]{1,0:T(8,128)S(1)}, u32[]{:S(2)}, u32[]{:S(2)}) collective-permute-start(f32[16,256]{1,0:T(8,128)S(1)} %get-tuple-element.60), channel_id=1, source_target_pairs={{1,0},{2,1},{3,2},{4,3},{5,4},{6,5},{7,6},{8,7},{9,8},{10,9},{11,1... | collective-permute-start | bytes 49160 | tf_op jit(solution)/shard_map/ppermute | solution.py:405
  60.8 2.4 %local_layer.1 = (bf16[128,1024]{1,0:T(8,128)(2,1)}, bf16[128,1024]{1,0:T(8,128)(2,1)}, f32[128,1024]{1,0:T(8,128)S(1)}, f32[128,1024]{1,0:T(8,128)S(1)}) custom-call(s32[3]{0:T(128)S(1)} %pad_add_fusion.place_ref, bf16[128,1024]{1,0:T(8,128)(2,1)S(1)} %copy-done.3, bf16[128,1024]{1,0:T(8,128)(2,1)S(1)} %copy-done, bf16[128,1024]{1,0:T(8,128)(2,1)S(1)} %copy-done.1, ...), custom_call_target="tpu_custom_call" | custom-call | flops 536870912 | bytes 3145728 | tf_op jit(solution)/shard_map/local_layer/pallas_call | solution.py:129
  63.2 0.0 collective-permute-done.3.stats_ref
  63.2 2.7 %late_keys.1 = (bf16[128,1024]{1,0:T(8,128)(2,1)}, bf16[128,1024]{1,0:T(8,128)(2,1)}, f32[8,128]{1,0:T(8,128)S(1)}) custom-call(s32[3]{0:T(128)S(1)} %pad_add_fusion.place_ref, bf16[128,1024]{1,0:T(8,128)(2,1)S(1)} %copy-done, bf16[128,1024]{1,0:T(8,128)(2,1)S(1)} %copy-done.1, bf16[2,128,1024]{2,1,0:T(8,128)(2,1)} %collective-permute-done.1.next_ref, ...), custom_call_target="tpu_custom_call" | custom-call | flops 536870912 | bytes 3145728 | tf_op jit(solution)/shard_map/late_keys/pallas_call | solution.py:175
  66.0 0.0 all-to-all-done.2.parts_ref
  66.0 0.1 sum_terms.1
  66.1 4.1 %collective-permute-start.4 = (bf16[128,256]{1,0:T(8,128)(2,1)S(1)}, bf16[128,256]{1,0:T(8,128)(2,1)S(1)}, u32[]{:S(2)}, u32[]{:S(2)}) collective-permute-start(bf16[128,256]{1,0:T(8,128)(2,1)S(1)} %get-tuple-element.69), channel_id=1, source_target_pairs={{0,8},{8,0},{1,9},{9,1},{2,10},{10,2},{3,11},{11,3},{4,12},{12,4},... | collective-permute-start | bytes 196616 | tf_op jit(solution)/shard_map/ppermute | solution.py:412
  70.2 0.9 %collective-permute-done.4.got_ref = bf16[128,256]{1,0:T(8,128)(2,1)S(1)} collective-permute-done((bf16[128,256]{1,0:T(8,128)(2,1)S(1)}, bf16[128,256]{1,0:T(8,128)(2,1)S(1)}, u32[]{:S(2)}, u32[]{:S(2)}) %collective-permute-start.4) | collective-permute-done | bytes 65568 | tf_op jit(solution)/shard_map/ppermute | solution.py:412
  71.1 0.7 %join_heads.1 = (bf16[128,128]{1,0:T(8,128)(2,1)}, bf16[128,128]{1,0:T(8,128)(2,1)}, bf16[128,128]{1,0:T(8,128)(2,1)}, bf16[128,128]{1,0:T(8,128)(2,1)}) custom-call(s32[1]{0:T(128)} %bitcast.10.core_ref, bf16[128,256]{1,0:T(8,128)(2,1)S(1)} %get-tuple-element.68.keep_ref, bf16[128,256]{1,0:T(8,128)(2,1)S(1)} %collective-permute-done.4.got_ref), custom_call_target="tpu_custom_call" | custom-call | tf_op jit(solution)/shard_map/join_heads/pallas_call | solution.py:352
  (1 shorter events, 0.0 us)
Async XLA Ops:
  0.6 12.1 %copy-start.1 = (bf16[128,1024]{1,0:T(8,128)(2,1)S(1)}, bf16[128,1024]{1,0:T(8,128)(2,1)}, u32[]{:S(2)}) copy-start(bf16[128,1024]{1,0:T(8,128)(2,1)} %v_ref.7) | copy-start | bytes 786436
  0.6 12.1 %copy-start.2 = (bf16[128,1024]{1,0:T(8,128)(2,1)S(1)}, bf16[128,1024]{1,0:T(8,128)(2,1)}, u32[]{:S(2)}) copy-start(bf16[128,1024]{1,0:T(8,128)(2,1)} %g_ref.5) | copy-start | bytes 786436
  2.6 10.1 %copy-start = (bf16[128,1024]{1,0:T(8,128)(2,1)S(1)}, bf16[128,1024]{1,0:T(8,128)(2,1)}, u32[]{:S(2)}) copy-start(bf16[128,1024]{1,0:T(8,128)(2,1)} %k_ref.7) | copy-start | bytes 786436
  2.6 17.4 %all-to-all-start = ((bf16[16,16,256]{2,1,0:T(8,128)(2,1)}), bf16[16,16,256]{2,1,0:T(8,128)(2,1)S(1)}, u32[]{:S(2)}, u32[]{:S(2)}) async-start(bf16[16,16,256]{2,1,0:T(8,128)(2,1)} %pack_heads.1), calls=%async_computation | async-start | bytes 262144 | tf_op jit(solution)/shard_map/all_to_all | solution.py:385
  21.2 22.0 %all-to-all-start.1 = ((bf16[16,256,128]{2,1,0:T(8,128)(2,1)}), bf16[16,256,128]{2,1,0:T(8,128)(2,1)S(1)}, u32[]{:S(2)}, u32[]{:S(2)}) async-start(bf16[16,256,128]{2,1,0:T(8,128)(2,1)} %broadcast_in_dim.13.room_ref), calls=%async_computation.1 | async-start | bytes 2097152 | tf_op jit(solution)/shard_map/all_to_all | solution.py:396
  28.0 19.6 %collective-permute-start = (bf16[2,128,1024]{2,1,0:T(8,128)(2,1)}, bf16[2,128,1024]{2,1,0:T(8,128)(2,1)S(1)}, u32[]{:S(2)}, u32[]{:S(2)}) collective-permute-start(bf16[2,128,1024]{2,1,0:T(8,128)(2,1)} %get-tuple-element.48), channel_id=1, source_target_pairs={{0,1},{1,2},{2,3},{3,4},{4,5},{5,6},{6,7},{7,8},{8,9},{9,10},{10,1... | collective-permute-start | bytes 1572872 | tf_op jit(solution)/shard_map/ppermute | solution.py:391
  31.4 16.2 %collective-permute-start.1 = (bf16[2,128,1024]{2,1,0:T(8,128)(2,1)}, bf16[2,128,1024]{2,1,0:T(8,128)(2,1)}, u32[]{:S(2)}, u32[]{:S(2)}) collective-permute-start(bf16[2,128,1024]{2,1,0:T(8,128)(2,1)} %get-tuple-element.49), channel_id=1, source_target_pairs={{1,0},{2,1},{3,2},{4,3},{5,4},{6,5},{7,6},{8,7},{9,8},{10,9},{11,1... | collective-permute-start | bytes 1572872 | tf_op jit(solution)/shard_map/ppermute | solution.py:392
  34.8 12.8 %collective-permute-start.2 = (bf16[2,128,1024]{2,1,0:T(8,128)(2,1)}, bf16[2,128,1024]{2,1,0:T(8,128)(2,1)S(1)}, u32[]{:S(2)}, u32[]{:S(2)}) collective-permute-start(bf16[2,128,1024]{2,1,0:T(8,128)(2,1)} %get-tuple-element.50), channel_id=1, source_target_pairs={{15,16},{31,32},{47,48},{63,64},{79,80},{95,96},{111,112},{127,128... | collective-permute-start | bytes 1572872 | tf_op jit(solution)/shard_map/ppermute | solution.py:398
  47.6 4.3 %copy-start.3 = (bf16[128,1024]{1,0:T(8,128)(2,1)S(1)}, bf16[128,1024]{1,0:T(8,128)(2,1)}, u32[]{:S(2)}) copy-start(bf16[128,1024]{1,0:T(8,128)(2,1)} %q_ref.5) | copy-start | bytes 786436
  47.6 18.3 %all-to-all-start.2 = ((bf16[16,256,128]{2,1,0:T(8,128)(2,1)}), bf16[16,256,128]{2,1,0:T(8,128)(2,1)S(1)}, u32[]{:S(2)}, u32[]{:S(2)}) async-start(bf16[16,256,128]{2,1,0:T(8,128)(2,1)} %get-tuple-element.66), calls=%async_computation.2 | async-start | bytes 2097152 | tf_op jit(solution)/shard_map/all_to_all | solution.py:401
  53.6 9.6 %collective-permute-start.3 = (f32[16,256]{1,0:T(8,128)S(1)}, f32[16,256]{1,0:T(8,128)S(1)}, u32[]{:S(2)}, u32[]{:S(2)}) collective-permute-start(f32[16,256]{1,0:T(8,128)S(1)} %get-tuple-element.60), channel_id=1, source_target_pairs={{1,0},{2,1},{3,2},{4,3},{5,4},{6,5},{7,6},{8,7},{9,8},{10,9},{11,1... | collective-permute-start | bytes 49160 | tf_op jit(solution)/shard_map/ppermute | solution.py:405
  66.1 5.0 %collective-permute-start.4 = (bf16[128,256]{1,0:T(8,128)(2,1)S(1)}, bf16[128,256]{1,0:T(8,128)(2,1)S(1)}, u32[]{:S(2)}, u32[]{:S(2)}) collective-permute-start(bf16[128,256]{1,0:T(8,128)(2,1)S(1)} %get-tuple-element.69), channel_id=1, source_target_pairs={{0,8},{8,0},{1,9},{9,1},{2,10},{10,2},{3,11},{11,3},{4,12},{12,4},... | collective-permute-start | bytes 196616 | tf_op jit(solution)/shard_map/ppermute | solution.py:412
